TPU v7x, 32 devices: a whole 2x2x4 slice. The times are simulated.
32 devices in a mesh: section: 4 (over y, core), dp: 8 (over z, x).
Axes of the slice: x: 2, y: 2, z: 4, core: 2. Of those that a mesh axis runs over, the one named last changes fastest.
Arguments:
- tokens: bfloat16 [32, 4, 512, 512], P('dp', 'section'), may hold values from -6 to 6
- doc_ids: int32 [32, 4, 512], P('dp', 'section'), may hold values from 0 to 3, never falling along the last dimension, each value on 1 to 256 neighbouring positions
- reset_flags: int32 [32, 4], P('dp', 'section'), may hold values from 0 to 1, as said below
- attn_gain: bfloat16 [512], replicated, may hold values from 0.5 to 1.5
- w_qkv: bfloat16 [512, 1536], replicated, may hold values from -0.25 to 0.25
- w_attn_out: bfloat16 [512, 512], replicated, may hold values from -0.75 to 0.75
- ffn_gain: bfloat16 [512], replicated, may hold values from 0.5 to 1.5
- w_in: bfloat16 [512, 2048], replicated, may hold values from -0.25 to 0.25
- w_out: bfloat16 [2048, 512], replicated, may hold values from -0.1875 to 0.1875
- write_gain: bfloat16 [512], replicated, may hold values from 0.5 to 1.5
- w_write: bfloat16 [512, 1536], replicated, may hold values from -0.25 to 0.25
- w_write_out: bfloat16 [512, 512], replicated, may hold values from -1 to 1
- init_memory: bfloat16 [64, 512], replicated, may hold values from -6 to 6
- out_grad: bfloat16 [32, 4, 512, 512], P('dp', 'section'), may hold values from -6 to 6
- memory_grad: bfloat16 [32, 4, 64, 512], P('dp', 'section'), may hold values from -6 to 6
Outputs:
- encoded: bfloat16 [32, 4, 512, 512], P('dp', 'section')
- memories: bfloat16 [32, 4, 64, 512], P('dp', 'section')
- tokens_grad: float32 [32, 4, 512, 512], P('dp', 'section')
- attn_gain_grad: float32 [512], replicated
- w_qkv_grad: float32 [512, 1536], replicated
- w_attn_out_grad: float32 [512, 512], replicated
- ffn_gain_grad: float32 [512], replicated
- w_in_grad: float32 [512, 2048], replicated
- w_out_grad: float32 [2048, 512], replicated
- write_gain_grad: float32 [512], replicated
- w_write_grad: float32 [512, 1536], replicated
- w_write_out_grad: float32 [512, 512], replicated
- init_memory_grad: float32 [64, 512], replicated
Inputs may be any that keep to these rules, and one draw needn't show every extreme that they name: `reset_flags`: the first segment of every stream has flag 1; among the 4 streams of each index of dp one has no other flag.
All inputs are finite; a program needn't handle non-finite values.
Results may differ from a plain program's by a relative error of at most 0.014.
Values may be sent and summed in bfloat16 or wider, within the bound.
No kernel may reach another device: no remote copies, remote signals or barrier semaphores. Data moves between devices by JAX's collectives and lax.ppermute only.
A program may use at most 256 MiB of HBM per device.

v0:
```python
import jax
import jax.numpy as jnp
import numpy as np
from jax import lax
from jax.experimental import pallas as pl
from jax.experimental.pallas import tpu as pltpu
from jax.sharding import PartitionSpec as P

HEADS = 8
HEAD_DIM = 64
HEADS_A_STEP = 8
EPS = 1e-06
MASKED = -1000000000.0
F32 = jnp.float32
BF16 = jnp.bfloat16
SQRT_2_PI = 0.7978845608028654
CUBIC = 0.044715
VMEM_LIMIT = 60 * 1024 * 1024


def nn(left, right):
    return lax.dot_general(left, right, (((1,), (0,)), ((), ())), preferred_element_type=F32)


def tn(left, right):
    return lax.dot_general(left, right, (((0,), (0,)), ((), ())), preferred_element_type=F32)


def nt(left, right):
    return lax.dot_general(left, right, (((1,), (1,)), ((), ())), preferred_element_type=F32)


def wide(column_tile, width):
    copies = max(1, width // 128)
    if width < 128:
        return column_tile[:, :width]
    return jnp.concatenate([column_tile] * copies, axis=1)


def inverse_rms(values):
    return lax.rsqrt(jnp.mean(values * values, axis=0, keepdims=True) + EPS)


def lane_sums(values):
    total = values[:, :128]
    for at in range(128, values.shape[1], 128):
        total = total + values[:, at : at + 128]
    return total


def head_mask(rows, columns):
    row_head = lax.broadcasted_iota(jnp.int32, (rows, columns), 0) // HEAD_DIM
    column_head = lax.broadcasted_iota(jnp.int32, (rows, columns), 1) // HEAD_DIM
    return row_head == column_head


def norm_back(grad_normed, normed, scale, gain, gain_inverse):
    weighed = grad_normed * normed
    mean = jnp.mean(weighed, axis=0, keepdims=True)
    return scale * (grad_normed * gain - normed * gain_inverse * mean), weighed


def gain_tiles(gains_ref, count=3):
    tiles = []
    for at in range(count):
        row = gains_ref[at : at + 1, :]
        tiles.append(jnp.broadcast_to(row, (128, row.shape[1])).T)
    return tiles


class Sources:
    def __init__(self, arrays, choices):
        self.arrays = arrays
        self.choices = choices

    def start(self, refs, at, place, buffer, sem):
        for condition, parts in self.choices(at, place):

            @pl.when(condition)
            def _():
                top = 0
                for number, index in parts:
                    source = refs[number].at[index]
                    target = buffer.at[pl.ds(top, source.shape[0]), :]
                    pltpu.make_async_copy(source, target, sem).start()
                    top += source.shape[0]

    def wait(self, buffer, sem):
        pltpu.make_async_copy(buffer, buffer, sem).wait()

    def rows_of(self, refs, steps, segment, place, buffer, sems):
        step = pl.program_id(0)
        slot = lax.rem(step, 2)

        @pl.when(step == 0)
        def _():
            self.start(refs, segment(0), place, buffer.at[0], sems.at[0])

        if steps > 1:

            @pl.when(step + 1 < steps)
            def _():
                self.start(refs, segment(step + 1), place, buffer.at[1 - slot], sems.at[1 - slot])

        self.wait(buffer.at[slot], sems.at[slot])
        return buffer.at[slot]


def forward_kernel(
    sources,
    segs,
    place_ref,
    mem0_ref,
    init_ref,
    gains_ref,
    spread_ref,
    fold_ref,
    *refs,
):
    wqkv_ref, wao_ref, win_ref, wout_ref, ww_ref, wwo_ref = refs[:6]
    refs = refs[6:]
    (
        enc_ref,
        a1_ref,
        a1m_ref,
        q_ref,
        kt_ref,
        ktm_ref,
        v_ref,
        vm_ref,
        e_ref,
        em_ref,
        att_ref,
        a2_ref,
        z_ref,
        gp_ref,
        a3_ref,
        a3m_ref,
        qw_ref,
        kwt_ref,
        kwtm_ref,
        vw_ref,
        vwm_ref,
        ew_ref,
        ewm_ref,
        watt_ref,
        stat_ref,
        last_ref,
        carry,
        bias,
        k_nat,
        km_nat,
        vt,
        vtm,
        hidden,
        row_buffer,
        row_sems,
    ) = refs[-35:]
    step = pl.program_id(0)
    rows_ref = sources.rows_of(
        refs[: len(sources.arrays)], segs, lambda s: s, place_ref[0], row_buffer, row_sems
    )
    width = wao_ref.shape[0]
    seg = q_ref.shape[2]
    slots = init_ref.shape[0]
    ff = win_ref.shape[0]

    @pl.when(step == 0)
    def _():
        carry[...] = mem0_ref[...].astype(F32)

    docs = rows_ref[seg : seg + 1, :].astype(F32)
    flag = rows_ref[seg + 1 : seg + 2, :].astype(F32)
    stat_ref[0, 5:6, :] = flag
    mem = jnp.where(flag[:, :slots] > 0.0, init_ref[...].astype(F32).T, carry[...])
    ga, gf, gw = gain_tiles(gains_ref)

    doc_rows = jnp.broadcast_to(docs, (128, seg)).T
    for at in range(0, seg, 128):
        bias[:, at : at + 128] = jnp.where(doc_rows == docs[:, at : at + 128], 0.0, MASKED)

    tokens = rows_ref[:seg, :].astype(F32).T
    r1 = inverse_rms(tokens)
    a1_ref[...] = (tokens * r1 * wide(ga, seg)).astype(BF16)
    rm = inverse_rms(mem)
    a1m_ref[0] = (mem * rm * ga[:, :slots]).astype(BF16)
    stat_ref[0, 0:1, :] = r1
    stat_ref[0, 4:5, :slots] = rm

    a1 = a1_ref[...]
    a1m = a1m_ref[0]
    q_ref[0] = (nn(wqkv_ref[:width, :], a1) * HEAD_DIM**-0.5).astype(BF16)
    kt = nn(wqkv_ref[width : 2 * width, :], a1).astype(BF16)
    kt_ref[0] = kt
    k_nat[...] = kt.T
    vt[...] = nn(wqkv_ref[2 * width :, :], a1).astype(BF16)
    v_ref[0] = vt[...].T
    ktm = nn(wqkv_ref[width : 2 * width, :], a1m).astype(BF16)
    ktm_ref[0] = ktm
    km_nat[...] = ktm.T
    vtm[...] = nn(wqkv_ref[2 * width :, :], a1m).astype(BF16)
    vm_ref[0] = vtm[...].T

    def pair(index, unused):
        lanes = pl.ds(pl.multiple_of(index * 128, 128), 128)
        keys = k_nat[:, lanes]
        mem_keys = km_nat[:, lanes]
        for half in range(2):
            head = index * 2 + half
            rows = pl.ds(pl.multiple_of(head * HEAD_DIM, HEAD_DIM), HEAD_DIM)
            queries = q_ref[0, rows, :]
            blank = jnp.zeros_like(queries)
            queries = jnp.concatenate([queries, blank] if half == 0 else [blank, queries], axis=0)
            scores = nn(keys, queries) + bias[...]
            mem_scores = nn(mem_keys, queries)
            top = jnp.maximum(
                jnp.max(scores, axis=0, keepdims=True), jnp.max(mem_scores, axis=0, keepdims=True)
            )
            raised = jnp.exp(scores - top)
            mem_raised = jnp.exp(mem_scores - top)
            inverse = 1.0 / (
                jnp.sum(raised, axis=0, keepdims=True) + jnp.sum(mem_raised, axis=0, keepdims=True)
            )
            raised = raised.astype(BF16)
            mem_raised = mem_raised.astype(BF16)
            e_ref[0, head] = raised
            em_ref[0, rows, :] = mem_raised
            mixed = nn(vt[rows, :], raised) + nn(vtm[rows, :], mem_raised)
            att_ref[rows, :] = (mixed * inverse).astype(BF16)
            stat_ref[0, pl.ds(8 + head, 1), :] = inverse
        return unused

    lax.fori_loop(0, HEADS // 2, pair, 0, unroll=HEADS // 2)

    h1 = rows_ref[:seg, :].astype(F32).T + nn(wao_ref[...], att_ref[...])
    r2 = inverse_rms(h1)
    stat_ref[0, 1:2, :] = r2
    a2_ref[...] = (h1 * r2 * wide(gf, seg)).astype(BF16)
    hidden[...] = h1
    a2 = a2_ref[...]
    for at in range(0, ff, 512):
        upper = nn(win_ref[at : at + 512, :], a2)
        square = upper * upper
        bent = jnp.tanh(upper * (SQRT_2_PI + (SQRT_2_PI * CUBIC) * square))
        cdf = 0.5 + 0.5 * bent
        z_ref[at : at + 512, :] = (upper * cdf).astype(BF16)
        slope = (0.5 * SQRT_2_PI) + (1.5 * SQRT_2_PI * CUBIC) * square
        gp_ref[0, at : at + 512, :] = (cdf + upper * (1.0 - bent * bent) * slope).astype(BF16)
    enc = hidden[...] + tn(wout_ref[...], z_ref[...])
    enc_ref[0, :seg, :] = enc.T.astype(BF16)
    r3 = inverse_rms(enc)
    stat_ref[0, 2:3, :] = r3
    a3_ref[...] = (enc * r3 * wide(gw, seg)).astype(BF16)
    a3m_ref[0] = (mem * rm * gw[:, :slots]).astype(BF16)
    a3 = a3_ref[...]
    a3m = a3m_ref[0]

    kwt = nn(ww_ref[width : 2 * width, :], a3).astype(BF16)
    kwt_ref[0] = kwt
    kw = kwt.T
    vwt = nn(ww_ref[2 * width :, :], a3).astype(BF16)
    vw_ref[0] = vwt.T
    kwtm = nn(ww_ref[width : 2 * width, :], a3m).astype(BF16)
    kwtm_ref[0] = kwtm
    vwtm = nn(ww_ref[2 * width :, :], a3m).astype(BF16)
    vwm_ref[0] = vwtm.T
    qwt = (nn(ww_ref[:width, :], a3m) * HEAD_DIM**-0.5).astype(BF16)
    own = head_mask(width, HEADS * slots)
    qw = jnp.where(own, nn(qwt, spread_ref[...]), 0.0).astype(BF16)
    qw_ref[0] = qw
    scores = nn(kw, qw)
    mem_scores = nn(kwtm.T, qw)
    slot_row = lax.broadcasted_iota(jnp.int32, mem_scores.shape, 0)
    slot_col = lax.broadcasted_iota(jnp.int32, mem_scores.shape, 1) % slots
    mem_scores = jnp.where(slot_row == slot_col, mem_scores, MASKED)
    top = jnp.maximum(
        jnp.max(scores, axis=0, keepdims=True), jnp.max(mem_scores, axis=0, keepdims=True)
    )
    raised = jnp.exp(scores - top)
    mem_raised = jnp.exp(mem_scores - top)
    inverse = 1.0 / (
        jnp.sum(raised, axis=0, keepdims=True) + jnp.sum(mem_raised, axis=0, keepdims=True)
    )
    stat_ref[0, 3:4, :] = inverse
    raised = raised.astype(BF16)
    mem_raised = mem_raised.astype(BF16)
    ew_ref[0] = raised
    ewm_ref[0] = mem_raised
    mixed = (nn(vwt, raised) + nn(vwtm, mem_raised)) * inverse
    watt = nn(jnp.where(own, mixed, 0.0).astype(BF16), fold_ref[...]).astype(BF16)
    watt_ref[0] = watt
    new_mem = (mem + nn(wwo_ref[...], watt)).astype(BF16).astype(F32)
    carry[...] = new_mem
    enc_ref[0, seg:, :] = new_mem.T.astype(BF16)
    last_ref[...] = new_mem.astype(BF16)


def chain_kernel(
    sources,
    segs,
    place_ref,
    carry0_ref,
    weights_gains_ref,
    spread_ref,
    fold_ref,
    wwo_ref,
    ww_ref,
    wout_ref,
    win_ref,
    wao_ref,
    wqkv_ref,
    a1m_ref,
    q_ref,
    vm_ref,
    em_ref,
    att_ref,
    a2_ref,
    gp_ref,
    a3_ref,
    a3m_ref,
    qw_ref,
    kwt_ref,
    kwtm_ref,
    vw_ref,
    vwm_ref,
    ew_ref,
    ewm_ref,
    stat_ref,
    *refs,
):
    source_refs, refs = refs[: len(sources.arrays)], refs[len(sources.arrays) :]
    bm_ref, gwkv_ref, gwm_ref, bf_ref, gu_ref, ba_ref, gh_ref, do_ref, dd_ref, dsm_ref = refs[:10]
    gkvm_ref, init_ref, gains_ref, sent_ref, carry, grad_buffer, grad_sems = refs[10:]
    gout_ref = sources.rows_of(
        source_refs, segs, lambda s: segs - 1 - s, place_ref[0], grad_buffer, grad_sems
    )
    step = pl.program_id(0)
    width = wao_ref.shape[0]
    ff = wout_ref.shape[0]
    seg = q_ref.shape[2]
    slots = a1m_ref.shape[2]
    reset = stat_ref[0, 5:6, :slots] > 0.0

    @pl.when(step == 0)
    def _():
        carry[...] = carry0_ref[...].astype(F32)
        init_ref[...] = jnp.zeros_like(init_ref)
        gains_ref[...] = jnp.zeros_like(gains_ref)

    ga, gf, gw = gain_tiles(weights_gains_ref)
    gai, gfi, gwi = 1.0 / ga, 1.0 / gf, 1.0 / gw
    own = head_mask(width, HEADS * slots)
    rm = stat_ref[0, 4:5, :slots]

    grad_mem = gout_ref[seg:, :].astype(F32).T + carry[...]
    branch_mem = grad_mem.astype(BF16)
    bm_ref[0] = branch_mem
    grad_watt = nn(wwo_ref[...], branch_mem).astype(BF16)
    inverse = stat_ref[0, 3:4, :]
    scaled = (jnp.where(own, nn(grad_watt, spread_ref[...]), 0.0) * inverse).astype(BF16)
    raised = ew_ref[0].astype(F32)
    mem_raised = ewm_ref[0].astype(F32)
    grad_probs = nn(vw_ref[0], scaled)
    mem_grad_probs = nn(vwm_ref[0], scaled)
    dots = (
        jnp.sum(raised * grad_probs, axis=0, keepdims=True)
        + jnp.sum(mem_raised * mem_grad_probs, axis=0, keepdims=True)
    ) * inverse
    grad_scores = (raised * (grad_probs - dots)).astype(BF16)
    mem_grad_scores = (mem_raised * (mem_grad_probs - dots)).astype(BF16)
    gwkv_ref[:width, :] = nt(qw_ref[0], grad_scores).astype(BF16)
    gwkv_ref[width:, :] = nt(scaled, ew_ref[0]).astype(BF16)
    grad_q = (nn(kwt_ref[0], grad_scores) + nn(kwtm_ref[0], mem_grad_scores)) * HEAD_DIM**-0.5
    gwm_ref[0, :width, :] = nn(jnp.where(own, grad_q, 0.0).astype(BF16), fold_ref[...]).astype(BF16)
    gwm_ref[0, width : 2 * width, :] = nt(qw_ref[0], mem_grad_scores).astype(BF16)
    gwm_ref[0, 2 * width :, :] = nt(scaled, ewm_ref[0]).astype(BF16)

    grad_a3 = nn(ww_ref[:, width:], gwkv_ref[...])
    grad_a3m = nn(ww_ref[...], gwm_ref[0])
    part, weighed = norm_back(
        grad_a3, a3_ref[...].astype(F32), stat_ref[0, 2:3, :], wide(gw, seg), wide(gwi, seg)
    )
    mem_part, mem_weighed = norm_back(
        grad_a3m, a3m_ref[0].astype(F32), rm, gw[:, :slots], gwi[:, :slots]
    )
    gains_ref[2] += lane_sums(weighed)
    gains_ref[2, :, :slots] += mem_weighed
    grad_mem_in = grad_mem + mem_part
    gh_ref[0] = gout_ref[:seg, :].astype(F32).T + part

    bf_ref[...] = gh_ref[0].astype(BF16)
    branch = bf_ref[...]
    for at in range(0, ff, 512):
        grad_z = nn(wout_ref[at : at + 512, :], branch)
        gu_ref[at : at + 512, :] = (grad_z * gp_ref[0, at : at + 512, :].astype(F32)).astype(BF16)
    grad_a2 = nn(win_ref[...], gu_ref[...])
    part, weighed = norm_back(
        grad_a2, a2_ref[...].astype(F32), stat_ref[0, 1:2, :], wide(gf, seg), wide(gfi, seg)
    )
    gains_ref[1] += lane_sums(weighed)
    gh_ref[0] += part

    ba_ref[...] = gh_ref[0].astype(BF16)
    grad_att = nn(wao_ref[...], ba_ref[...]).astype(BF16)
    products = grad_att.astype(F32) * att_ref[...].astype(F32)
    rows = []
    dots = []
    for head in range(HEADS):
        span = slice(head * HEAD_DIM, (head + 1) * HEAD_DIM)
        inverse = stat_ref[0, 8 + head : 9 + head, :]
        dots.append(jnp.sum(products[span, :], axis=0, keepdims=True) * inverse)
        rows.append((grad_att[span, :].astype(F32) * inverse).astype(BF16))
    scaled = jnp.concatenate(rows, axis=0)
    do_ref[0] = scaled
    dd_ref[0] = jnp.concatenate(dots, axis=0)
    mem_values = jnp.concatenate([vm_ref[0].astype(F32)] * HEADS, axis=0)
    mem_values = jnp.where(own, mem_values, 0.0).astype(BF16)
    grad_probs = nn(mem_values, scaled)
    parts = []
    for head in range(HEADS):
        span = slice(head * slots, (head + 1) * slots)
        parts.append(
            (em_ref[0, span, :].astype(F32) * (grad_probs[span, :] - dots[head])).astype(BF16)
        )
    grad_scores = jnp.concatenate(parts, axis=0)
    dsm_ref[0] = grad_scores
    grad_k = jnp.where(own, nt(q_ref[0], grad_scores), 0.0).astype(BF16)
    grad_v = jnp.where(own, nt(scaled, em_ref[0]), 0.0).astype(BF16)
    gkvm_ref[0, :width, :] = nn(grad_k, fold_ref[...]).astype(BF16)
    gkvm_ref[0, width:, :] = nn(grad_v, fold_ref[...]).astype(BF16)
    grad_a1m = nn(wqkv_ref[:, width:], gkvm_ref[0])
    mem_part, mem_weighed = norm_back(
        grad_a1m, a1m_ref[0].astype(F32), rm, ga[:, :slots], gai[:, :slots]
    )
    gains_ref[0, :, :slots] += mem_weighed
    grad_mem_in = grad_mem_in + mem_part
    init_ref[...] += jnp.where(reset, grad_mem_in, 0.0)
    carry[...] = jnp.where(reset, 0.0, grad_mem_in).astype(BF16).astype(F32)
    sent_ref[...] = carry[...].astype(BF16)


def attention_kernel(
    place_ref,
    do_ref,
    dd_ref,
    dsm_ref,
    gh_ref,
    q_ref,
    kt_ref,
    ktm_ref,
    v_ref,
    e_ref,
    a1_ref,
    stat_ref,
    gains_ref,
    wqkv_ref,
    *refs,
):
    gqkv_ref, out_ref, gain_ref = refs[-3:]
    pair = pl.program_id(1)
    width = wqkv_ref.shape[0]
    seg = q_ref.shape[2]
    for half in range(HEADS_A_STEP):
        head = pair * HEADS_A_STEP + half
        base = pl.multiple_of(head * HEAD_DIM, HEAD_DIM)
        span = slice(half * HEAD_DIM, (half + 1) * HEAD_DIM)
        grads = do_ref[0, span, :]
        blank = jnp.zeros_like(grads)
        padded = jnp.concatenate([grads, blank] if half % 2 == 0 else [blank, grads], axis=0)
        dots = dd_ref[0, pl.ds(head, 1), :]
        lanes = slice(half // 2 * 128, half // 2 * 128 + 128)
        grad_probs = nn(v_ref[0, :, lanes], padded)
        inner = (e_ref[0, half].astype(F32) * (grad_probs - dots)).astype(BF16)
        grad_q = nn(kt_ref[0, span, :], inner) + nn(ktm_ref[0, span, :], dsm_ref[0, span, :])
        gqkv_ref[pl.ds(base, HEAD_DIM), :] = (grad_q * HEAD_DIM**-0.5).astype(BF16)
        gqkv_ref[pl.ds(width + base, HEAD_DIM), :] = nt(q_ref[0, span, :], inner).astype(BF16)
        gqkv_ref[pl.ds(2 * width + base, HEAD_DIM), :] = nt(grads, e_ref[0, half]).astype(BF16)

    @pl.when((pl.program_id(0) == 0) & (pair == 0))
    def _():
        gain_ref[...] = jnp.zeros_like(gain_ref)

    @pl.when(pair == pl.num_programs(1) - 1)
    def _():
        grad_a1 = nn(wqkv_ref[...], gqkv_ref[...])
        (ga,) = gain_tiles(gains_ref, 1)
        part, weighed = norm_back(
            grad_a1,
            a1_ref[...].astype(F32),
            stat_ref[0, 0:1, :],
            wide(ga, seg),
            wide(1.0 / ga, seg),
        )
        gain_ref[...] += lane_sums(weighed)
        out_ref[0] = (gh_ref[0] + part).T.astype(BF16)


def whole(array):
    zeros = (0,) * array.ndim
    return pl.BlockSpec(array.shape, lambda *unused: zeros, pipeline_mode=pl.Buffered(1))


def params():
    return pltpu.CompilerParams(dimension_semantics=("arbitrary",), vmem_limit_bytes=VMEM_LIMIT)


def cost(microseconds):
    return pl.CostEstimate(
        flops=int(microseconds * 1e9), bytes_accessed=1 << 20, transcendentals=0
    )


def forward_chain(sources, place, mem0, consts, w):
    segs = consts["segs"]
    seg = consts["seg"]
    width, slots = mem0.shape
    ff = w["in_t"].shape[0]

    def flat(height):
        return (
            jax.ShapeDtypeStruct((height, segs * seg), BF16),
            pl.BlockSpec((height, seg), lambda s, f: (0, s)),
        )

    def stack(*shape, dtype=BF16):
        tail = (0,) * len(shape)
        return (
            jax.ShapeDtypeStruct((segs,) + shape, dtype),
            pl.BlockSpec((1,) + shape, lambda s, f: (s,) + tail),
        )

    outs = dict(
        enc=stack(seg + slots, width),
        a1=flat(width),
        a1m=stack(width, slots),
        q=stack(width, seg),
        kt=stack(width, seg),
        ktm=stack(width, slots),
        v=stack(seg, width),
        vm=stack(slots, width),
        e=stack(HEADS, seg, seg),
        em=stack(HEADS * slots, seg),
        att=flat(width),
        a2=flat(width),
        z=flat(ff),
        gp=stack(ff, seg),
        a3=flat(width),
        a3m=stack(width, slots),
        qw=stack(width, HEADS * slots),
        kwt=stack(width, seg),
        kwtm=stack(width, slots),
        vw=stack(seg, width),
        vwm=stack(slots, width),
        ew=stack(seg, HEADS * slots),
        ewm=stack(slots, HEADS * slots),
        watt=stack(width, slots),
        stat=stack(16, seg, dtype=F32),
        last=(
            jax.ShapeDtypeStruct((width, slots), BF16),
            pl.BlockSpec((width, slots), lambda s, f: (0, 0)),
        ),
    )
    fixed = [
        mem0,
        consts["init"],
        consts["gains"],
        consts["spread"],
        consts["fold"],
    ]
    weights = [w[name] for name in ("qkv_t", "ao_t", "in_t", "out", "write_t", "wo_t")]
    results = pl.pallas_call(
        lambda *refs: forward_kernel(sources, segs, *refs),
        grid_spec=pltpu.PrefetchScalarGridSpec(
            num_scalar_prefetch=1,
            grid=(segs,),
            in_specs=[whole(a) for a in fixed + weights]
            + [pl.BlockSpec(memory_space=pl.ANY)] * len(sources.arrays),
            out_specs=[spec for _, spec in outs.values()],
            scratch_shapes=[
                pltpu.VMEM((width, slots), F32),
                pltpu.VMEM((seg, seg), F32),
                pltpu.VMEM((seg, width), BF16),
                pltpu.VMEM((slots, width), BF16),
                pltpu.VMEM((width, seg), BF16),
                pltpu.VMEM((width, slots), BF16),
                pltpu.VMEM((width, seg), F32),
                pltpu.VMEM((2, seg + 16, width), BF16),
                pltpu.SemaphoreType.DMA((2,)),
            ],
        ),
        out_shape=[shape for shape, _ in outs.values()],
        compiler_params=params(),
        cost_estimate=cost(15 * segs),
        name="forward_chain",
    )(place, *fixed, *weights, *sources.arrays)
    return dict(zip(outs, results))


def backward_chain(kept, sources, place, carry0, consts, w):
    segs = consts["segs"]
    width, slots = kept["a1m"].shape[1:]
    seg = kept["q"].shape[2]
    ff = kept["gp"].shape[1]
    last = segs - 1

    def flat(height):
        return (
            jax.ShapeDtypeStruct((height, segs * seg), BF16),
            pl.BlockSpec((height, seg), lambda s, f: (0, last - s)),
        )

    def stack(*shape, dtype=BF16):
        tail = (0,) * len(shape)
        return (
            jax.ShapeDtypeStruct((segs,) + shape, dtype),
            pl.BlockSpec((1,) + shape, lambda s, f: (last - s,) + tail),
        )

    def single(*shape, dtype=F32):
        tail = (0,) * len(shape)
        return (jax.ShapeDtypeStruct(shape, dtype), pl.BlockSpec(shape, lambda s, f: tail))

    outs = dict(
        bm=stack(width, slots),
        gwkv=flat(2 * width),
        gwm=stack(3 * width, slots),
        bf=flat(width),
        gu=flat(ff),
        ba=flat(width),
        gh=stack(width, seg, dtype=F32),
        do=stack(width, seg),
        dd=stack(HEADS, seg, dtype=F32),
        dsm=stack(HEADS * slots, seg),
        gkvm=stack(2 * width, slots),
        init=single(width, slots),
        gains=single(3, width, 128),
        sent=single(width, slots, dtype=BF16),
    )
    fixed = [
        carry0,
        consts["gains"],
        consts["spread"],
        consts["fold"],
    ]
    weights = [w[name] for name in ("wo", "write", "out", "in", "ao", "qkv")]
    blocked = ["a1m", "q", "vm", "em", "att", "a2", "gp", "a3", "a3m", "qw"]
    blocked += ["kwt", "kwtm", "vw", "vwm", "ew", "ewm", "stat"]

    def spec_of(array):
        if array.ndim == 2:
            return pl.BlockSpec((array.shape[0], seg), lambda s, f: (0, last - s))
        tail = (0,) * (array.ndim - 1)
        return pl.BlockSpec((1,) + array.shape[1:], lambda s, f: (last - s,) + tail)

    results = pl.pallas_call(
        lambda *refs: chain_kernel(sources, segs, *refs),
        grid_spec=pltpu.PrefetchScalarGridSpec(
            num_scalar_prefetch=1,
            grid=(segs,),
            in_specs=[whole(a) for a in fixed + weights]
            + [spec_of(kept[name]) for name in blocked]
            + [pl.BlockSpec(memory_space=pl.ANY)] * len(sources.arrays),
            out_specs=[spec for _, spec in outs.values()],
            scratch_shapes=[
                pltpu.VMEM((width, slots), F32),
                pltpu.VMEM((2, seg + slots, width), BF16),
                pltpu.SemaphoreType.DMA((2,)),
            ],
        ),
        out_shape=[shape for shape, _ in outs.values()],
        compiler_params=params(),
        cost_estimate=cost(11 * segs),
        name="backward_chain",
    )(place, *fixed, *weights, *[kept[name] for name in blocked], *sources.arrays)
    return dict(zip(outs, results))


def attention_back(kept, grads, which, consts, w, before):
    segs, width, seg = kept["q"].shape
    count = which.shape[0]
    pair = HEADS_A_STEP * HEAD_DIM

    def by_pair(rows, lanes):
        return pl.BlockSpec((1, rows, lanes), lambda s, h, f: (f[s], h, 0))

    def by_seg(array):
        tail = (0,) * (array.ndim - 1)
        return pl.BlockSpec((1,) + array.shape[1:], lambda s, h, f: (f[s],) + tail)

    inputs = [
        (grads["do"], by_pair(pair, seg)),
        (grads["dd"], by_seg(grads["dd"])),
        (grads["dsm"], by_pair(pair, seg)),
        (grads["gh"], by_seg(grads["gh"])),
        (kept["q"], by_pair(pair, seg)),
        (kept["kt"], by_pair(pair, seg)),
        (kept["ktm"], by_pair(pair, kept["ktm"].shape[2])),
        (kept["v"], pl.BlockSpec((1, seg, pair), lambda s, h, f: (f[s], 0, h))),
        (kept["e"], pl.BlockSpec((1, HEADS_A_STEP, seg, seg), lambda s, h, f: (f[s], h, 0, 0))),
        (kept["a1"], pl.BlockSpec((width, seg), lambda s, h, f: (0, f[s]))),
        (kept["stat"], by_seg(kept["stat"])),
        (consts["gains"], whole(consts["gains"])),
        (w["qkv"], whole(w["qkv"])),
    ]
    passed = [] if before is None else [before]
    return pl.pallas_call(
        attention_kernel,
        grid_spec=pltpu.PrefetchScalarGridSpec(
            num_scalar_prefetch=1,
            grid=(count, HEADS // HEADS_A_STEP),
            in_specs=[spec for _, spec in inputs]
            + [pl.BlockSpec(memory_space=pl.ANY)] * len(passed),
            out_specs=[
                pl.BlockSpec((3 * width, seg), lambda s, h, f: (0, f[s])),
                pl.BlockSpec((1, seg, width), lambda s, h, f: (s, 0, 0)),
                pl.BlockSpec((width, 128), lambda s, h, f: (0, 0)),
            ],
        ),
        out_shape=[
            jax.ShapeDtypeStruct((3 * width, segs * seg), BF16),
            jax.ShapeDtypeStruct((count, seg, width), BF16),
            jax.ShapeDtypeStruct((width, 128), F32),
        ],
        input_output_aliases={1 + len(inputs): 0} if passed else {},
        compiler_params=pltpu.CompilerParams(
            dimension_semantics=("arbitrary", "arbitrary"), vmem_limit_bytes=VMEM_LIMIT
        ),
        cost_estimate=cost(10 * count),
        name="attention_back",
    )(which, *[array for array, _ in inputs], *passed)


def swap_pairs(value, axis, mask):
    size = lax.axis_size(axis)
    return lax.ppermute(value, axis, [(i, i ^ mask) for i in range(size)])


def sum_phases(dp_first=False):
    section = [("section", 1 << at) for at in range(lax.axis_size("section").bit_length() - 1)]
    dp = [("dp", 1 << at) for at in range(lax.axis_size("dp").bit_length() - 1)]
    phases = [(step, step) for step in section[:1]]
    crossed = []
    if len(section) > 1 and dp:
        crossed = [(dp[0], section[1]), (section[1], dp[0])]
        section, dp = section[2:], dp[1:]
    else:
        section = section[1:]
    straight = [(step, step) for step in dp + section]
    return phases + (straight + crossed if dp_first else crossed + straight)


def phase_swap(value, phase):
    sections, dps = lax.axis_size("section"), lax.axis_size("dp")
    route = []
    for section in range(sections):
        axis, mask = phase[section % 2]
        for dp in range(dps):
            to = ((section ^ mask) * dps + dp) if axis == "section" else (section * dps + (dp ^ mask))
            route.append((section * dps + dp, to))
    return lax.ppermute(value, ("section", "dp"), route)


def phase_bit(phase):
    bits = [(lax.axis_index(axis) // mask) % 2 for axis, mask in phase]
    return jnp.where(lax.axis_index("section") % 2 == 0, bits[0], bits[1])


def half_of(value, side):
    half = value.shape[0] // 2
    return lax.dynamic_slice_in_dim(value, side * half, half, 0)


def fetch(source, target, sem):
    copy = pltpu.make_async_copy(source, target, sem)
    copy.start()
    return copy


def slot_sum(left, right):
    join = lambda ref: jnp.concatenate([ref[at] for at in range(ref.shape[0])], axis=1)
    return nt(join(left), join(right))


def early_weights_kernel(
    side_ref, a2_ref, gu_ref, bf_ref, z_ref, a3_ref, gwkv_ref, a3m_ref, gwm_ref, watt_ref, bm_ref, *refs
):
    ffn_ref, write_ref, a2, gu, z, bf, a3, gw, a3m, gwm, left, right, staged, in_sems, out_sems = refs
    side = side_ref[0]
    width = a2.shape[0]
    folds = gu.shape[0]
    base = side * (folds * width)
    loads = []

    def load(source, target):
        loads.append(fetch(source, target, in_sems.at[len(loads)]))

    def wait(count):
        for _ in range(count):
            loads[wait.done].wait()
            wait.done += 1

    wait.done = 0
    load(a2_ref, a2)
    for at in range(folds):
        rows = pl.ds(pl.multiple_of(base + at * width, width), width)
        load(gu_ref.at[rows, :], gu.at[at])
    load(bf_ref, bf)
    for at in range(folds):
        rows = pl.ds(pl.multiple_of(base + at * width, width), width)
        load(z_ref.at[rows, :], z.at[at])
    load(a3_ref, a3)
    load(gwkv_ref.at[pl.ds(pl.multiple_of(side * width, width), width), :], gw)
    load(a3m_ref, a3m)
    load(gwm_ref.at[:, pl.ds(pl.multiple_of((1 + side) * width, width), width), :], gwm)
    last = in_sems.at[len(loads)]

    @pl.when(side == 0)
    def _():
        pltpu.make_async_copy(a3m_ref, left, last).start()
        pltpu.make_async_copy(gwm_ref.at[:, pl.ds(0, width), :], right, last).start()

    @pl.when(side == 1)
    def _():
        pltpu.make_async_copy(watt_ref, left, last).start()
        pltpu.make_async_copy(bm_ref, right, last).start()

    stores = []

    def put(tile, value):
        columns = slice(tile * width, (tile + 1) * width)
        staged[:, columns] = value.astype(BF16)
        out, first = (ffn_ref, 0) if tile < 2 * folds else (write_ref, 2 * folds)
        target = out.at[:, pl.ds((tile - first) * width, width)]
        stores.append(fetch(staged.at[:, columns], target, out_sems.at[tile]))

    wait(1)
    for at in range(folds):
        wait(1)
        put(at, nt(a2[...], gu[at]))
    wait(1)
    for at in range(folds):
        wait(1)
        put(folds + at, nt(z[at], bf[...]))
    wait(4)
    put(2 * folds, nt(a3[...], gw[...]) + slot_sum(a3m, gwm))
    pltpu.make_async_copy(watt_ref, left, last).wait()
    pltpu.make_async_copy(bm_ref, right, last).wait()
    put(2 * folds + 1, slot_sum(left, right))
    for store in stores:
        store.wait()


def early_weights(kept, grads, side):
    width, tokens = kept["a2"].shape
    folds = kept["z"].shape[0] // 2 // width
    inputs = [kept["a2"], grads["gu"], grads["bf"], kept["z"], kept["a3"], grads["gwkv"]]
    inputs += [kept["a3m"], grads["gwm"], kept["watt"], grads["bm"]]
    anywhere = pl.BlockSpec(memory_space=pl.ANY)
    full = pltpu.VMEM((width, tokens), BF16)
    several = pltpu.VMEM((folds, width, tokens), BF16)
    slots = pltpu.VMEM(kept["a3m"].shape, BF16)
    out = jax.ShapeDtypeStruct((width, (2 * folds + 2) * width), BF16)
    return pl.pallas_call(
        early_weights_kernel,
        grid_spec=pltpu.PrefetchScalarGridSpec(
            num_scalar_prefetch=1,
            grid=(1,),
            in_specs=[anywhere] * len(inputs),
            out_specs=[anywhere] * 2,
            scratch_shapes=[full, several, several, full, full, full]
            + [slots] * 4
            + [
                pltpu.VMEM(out.shape, BF16),
                pltpu.SemaphoreType.DMA((7 + 2 * folds,)),
                pltpu.SemaphoreType.DMA((2 * folds + 2,)),
            ],
        ),
        out_shape=[
            jax.ShapeDtypeStruct((width, 2 * folds * width), BF16),
            jax.ShapeDtypeStruct((width, 2 * width), BF16),
        ],
        compiler_params=params(),
        cost_estimate=cost(9),
        name="early_weights",
    )(side, *inputs)


def late_weights_kernel(count, side_ref, a1_ref, gqkv_ref, att_ref, ba_ref, a1m_ref, gkvm_ref, *refs):
    init_ref, gains_ref, refs = refs[0], refs[1], refs[2:]
    part_refs, refs = refs[:count], refs[count:]
    out_ref, a1, main, left, right, a1m, gkvm, init, gains, parts, staged, in_sems, out_sems = refs
    side = side_ref[0]
    width = a1.shape[0]
    slots = init.shape[1]
    rows = pl.ds(pl.multiple_of((1 + side) * width, width), width)
    kv_rows = pl.ds(pl.multiple_of(side * width, width), width)
    loads = [
        fetch(a1_ref, a1, in_sems.at[0]),
        fetch(gqkv_ref.at[rows, :], main, in_sems.at[1]),
        fetch(a1m_ref, a1m, in_sems.at[2]),
        fetch(gkvm_ref.at[:, kv_rows, :], gkvm, in_sems.at[3]),
    ]

    @pl.when(side == 0)
    def _():
        pltpu.make_async_copy(a1_ref, left, in_sems.at[4]).start()
        pltpu.make_async_copy(gqkv_ref.at[pl.ds(0, width), :], right, in_sems.at[5]).start()

    @pl.when(side == 1)
    def _():
        pltpu.make_async_copy(att_ref, left, in_sems.at[4]).start()
        pltpu.make_async_copy(ba_ref, right, in_sems.at[5]).start()

    others = [fetch(init_ref, init, in_sems.at[6]), fetch(gains_ref, gains, in_sems.at[7])]
    others += [fetch(ref, parts.at[at], in_sems.at[8 + at]) for at, ref in enumerate(part_refs)]
    stores = []

    def put(columns, value):
        staged[:, columns] = value.astype(BF16)
        stores.append(fetch(staged.at[:, columns], out_ref.at[:, columns], out_sems.at[len(stores)]))

    for load in loads:
        load.wait()
    put(slice(0, width), nt(a1[...], main[...]) + slot_sum(a1m, gkvm))
    pltpu.make_async_copy(att_ref, left, in_sems.at[4]).wait()
    pltpu.make_async_copy(ba_ref, right, in_sems.at[5]).wait()
    put(slice(width, 2 * width), nt(left[...], right[...]))
    for load in others:
        load.wait()
    columns = [gains[0], gains[1], gains[2]]
    for at in range(count):
        columns[0] = columns[0] + parts[at]
    lane = lax.broadcasted_iota(jnp.int32, init.shape, 1)
    extras = jnp.zeros(init.shape, F32)
    for at, column in enumerate(columns):
        extras = jnp.where(lane == at, jnp.sum(column, axis=1, keepdims=True), extras)
    extras = jnp.where(side == 0, init[...], extras)
    extras = jnp.concatenate([extras, jnp.zeros_like(extras)], axis=1)
    put(slice(2 * width, 2 * width + 2 * slots), extras)
    for store in stores:
        store.wait()


def late_weights(kept, grads, gqkv, gain_parts, side):
    width, tokens = kept["a1"].shape
    count = len(gain_parts)
    inputs = [kept["a1"], gqkv, kept["att"], grads["ba"], kept["a1m"], grads["gkvm"]]
    inputs += [grads["init"], grads["gains"]] + list(gain_parts)
    slots = grads["init"].shape[1]
    anywhere = pl.BlockSpec(memory_space=pl.ANY)
    full = pltpu.VMEM((width, tokens), BF16)
    small = pltpu.VMEM(kept["a1m"].shape, BF16)
    out = jax.ShapeDtypeStruct((width, 2 * width + 2 * slots), BF16)
    return pl.pallas_call(
        lambda *refs: late_weights_kernel(count, *refs),
        grid_spec=pltpu.PrefetchScalarGridSpec(
            num_scalar_prefetch=1,
            grid=(1,),
            in_specs=[anywhere] * len(inputs),
            out_specs=anywhere,
            scratch_shapes=[full] * 4
            + [small] * 2
            + [
                pltpu.VMEM(grads["init"].shape, F32),
                pltpu.VMEM(grads["gains"].shape, F32),
                pltpu.VMEM((count,) + gain_parts[0].shape, F32),
                pltpu.VMEM(out.shape, BF16),
                pltpu.SemaphoreType.DMA((8 + count,)),
                pltpu.SemaphoreType.DMA((3,)),
            ],
        ),
        out_shape=out,
        compiler_params=params(),
        cost_estimate=cost(4),
        name="late_weights",
    )(side, *inputs)


class Sum:
    def __init__(self, value, share, halve_all=False, dp_first=False):
        self.phases = sum_phases(dp_first)
        inner = self.phases[1:]
        self.value = value
        self.share = share
        halvings = 0
        most = len(inner) - (0 if halve_all else 1)
        while halvings < most and value.shape[0] >> (halvings + 1) >= 16:
            halvings += 1
        self.halved = inner[:halvings]
        self.steps = [("halve", phase) for phase in self.halved]
        self.steps += [("add", phase) for phase in inner[halvings:]]
        self.steps += [("double", phase) for phase in reversed(self.halved)]
        self.steps += [("last", self.phases[0])]
        self.started = None

    def prepare(self):
        kind, phase = self.steps.pop(0)
        if kind == "halve":
            bit = phase_bit(phase)
            value = self.value
            self.sent, self.value = half_of(value, 1 - bit), half_of(value, bit)
            if self.share is not None:
                self.sent = self.sent + half_of(self.share, 1 - bit)
                self.value = self.value + half_of(self.share, bit)
        else:
            if self.share is not None:
                self.value = self.value + self.share
            self.sent = self.value
        self.share = None
        self.ready = (kind, phase)

    def launch(self):
        kind, phase = self.ready
        if kind == "last" and isinstance(self.sent, tuple):
            self.started = (kind, tuple(phase_swap(piece, phase) for piece in self.sent))
        else:
            self.started = (kind, phase_swap(self.sent, phase))

    def finish(self, *after):
        kind, other = self.started
        self.started = None
        other, after = lax.optimization_barrier((other, after))
        if kind in ("halve", "add"):
            self.value = self.value + other
        elif kind == "double" and len(self.steps) == 1:
            self.value = (self.value, other)
        elif kind == "double":
            self.value = jnp.concatenate([self.value, other], axis=0)
        elif isinstance(other, tuple):
            self.value = (self.value, other)
        else:
            self.value = ((self.value,), (other,))
        return list(after)

    def places(self):
        own = sum(phase_bit(phase) << at for at, phase in enumerate(reversed(self.halved)))
        swapped = [(late, early) for early, late in self.halved]
        other = sum(phase_bit(phase) << at for at, phase in enumerate(reversed(swapped)))
        numbers = jnp.stack([phase_bit(self.phases[0]), jnp.int32(own), jnp.int32(other)])
        return numbers.astype(jnp.int32), 1 << len(self.halved)


def advance(totals, *after, extra=()):
    going = []
    for total in totals:
        if total.started is not None:
            total.finish(*after)
        if total.steps:
            total.prepare()
            going.append(total)
    joined, extra = lax.optimization_barrier(([total.sent for total in going], list(extra)))
    for total, sent in zip(going, joined):
        if total.value is total.sent:
            total.value = sent
        total.sent = sent
        total.launch()
    return joined, extra


def unpack_kernel(count, parts, regions, kept, place_ref, *refs):
    own_refs, other_refs, refs = refs[:parts], refs[parts : 2 * parts], refs[2 * parts :]
    gains_ref = None
    if kept:
        gains_ref, refs = refs[0], refs[1:]
    outs = len(refs) // 2
    out_refs, staged, sems = refs[:outs], refs[outs : 2 * outs], refs[2 * outs]
    each = count // parts
    rows = own_refs[0].shape[0] // each
    height = rows * count

    def take(refs, side, number, sem):
        copies = []
        for start, stop, at, top, left in regions[side]:
            for block in range(count):
                target = pl.multiple_of(top + (block ^ place_ref[number]) * rows, rows)
                inner = (block % each) * rows
                value = refs[block // each][inner : inner + rows, start:stop].astype(F32)
                staged[at][pl.ds(target, rows), left : left + stop - start] = value
            if at >= outs - kept:
                continue
            slab = (pl.ds(top, height), pl.ds(left, stop - start))
            copies.append((staged[at].at[slab], out_refs[at].at[slab], sems.at[sem + len(copies)]))
            pltpu.make_async_copy(*copies[-1]).start()
        return copies

    for side in range(2):

        @pl.when(place_ref[0] == side)
        def _():
            copies = take(own_refs, side, 1, 0)
            copies += take(other_refs, 1 - side, 2, len(copies))
            for copy in copies:
                pltpu.make_async_copy(*copy).wait()

    if kept:
        init_ref, total_ref = out_refs[outs - 2 :]
        init_ref[...] = staged[outs - 2][...].T[: init_ref.shape[0], :]
        total_ref[...] = staged[outs - 1][...].T[: total_ref.shape[0], :] / gains_ref[...]


def unpacked(total, regions, shapes, slots=0, gains=None):
    own, other = total.value
    places, count = total.places()
    parts = len(own)
    kept = 0 if gains is None else 2
    vmem = pl.BlockSpec(memory_space=pltpu.VMEM)
    outs = [jax.ShapeDtypeStruct(shape, F32) for shape in shapes[: len(shapes) - kept]]
    specs = [pl.BlockSpec(memory_space=pl.ANY)] * len(outs)
    inputs = [*own, *other]
    if kept:
        inputs.append(gains)
        outs += [jax.ShapeDtypeStruct((rows, shapes[-1][0]), F32) for rows in (slots, gains.shape[0])]
        specs += [vmem] * 2
    return pl.pallas_call(
        lambda *refs: unpack_kernel(count, parts, regions, kept, *refs),
        in_specs=[pl.BlockSpec(memory_space=pltpu.SMEM)] + [vmem] * len(inputs),
        out_specs=specs,
        out_shape=outs,
        scratch_shapes=[pltpu.VMEM(shape, F32) for shape in shapes]
        + [pltpu.SemaphoreType.DMA((len(regions[0]) + len(regions[1]),))],
        compiler_params=pltpu.CompilerParams(vmem_limit_bytes=VMEM_LIMIT),
        cost_estimate=cost(4),
        name="unpack",
    )(places, *inputs)


def pieces_in(value, place):
    parts = [lax.dynamic_index_in_dim(value, place, 0, keepdims=True)]
    sent = []
    for mask in range(1, lax.axis_size("section")):
        sent.append(lax.dynamic_index_in_dim(value, place ^ mask, 0, keepdims=True))
        parts.append(swap_pairs(sent[-1], "section", mask))
    return in_rank_order(jnp.concatenate(parts, axis=0), place), sent, parts[1:]


def in_rank_order(pieces, place):
    count = pieces.shape[0]
    return jnp.stack(
        [lax.dynamic_index_in_dim(pieces, at ^ place, 0, keepdims=False) for at in range(count)]
    )


def sources_in(arrays, place):
    sections = lax.axis_size("section")
    sent = []
    for mask in range(1, sections):
        picked = [lax.dynamic_index_in_dim(a, place ^ mask, 0, keepdims=True) for a in arrays]
        sent.append(jnp.concatenate(picked, axis=1))
    sent = list(lax.optimization_barrier(tuple(sent)))
    pieces = [swap_pairs(value, "section", mask + 1) for mask, value in enumerate(sent)]
    own = len(arrays)

    def choose(at, here):
        yield (at ^ here) == 0, [(number, here) for number in range(own)]
        for other in range(1, sections):
            yield (at ^ here) == other, [(own + other - 1, 0)]

    return Sources(list(arrays) + pieces, choose), pieces, sent


def gathered_sources(arrays, chunks):
    rows = gathered_in(jnp.concatenate(arrays, axis=1), chunks)
    return Sources([rows], lambda at, here: [(at >= 0, [(0, at)])])


def gathered_in(value, chunks):
    place = lax.axis_index("section")
    gathered = lax.all_gather(value, "section")
    own = lax.dynamic_index_in_dim(gathered, place // chunks, 1, keepdims=False)
    count = gathered.shape[0] // chunks
    return lax.dynamic_slice_in_dim(own, (place % chunks) * count, count, 0)


def gathered_out(value, chunks):
    place = lax.axis_index("section")
    gathered = lax.all_gather(value, "section")
    sections = gathered.shape[0]
    by_stream = gathered.reshape((sections // chunks, chunks * value.shape[0]) + value.shape[1:])
    return lax.dynamic_index_in_dim(by_stream, place, 1, keepdims=False)


def tied(value, *others):
    return lax.optimization_barrier((value,) + others)[0]


def body(
    tokens,
    doc_ids,
    reset_flags,
    attn_gain,
    w_qkv,
    w_attn_out,
    ffn_gain,
    w_in,
    w_out,
    write_gain,
    w_write,
    w_write_out,
    init_memory,
    out_grad,
    memory_grad,
):
    streams, _, seg, width = tokens.shape
    slots = init_memory.shape[0]
    sections = lax.axis_size("section")
    chunks = sections // streams
    segs = sections // chunks
    place = lax.axis_index("section")

    spread = np.tile(np.eye(slots, dtype=np.float32), (1, HEADS))
    consts = dict(
        segs=segs,
        seg=seg,
        init=init_memory,
        gains=jnp.stack([attn_gain, ffn_gain, write_gain]).astype(F32),
        spread=jnp.asarray(spread, BF16),
        fold=jnp.asarray(spread.T, BF16),
    )
    w = dict(
        qkv=w_qkv,
        ao=w_attn_out,
        out=w_out,
        write=w_write,
        wo=w_write_out,
        qkv_t=w_qkv.T,
        ao_t=w_attn_out.T,
        in_t=w_in.T,
        write_t=w_write.T,
        wo_t=w_write_out.T,
    )
    w["in"] = w_in

    marks = jnp.concatenate(
        [doc_ids[:, 0], jnp.broadcast_to(reset_flags, (streams, seg))], axis=1
    ).reshape(streams, 2, seg)
    marks = jnp.pad(marks, ((0, 0), (0, 14), (0, 0))).astype(BF16)
    parts_in = [tokens[:, 0], marks]
    grads_in = [out_grad[:, 0], memory_grad[:, 0]]
    empty = jnp.zeros((width, slots), BF16)
    if chunks == 1:
        rows, pieces, _ = sources_in(parts_in, place)
        gout, _, sent = sources_in([tied(value, *pieces) for value in grads_in], place)
        xor = place
    else:
        rows = gathered_sources(parts_in, chunks)
        gout = gathered_sources(grads_in, chunks)
        sent = []
        xor = 0
    xor = jnp.full((1,), xor, jnp.int32)

    arriving = empty
    then = tied(xor, *sent)
    for turn in range(chunks):
        kept = forward_chain(rows, then, arriving, consts, w)
        if turn < chunks - 1:
            arriving = lax.ppermute(
                kept["last"], "section", [(i, i + 1) for i in range(sections - 1)]
            )
    if chunks == 1:
        done, sent, pieces = pieces_in(kept["enc"], place)
        then = tied(xor, *sent)
    else:
        done = gathered_out(kept["enc"], chunks)
        pieces = []
        then = xor

    returning = empty
    for turn in range(chunks):
        grads = backward_chain(kept, gout, then, returning, consts, w)
        if turn < chunks - 1:
            returning = lax.ppermute(
                grads["sent"], "section", [(i + 1, i) for i in range(sections - 1)]
            )

    ff = w_in.shape[1]
    folds = ff // width
    cores = sum_phases()[0]
    side = phase_bit(cores).reshape(1)
    grads = dict(grads, gu=tied(grads['gu'], *pieces))
    sent = early_weights(kept, grads, 1 - side)
    shares = [phase_swap(value, cores) for value in sent]
    halves = early_weights(kept, grads, tied(side, *sent))
    ffn = Sum(halves[0], shares[0], halve_all=True)
    write = Sum(halves[1], shares[1], dp_first=True)
    groups = [ffn, write]
    after, _ = advance(groups)
    turns = [[2], [0, 3], [1]] if segs == 4 else [[at] for at in range(segs)]
    gqkv = None
    gain_parts = []
    outgoing, incoming = {}, {}
    leaving, arriving = [], []
    for turn in turns:
        which = tied(jnp.concatenate([xor ^ at for at in turn]), *after, *arriving)
        gqkv, out, part = attention_back(kept, grads, which, consts, w, gqkv)
        gain_parts.append(part)
        after, (out,) = advance(groups, part, extra=[out])
        arriving, leaving = leaving, []
        for number, at in enumerate(turn):
            outgoing[at] = out[number : number + 1]
            if chunks == 1 and at:
                incoming[at] = swap_pairs(outgoing[at], "section", at)
                leaving.append(incoming[at])

    sent = late_weights(kept, grads, gqkv, gain_parts, tied(1 - side, *after, *arriving))
    after, (sent,) = advance(groups, sent, extra=[sent])
    share = phase_swap(sent, cores)
    mine = tied(side, sent, *after, *leaving)
    late = Sum(late_weights(kept, grads, gqkv, gain_parts, mine), share)

    half = ff // 2

    def paired(number, start, at):
        main = (start, start + width, at, 0, (1 + number) * width)
        other = (start + width, start + 2 * width, at + number, 0, 0)
        return [main, other]

    ffn_regions = [
        [(0, half, 0, 0, number * half)]
        + [
            (half + at * width, half + (at + 1) * width, 1, number * half + at * width, 0)
            for at in range(half // width)
        ]
        for number in range(2)
    ]
    write_regions = [paired(number, 0, 0) for number in range(2)]
    late_regions = [
        paired(number, 0, 0) + [(2 * width, 2 * width + 128, 2 + number, 0, 0)]
        for number in range(2)
    ]
    square, triple = (width, width), (width, 3 * width)
    advance([late])
    advance(groups, late.sent)
    if chunks == 1:
        incoming[0] = tied(outgoing[0], late.sent)
        back = in_rank_order(jnp.concatenate([incoming[at] for at in range(segs)]), place)
    else:
        back = gathered_out(jnp.concatenate([outgoing[at] for at in range(segs)]), chunks)
    (token_grads,) = late.finish(back.astype(F32))
    advance([late])
    advance(groups, late.sent)
    (done,) = late.finish(done)
    advance([late])
    advance([late])
    advance(groups, late.sent)
    advance([late])
    advance([late])
    while ffn.steps or write.steps:
        advance(groups, late.sent)
    if late.steps:
        advance([late])
    advance(groups, late.sent)
    grad_in, grad_out = unpacked(ffn, ffn_regions, [(width, ff), (ff, width)])
    grad_write, grad_wo = unpacked(write, write_regions, [triple, square])
    grad_in, grad_write = late.finish(grad_in, grad_write)
    while late.steps:
        advance([late])
    if late.started is not None:
        late.finish()
    grad_qkv, grad_ao, grad_init, gains = unpacked(
        late, late_regions, [triple, square, (width, 128), (width, 128)], slots, consts["gains"]
    )
    return (
        done[:, None, :seg],
        done[:, None, seg:],
        token_grads[:, None],
        gains[0],
        grad_qkv,
        grad_ao,
        gains[1],
        grad_in,
        grad_out,
        gains[2],
        grad_write,
        grad_wo,
        grad_init,
    )


def solution(mesh):
    local = P("dp", "section")
    return jax.shard_map(
        body,
        mesh=mesh,
        in_specs=(local,) * 3 + (P(),) * 10 + (local,) * 2,
        out_specs=(local,) * 3 + (P(),) * 10,
        check_vma=False,
    )
```

profile of v0, /device:TPU:0, one launch (start us, length us, event | category | flops | bytes accessed | tf_op | source)
XLA Modules:
  0.0 337.6 jit_solution(2755332633541451048)
XLA Ops:
  2.2 1.5 dynamic-slice_bitcast_fusion
  3.7 0.8 pad_maximum_fusion.9
  4.5 1.0 pad_maximum_fusion.7
  6.0 2.5 collective-permute-start.1
  8.7 2.5 copy.34
  11.2 2.7 copy.35
  14.0 1.6 copy.32
  15.5 2.2 copy.36
  17.7 2.1 copy.33
  20.4 1.6 collective-permute-done.1.refs_15_
  22.0 11.2 %collective-permute-done.2.refs_16_ = bf16[1,528,512]{2,1,0:T(8,128)(2,1)} collective-permute-done((bf16[1,528,512]{2,1,0:T(8,128)(2,1)}, bf16[1,528,512]{2,1,0:T(8,128)(2,1)}, u32[]{:S(2)}, u32[]{:S(2)}) %collective-permute-start.2) | collective-permute-done | bytes 540704 | tf_op jit(solution)/shard_map/ppermute | solution.py:735
  33.7 1.6 collective-permute-start.4
  36.1 61.1 %forward_chain.1 = (bf16[4,576,512]{2,1,0:T(8,128)(2,1)}, bf16[512,2048]{1,0:T(8,128)(2,1)}, bf16[4,512,64]{2,1,0:T(8,128)(2,1)}, bf16[4,512,512]{2,1,0:T(8,128)...) custom-call(s32[1]{0:T(128)} %bitcast.1.refs_0_, ...), custom_call_target="tpu_custom_call" | custom-call | flops 60000002048 | bytes 1048576 | tf_op jit(solution)/shard_map/forward_chain/pallas_call | solution.py:571
  97.2 2.8 constant_dynamic-slice_fusion.5
  100.5 1.6 collective-permute-start.7
  102.1 48.5 %backward_chain.1 = (bf16[4,512,64]{2,1,0:T(8,128)(2,1)}, bf16[1024,2048]{1,0:T(8,128)(2,1)}, bf16[4,1536,64]{2,1,0:T(8,128)(2,1)}, bf16[512,2048]{1,0:T(8,128)(...) custom-call(s32[1]{0:T(128)} %bitcast.1.refs_0_, ...), custom_call_target="tpu_custom_call" | custom-call | flops 44000002048 | bytes 1048576 | tf_op jit(solution)/shard_map/backward_chain/pallas_call | solution.py:655
  150.7 10.8 %early_weights.2 = (bf16[512,2048]{1,0:T(8,128)(2,1)}, bf16[512,1024]{1,0:T(8,128)(2,1)}) custom-call(s32[1]{0:T(128)S(6)} %sub.100.side_ref.refs_0_, bf16[512,2048]{1,0:T(8,128)(2,1)} %get-tuple-element.152.refs_16_.a2_ref, bf16[2048,2048]{1,0:T(8,128)(2,1)} %get-tuple-element.172.gu_ref, bf16[512,2048]{1,0:T(8,128)(2,1)} %get-tuple-element.173.bf_ref, ...), custom_call_target="tpu_custom_call" | custom-call | flops 8999999488 | bytes 1048576 | tf_op jit(solution)/shard_map/early_weights/pallas_call | solution.py:863
  162.7 10.3 %early_weights.3 = (bf16[512,2048]{1,0:T(8,128)(2,1)}, bf16[512,1024]{1,0:T(8,128)(2,1)}) custom-call(s32[1]{0:T(128)} %bitcast.side_ref.refs_0_, bf16[512,2048]{1,0:T(8,128)(2,1)} %get-tuple-element.152.refs_16_.a2_ref, bf16[2048,2048]{1,0:T(8,128)(2,1)} %get-tuple-element.172.gu_ref, bf16[512,2048]{1,0:T(8,128)(2,1)} %get-tuple-element.173.bf_ref, ...), custom_call_target="tpu_custom_call" | custom-call | flops 8999999488 | bytes 1048576 | tf_op jit(solution)/shard_map/early_weights/pallas_call | solution.py:863
  173.0 2.2 dynamic-slice_add_fusion.3
  175.2 2.6 dynamic-slice_add_fusion
  177.8 1.6 collective-permute-start.12
  179.4 1.5 collective-permute-start.11
  180.9 11.4 %attention_back.3 = (bf16[1536,2048]{1,0:T(8,128)(2,1)}, bf16[1,512,512]{2,1,0:T(8,128)(2,1)}, f32[512,128]{1,0:T(8,128)}) custom-call(s32[1]{0:T(128)S(6)} %xor.15.place_ref, bf16[4,512,512]{2,1,0:T(8,128)(2,1)} %get-tuple-element.187.do_ref, f32[4,8,512]{2,1,0:T(8,128)} %get-tuple-element.188.dd_ref, bf16[4,512,512]{2,1,0:T(8,128)(2,1)} %get-tuple-element.189.dsm_ref, ...), custom_call_target="tpu_custom_call" | custom-call | flops 10000000000 | bytes 1048576 | tf_op jit(solution)/shard_map/attention_back/pallas_call | solution.py:706
  192.4 1.6 add_add_fusion.2
  194.8 1.8 add_add_fusion
  196.7 2.7 collective-permute-start.14
  199.4 1.5 collective-permute-start.13
  201.4 19.4 %attention_back.4 = (bf16[1536,2048]{1,0:T(8,128)(2,1)}, bf16[2,512,512]{2,1,0:T(8,128)(2,1)}, f32[512,128]{1,0:T(8,128)}) custom-call(s32[2]{0:T(128)} %pad_add_fusion.place_ref, bf16[4,512,512]{2,1,0:T(8,128)(2,1)} %get-tuple-element.187.do_ref, f32[4,8,512]{2,1,0:T(8,128)} %get-tuple-element.188.dd_ref, ...), custom_call_target="tpu_custom_call", output_to_operand_aliasing={{0}: (14, {})} | custom-call | flops 20000000000 | bytes 1048576 | tf_op jit(solution)/shard_map/attention_back/pallas_call | solution.py:706
  221.1 1.4 collective-permute-start.17
  222.5 1.6 collective-permute-start.15
  224.3 11.2 %attention_back.5 = (bf16[1536,2048]{1,0:T(8,128)(2,1)}, bf16[1,512,512]{2,1,0:T(8,128)(2,1)}, f32[512,128]{1,0:T(8,128)}) custom-call(s32[1]{0:T(128)S(6)} %xor.17.place_ref, bf16[4,512,512]{2,1,0:T(8,128)(2,1)} %get-tuple-element.187.do_ref, f32[4,8,512]{2,1,0:T(8,128)} %get-tuple-element.188.dd_ref, ...), custom_call_target="tpu_custom_call", output_to_operand_aliasing={{0}: (14, {})} | custom-call | flops 10000000000 | bytes 1048576 | tf_op jit(solution)/shard_map/attention_back/pallas_call | solution.py:706
  235.7 1.6 collective-permute-start.20
  237.6 0.9 collective-permute-done.19
  239.3 6.4 %late_weights.2 = bf16[512,1152]{1,0:T(8,128)(2,1)} custom-call(s32[1]{0:T(128)S(6)} %sub.100.side_ref.refs_0_, bf16[512,2048]{1,0:T(8,128)(2,1)} %get-tuple-element.195.a1_ref.refs_1_, bf16[1536,2048]{1,0:T(8,128)(2,1)} %get-tuple-element.221.refs_2_, bf16[512,2048]{1,0:T(8,128)(2,1)} %get-tuple-element.159.refs_15_.refs_3_, ...), custom_call_target="tpu_custom_call" | custom-call | flops 4000000000 | bytes 1048576 | tf_op jit(solution)/shard_map/late_weights/pallas_call | solution.py:954
  247.6 1.2 constant_dynamic-slice_fusion.4
  248.8 1.0 collective-permute-start.31
  249.8 1.5 collective-permute-start.30
  251.3 6.5 %late_weights.3 = bf16[512,1152]{1,0:T(8,128)(2,1)} custom-call(s32[1]{0:T(128)} %bitcast.side_ref.refs_0_, bf16[512,2048]{1,0:T(8,128)(2,1)} %get-tuple-element.195.a1_ref.refs_1_, bf16[1536,2048]{1,0:T(8,128)(2,1)} %get-tuple-element.221.refs_2_, bf16[512,2048]{1,0:T(8,128)(2,1)} %get-tuple-element.159.refs_15_.refs_3_, ...), custom_call_target="tpu_custom_call" | custom-call | flops 4000000000 | bytes 1048576 | tf_op jit(solution)/shard_map/late_weights/pallas_call | solution.py:954
  257.9 1.4 dynamic-slice_add_fusion.1
  259.3 1.0 collective-permute-start.23
  260.3 0.9 pad_maximum_fusion.14
  261.2 1.6 collective-permute-start.33
  263.1 1.1 constant_dynamic-update-slice_fusion.1
  264.4 2.4 maximum_convert_fusion
  266.8 2.5 collective-permute-done.23
  269.3 1.3 add_add_fusion.1
  271.5 3.6 %collective-permute-done.33 = bf16[128,1024]{1,0:T(8,128)(2,1)S(1)} collective-permute-done((bf16[128,1024]{1,0:T(8,128)(2,1)S(1)}, bf16[128,1024]{1,0:T(8,128)(2,1)S(1)}, u32[]{:S(2)}, u32[]{:S(2)}) %collective-permute-start.33) | collective-permute-done | bytes 262176 | tf_op jit(solution)/shard_map/ppermute | solution.py:760
  275.6 1.7 collective-permute-done.24
  278.8 1.6 collective-permute-start.35
  281.0 3.4 %collective-permute-done.25 = bf16[64,1152]{1,0:T(8,128)(2,1)S(1)} collective-permute-done((bf16[64,1152]{1,0:T(8,128)(2,1)S(1)}, bf16[64,1152]{1,0:T(8,128)(2,1)S(1)}, u32[]{:S(2)}, u32[]{:S(2)}) %collective-permute-start.25) | collective-permute-done | bytes 147488 | tf_op jit(solution)/shard_map/ppermute | solution.py:760
  284.4 8.3 %collective-permute-done.35.refs_2_ = bf16[256,1024]{1,0:T(8,128)(2,1)} collective-permute-done((bf16[256,1024]{1,0:T(8,128)(2,1)}, bf16[256,1024]{1,0:T(8,128)(2,1)}, u32[]{:S(2)}, u32[]{:S(2)}) %collective-permute-start.35) | collective-permute-done | bytes 524320 | tf_op jit(solution)/shard_map/ppermute | solution.py:760
  292.7 1.1 pad_maximum_fusion.2.refs_1_
  293.7 1.4 collective-permute-start.36
  295.9 6.8 %collective-permute-done.26 = bf16[64,1152]{1,0:T(8,128)(2,1)S(1)} collective-permute-done((bf16[64,1152]{1,0:T(8,128)(2,1)S(1)}, bf16[64,1152]{1,0:T(8,128)(2,1)S(1)}, u32[]{:S(2)}, u32[]{:S(2)}) %collective-permute-start.26) | collective-permute-done | bytes 147488 | tf_op jit(solution)/shard_map/ppermute | solution.py:760
  303.5 4.5 %collective-permute-done.27 = bf16[64,1152]{1,0:T(8,128)(2,1)S(1)} collective-permute-done((bf16[64,1152]{1,0:T(8,128)(2,1)S(1)}, bf16[64,1152]{1,0:T(8,128)(2,1)S(1)}, u32[]{:S(2)}, u32[]{:S(2)}) %collective-permute-start.27) | collective-permute-done | bytes 147488 | tf_op jit(solution)/shard_map/ppermute | solution.py:760
  307.9 0.9 collective-permute-done.36.refs_2_
  311.7 4.4 %collective-permute-done.28 = bf16[128,1152]{1,0:T(8,128)(2,1)S(1)} collective-permute-done((bf16[128,1152]{1,0:T(8,128)(2,1)S(1)}, bf16[128,1152]{1,0:T(8,128)(2,1)S(1)}, u32[]{:S(2)}, u32[]{:S(2)}) %collective-permute-start.28) | collective-permute-done | bytes 294944 | tf_op jit(solution)/shard_map/ppermute | solution.py:760
  316.1 1.5 collective-permute-start.29
  317.6 3.6 %unpack.4 = (f32[512,1536]{1,0:T(8,128)}, f32[512,512]{1,0:T(8,128)}) custom-call(s32[3]{0:T(128)} %pad_add_fusion.3.refs_0_, bf16[256,1024]{1,0:T(8,128)(2,1)} %pad_maximum_fusion.11.refs_1_, bf16[256,1024]{1,0:T(8,128)(2,1)} %collective-permute-done.35.refs_2_, bf16[256,1024]{1,0:T(8,128)(2,1)} %collective-permute-done.39.refs_3_, ...), custom_call_target="tpu_custom_call" | custom-call | flops 4000000000 | bytes 1048576 | tf_op jit(solution)/shard_map/unpack/pallas_call | solution.py:1114
  321.3 5.7 %unpack.3 = (f32[512,2048]{1,0:T(8,128)}, f32[2048,512]{1,0:T(8,128)}) custom-call(s32[3]{0:T(128)} %get-tuple-element.316.refs_0_, bf16[256,2048]{1,0:T(8,128)(2,1)} %pad_maximum_fusion.2.refs_1_, bf16[256,2048]{1,0:T(8,128)(2,1)} %collective-permute-done.36.refs_2_, bf16[256,2048]{1,0:T(8,128)(2,1)} %collective-permute-done.37.refs_3_, ...), custom_call_target="tpu_custom_call" | custom-call | flops 4000000000 | bytes 1048576 | tf_op jit(solution)/shard_map/unpack/pallas_call | solution.py:1114
  328.3 1.5 slice_bitcast_fusion
  329.8 0.9 copy-done.25
  331.5 4.5 %unpack.5 = (f32[512,1536]{1,0:T(8,128)}, f32[512,512]{1,0:T(8,128)}, f32[64,512]{1,0:T(8,128)}, f32[3,512]{1,0:T(4,128)}) custom-call(s32[3]{0:T(128)} %get-tuple-element.315.refs_0_, bf16[256,1152]{1,0:T(8,128)(2,1)} %copy-done.17, bf16[256,1152]{1,0:T(8,128)(2,1)} %collective-permute-done.29.refs_2_, bf16[256,1152]{1,0:T(8,128)(2,1)} %copy-done.25, ...), custom_call_target="tpu_custom_call" | custom-call | flops 4000000000 | bytes 1048576 | tf_op jit(solution)/shard_map/unpack/pallas_call | solution.py:1114
  336.0 1.4 fusion.4
  (157 shorter events, 21.1 us)
Async XLA Ops:
  3.6 5.1 %copy-start.22 = (bf16[512]{0:T(512)(128)(2,1)S(1)}, bf16[512]{0:T(512)(128)(2,1)}, u32[]{:S(2)}) copy-start(bf16[512]{0:T(512)(128)(2,1)} %param.20) | copy-start | bytes 3076
  3.6 5.0 %copy-start.23 = (bf16[512]{0:T(512)(128)(2,1)S(1)}, bf16[512]{0:T(512)(128)(2,1)}, u32[]{:S(2)}) copy-start(bf16[512]{0:T(512)(128)(2,1)} %param.23) | copy-start | bytes 3076
  3.7 5.0 %copy-start.24 = (bf16[512]{0:T(512)(128)(2,1)S(1)}, bf16[512]{0:T(512)(128)(2,1)}, u32[]{:S(2)}) copy-start(bf16[512]{0:T(512)(128)(2,1)} %param.26) | copy-start | bytes 3076
  3.7 5.1 %copy-start.7 = (bf16[512,2048]{1,0:T(8,128)(2,1)S(1)}, bf16[512,2048]{1,0:T(8,128)(2,1)}, u32[]{:S(2)}) copy-start(bf16[512,2048]{1,0:T(8,128)(2,1)} %refs_8_.1) | copy-start | bytes 6291460
  5.6 14.9 %collective-permute-start = (bf16[1,528,512]{2,1,0:T(8,128)(2,1)}, bf16[1,528,512]{2,1,0:T(8,128)(2,1)}, u32[]{:S(2)}, u32[]{:S(2)}) collective-permute-start(bf16[1,528,512]{2,1,0:T(8,128)(2,1)} %get-tuple-element.143), channel_id=1, source_target_pairs={{0,8},{8,0},{16,24},{24,16},{1,9},{9,1},{17,25},{25,17},{2,10},{10... | collective-permute-start | bytes 1622024 | tf_op jit(solution)/shard_map/ppermute | solution.py:735
  6.0 16.0 %collective-permute-start.1 = (bf16[1,528,512]{2,1,0:T(8,128)(2,1)}, bf16[1,528,512]{2,1,0:T(8,128)(2,1)}, u32[]{:S(2)}, u32[]{:S(2)}) collective-permute-start(bf16[1,528,512]{2,1,0:T(8,128)(2,1)} %get-tuple-element.144), channel_id=1, source_target_pairs={{0,16},{8,24},{16,0},{24,8},{1,17},{9,25},{17,1},{25,9},{2,18},{10... | collective-permute-start | bytes 1622024 | tf_op jit(solution)/shard_map/ppermute | solution.py:735
  8.5 24.7 %collective-permute-start.2 = (bf16[1,528,512]{2,1,0:T(8,128)(2,1)}, bf16[1,528,512]{2,1,0:T(8,128)(2,1)}, u32[]{:S(2)}, u32[]{:S(2)}) collective-permute-start(bf16[1,528,512]{2,1,0:T(8,128)(2,1)} %pad_maximum_fusion.9), channel_id=1, source_target_pairs={{0,24},{8,16},{16,8},{24,0},{1,25},{9,17},{17,9},{25,1},{2,26},{10... | collective-permute-start | bytes 1622024 | tf_op jit(solution)/shard_map/ppermute | solution.py:735
  11.2 2.7 copy-start
  15.5 17.7 %copy-start.8 = (bf16[4,1,512,512]{3,2,1,0:T(8,128)(2,1)S(1)}, bf16[4,1,512,512]{3,2,1,0:T(8,128)(2,1)}, u32[]{:S(2)}) copy-start(bf16[4,1,512,512]{3,2,1,0:T(8,128)(2,1)} %param.30) | copy-start | bytes 6291460
  17.7 15.6 %copy-start.21 = (bf16[4,1,64,512]{3,2,1,0:T(8,128)(2,1)S(1)}, bf16[4,1,64,512]{3,2,1,0:T(8,128)(2,1)}, u32[]{:S(2)}) copy-start(bf16[4,1,64,512]{3,2,1,0:T(8,128)(2,1)} %param.31) | copy-start | bytes 786436
  33.5 68.6 %collective-permute-start.3 = (bf16[1,576,512]{2,1,0:T(8,128)(2,1)S(1)}, bf16[1,576,512]{2,1,0:T(8,128)(2,1)}, u32[]{:S(2)}, u32[]{:S(2)}) collective-permute-start(bf16[1,576,512]{2,1,0:T(8,128)(2,1)S(1)} %pad_maximum_fusion.3), channel_id=1, source_target_pairs={{0,8},{8,0},{16,24},{24,16},{1,9},{9,1},{17,25},{25,17},{2,10},{10... | collective-permute-start | bytes 1769480 | tf_op jit(solution)/shard_map/ppermute | solution.py:735
  33.7 68.4 %collective-permute-start.4 = (bf16[1,576,512]{2,1,0:T(8,128)(2,1)S(1)}, bf16[1,576,512]{2,1,0:T(8,128)(2,1)}, u32[]{:S(2)}, u32[]{:S(2)}) collective-permute-start(bf16[1,576,512]{2,1,0:T(8,128)(2,1)S(1)} %pad_maximum_fusion.4), channel_id=1, source_target_pairs={{0,16},{8,24},{16,0},{24,8},{1,17},{9,25},{17,1},{25,9},{2,18},{10... | collective-permute-start | bytes 1769480 | tf_op jit(solution)/shard_map/ppermute | solution.py:735
  35.3 66.8 %collective-permute-start.5 = (bf16[1,576,512]{2,1,0:T(8,128)(2,1)S(1)}, bf16[1,576,512]{2,1,0:T(8,128)(2,1)}, u32[]{:S(2)}, u32[]{:S(2)}) collective-permute-start(bf16[1,576,512]{2,1,0:T(8,128)(2,1)S(1)} %pad_maximum_fusion.5), channel_id=1, source_target_pairs={{0,24},{8,16},{16,8},{24,0},{1,25},{9,17},{17,9},{25,1},{2,26},{10... | collective-permute-start | bytes 1769480 | tf_op jit(solution)/shard_map/ppermute | solution.py:735
  100.0 50.6 %collective-permute-start.6 = (bf16[1,576,512]{2,1,0:T(8,128)(2,1)}, bf16[1,576,512]{2,1,0:T(8,128)(2,1)S(1)}, u32[]{:S(2)}, u32[]{:S(2)}) collective-permute-start(bf16[1,576,512]{2,1,0:T(8,128)(2,1)} %get-tuple-element.293), channel_id=1, source_target_pairs={{0,8},{8,0},{16,24},{24,16},{1,9},{9,1},{17,25},{25,17},{2,10},{10... | collective-permute-start | bytes 1769480 | tf_op jit(solution)/shard_map/ppermute | solution.py:735
  100.5 50.2 %collective-permute-start.7 = (bf16[1,576,512]{2,1,0:T(8,128)(2,1)}, bf16[1,576,512]{2,1,0:T(8,128)(2,1)S(1)}, u32[]{:S(2)}, u32[]{:S(2)}) collective-permute-start(bf16[1,576,512]{2,1,0:T(8,128)(2,1)} %get-tuple-element.292), channel_id=1, source_target_pairs={{0,16},{8,24},{16,0},{24,8},{1,17},{9,25},{17,1},{25,9},{2,18},{10... | collective-permute-start | bytes 1769480 | tf_op jit(solution)/shard_map/ppermute | solution.py:735
  102.1 48.6 %collective-permute-start.8 = (bf16[1,576,512]{2,1,0:T(8,128)(2,1)}, bf16[1,576,512]{2,1,0:T(8,128)(2,1)S(1)}, u32[]{:S(2)}, u32[]{:S(2)}) collective-permute-start(bf16[1,576,512]{2,1,0:T(8,128)(2,1)} %get-tuple-element.291), channel_id=1, source_target_pairs={{0,24},{8,16},{16,8},{24,0},{1,25},{9,17},{17,9},{25,1},{2,26},{10... | collective-permute-start | bytes 1769480 | tf_op jit(solution)/shard_map/ppermute | solution.py:735
  150.7 10.9 %copy-start.11 = (bf16[1,576,512]{2,1,0:T(8,128)(2,1)}, bf16[1,576,512]{2,1,0:T(8,128)(2,1)S(1)}, u32[]{:S(2)}) copy-start(bf16[1,576,512]{2,1,0:T(8,128)(2,1)S(1)} %collective-permute-done.6) | copy-start | bytes 1769476
  150.7 10.9 %copy-start.13 = (bf16[1,576,512]{2,1,0:T(8,128)(2,1)}, bf16[1,576,512]{2,1,0:T(8,128)(2,1)S(1)}, u32[]{:S(2)}) copy-start(bf16[1,576,512]{2,1,0:T(8,128)(2,1)S(1)} %collective-permute-done.7) | copy-start | bytes 1769476
  150.7 10.9 %copy-start.15 = (bf16[1,576,512]{2,1,0:T(8,128)(2,1)}, bf16[1,576,512]{2,1,0:T(8,128)(2,1)S(1)}, u32[]{:S(2)}) copy-start(bf16[1,576,512]{2,1,0:T(8,128)(2,1)S(1)} %collective-permute-done.8) | copy-start | bytes 1769476
  161.6 13.6 %collective-permute-start.9 = (bf16[512,2048]{1,0:T(8,128)(2,1)}, bf16[512,2048]{1,0:T(8,128)(2,1)S(1)}, u32[]{:S(2)}, u32[]{:S(2)}) collective-permute-start(bf16[512,2048]{1,0:T(8,128)(2,1)} %get-tuple-element.179), channel_id=1, source_target_pairs={{0,8},{1,9},{2,10},{3,11},{4,12},{5,13},{6,14},{7,15},{8,0},{9,1},... | collective-permute-start | bytes 6291464 | tf_op jit(solution)/shard_map/ppermute | solution.py:760
  162.1 10.9 %collective-permute-start.10 = (bf16[512,1024]{1,0:T(8,128)(2,1)}, bf16[512,1024]{1,0:T(8,128)(2,1)}, u32[]{:S(2)}, u32[]{:S(2)}) collective-permute-start(bf16[512,1024]{1,0:T(8,128)(2,1)} %get-tuple-element.180), channel_id=1, source_target_pairs={{0,8},{1,9},{2,10},{3,11},{4,12},{5,13},{6,14},{7,15},{8,0},{9,1},... | collective-permute-start | bytes 3145736 | tf_op jit(solution)/shard_map/ppermute | solution.py:760
  177.8 14.6 %collective-permute-start.12 = (bf16[256,1024]{1,0:T(8,128)(2,1)}, bf16[256,1024]{1,0:T(8,128)(2,1)}, u32[]{:S(2)}, u32[]{:S(2)}) collective-permute-start(bf16[256,1024]{1,0:T(8,128)(2,1)} %dynamic-slice_add_fusion.3), channel_id=1, source_target_pairs={{0,2},{1,3},{2,0},{3,1},{4,6},{5,7},{6,4},{7,5},{8,10},{9,11},{10,... | collective-permute-start | bytes 1572872 | tf_op jit(solution)/shard_map/ppermute | solution.py:760
  179.4 15.4 %collective-permute-start.11 = (bf16[256,2048]{1,0:T(8,128)(2,1)}, bf16[256,2048]{1,0:T(8,128)(2,1)}, u32[]{:S(2)}, u32[]{:S(2)}) collective-permute-start(bf16[256,2048]{1,0:T(8,128)(2,1)} %dynamic-slice_add_fusion), channel_id=1, source_target_pairs={{0,1},{1,0},{2,3},{3,2},{4,5},{5,4},{6,7},{7,6},{8,24},{9,25},{10,... | collective-permute-start | bytes 3145736 | tf_op jit(solution)/shard_map/ppermute | solution.py:760
  180.9 11.5 %copy-start.9 = (bf16[512,1024]{1,0:T(8,128)(2,1)S(1)}, bf16[512,1024]{1,0:T(8,128)(2,1)}, u32[]{:S(2)}) copy-start(bf16[512,1024]{1,0:T(8,128)(2,1)} %get-tuple-element.183) | copy-start | bytes 3145732
  196.7 24.2 %collective-permute-start.14 = (bf16[128,1024]{1,0:T(8,128)(2,1)S(1)}, bf16[128,1024]{1,0:T(8,128)(2,1)S(1)}, u32[]{:S(2)}, u32[]{:S(2)}) collective-permute-start(bf16[128,1024]{1,0:T(8,128)(2,1)S(1)} %constant_dynamic-slice_fusion.14), channel_id=1, source_target_pairs={{0,4},{1,5},{2,6},{3,7},{4,0},{5,1},{6,2},{7,3},{8,12},{9,13},{10,... | collective-permute-start | bytes 786440 | tf_op jit(solution)/shard_map/ppermute | solution.py:760
  199.4 21.6 %collective-permute-start.13 = (bf16[128,2048]{1,0:T(8,128)(2,1)S(1)}, bf16[128,2048]{1,0:T(8,128)(2,1)S(1)}, u32[]{:S(2)}, u32[]{:S(2)}) collective-permute-start(bf16[128,2048]{1,0:T(8,128)(2,1)S(1)} %constant_dynamic-slice_fusion.15), channel_id=1, source_target_pairs={{0,16},{1,17},{2,18},{3,19},{4,20},{5,21},{6,22},{7,23},{8,9},{9,8... | collective-permute-start | bytes 1572872 | tf_op jit(solution)/shard_map/ppermute | solution.py:760
  200.9 23.3 %collective-permute-start.16 = (bf16[1,512,512]{2,1,0:T(8,128)(2,1)}, bf16[1,512,512]{2,1,0:T(8,128)(2,1)}, u32[]{:S(2)}, u32[]{:S(2)}) collective-permute-start(bf16[1,512,512]{2,1,0:T(8,128)(2,1)} %get-tuple-element.210), channel_id=1, source_target_pairs={{0,16},{8,24},{16,0},{24,8},{1,17},{9,25},{17,1},{25,9},{2,18},{10... | collective-permute-start | bytes 1572872 | tf_op jit(solution)/shard_map/ppermute | solution.py:735
  201.4 19.4 %copy-start.6 = (bf16[256,1024]{1,0:T(8,128)(2,1)S(1)}, bf16[256,1024]{1,0:T(8,128)(2,1)}, u32[]{:S(2)}) copy-start(bf16[256,1024]{1,0:T(8,128)(2,1)} %copy-done.5) | copy-start | bytes 1572868
  220.8 3.3 copy-start.10
  221.1 14.4 %collective-permute-start.17 = (bf16[64,1024]{1,0:T(8,128)(2,1)S(1)}, bf16[64,1024]{1,0:T(8,128)(2,1)S(1)}, u32[]{:S(2)}, u32[]{:S(2)}) collective-permute-start(bf16[64,1024]{1,0:T(8,128)(2,1)S(1)} %constant_dynamic-slice_fusion.12), channel_id=1, source_target_pairs={{0,1},{1,0},{2,3},{3,2},{4,5},{5,4},{6,7},{7,6},{8,24},{9,25},{10,... | collective-permute-start | bytes 393224 | tf_op jit(solution)/shard_map/ppermute | solution.py:760
  222.5 13.0 %collective-permute-start.15 = (bf16[64,2048]{1,0:T(8,128)(2,1)S(1)}, bf16[64,2048]{1,0:T(8,128)(2,1)S(1)}, u32[]{:S(2)}, u32[]{:S(2)}) collective-permute-start(bf16[64,2048]{1,0:T(8,128)(2,1)S(1)} %constant_dynamic-slice_fusion.13), channel_id=1, source_target_pairs={{0,2},{1,3},{2,0},{3,1},{4,6},{5,7},{6,4},{7,5},{8,10},{9,11},{10,... | collective-permute-start | bytes 786440 | tf_op jit(solution)/shard_map/ppermute | solution.py:760
  224.2 14.2 %collective-permute-start.19 = (bf16[1,512,512]{2,1,0:T(8,128)(2,1)S(1)}, bf16[1,512,512]{2,1,0:T(8,128)(2,1)S(1)}, u32[]{:S(2)}, u32[]{:S(2)}) collective-permute-start(bf16[1,512,512]{2,1,0:T(8,128)(2,1)S(1)} %get-tuple-element.305), channel_id=1, source_target_pairs={{0,24},{8,16},{16,8},{24,0},{1,25},{9,17},{17,9},{25,1},{2,26},{10... | collective-permute-start | bytes 1572872 | tf_op jit(solution)/shard_map/ppermute | solution.py:735
  235.7 10.0 %collective-permute-start.20 = (bf16[64,1024]{1,0:T(8,128)(2,1)S(1)}, bf16[64,1024]{1,0:T(8,128)(2,1)S(1)}, u32[]{:S(2)}, u32[]{:S(2)}) collective-permute-start(bf16[64,1024]{1,0:T(8,128)(2,1)S(1)} %dynamic-slice_add_fusion.8), channel_id=1, source_target_pairs={{0,16},{1,17},{2,18},{3,19},{4,20},{5,21},{6,22},{7,23},{8,9},{9,8... | collective-permute-start | bytes 393224 | tf_op jit(solution)/shard_map/ppermute | solution.py:760
  237.2 9.5 %collective-permute-start.18 = (bf16[32,2048]{1,0:T(8,128)(2,1)S(1)}, bf16[32,2048]{1,0:T(8,128)(2,1)S(1)}, u32[]{:S(2)}, u32[]{:S(2)}) collective-permute-start(bf16[32,2048]{1,0:T(8,128)(2,1)S(1)} %constant_dynamic-slice_fusion.11), channel_id=1, source_target_pairs={{0,4},{1,5},{2,6},{3,7},{4,0},{5,1},{6,2},{7,3},{8,12},{9,13},{10,... | collective-permute-start | bytes 393224 | tf_op jit(solution)/shard_map/ppermute | solution.py:760
  239.3 8.1 %copy-start.12 = (bf16[1,576,512]{2,1,0:T(8,128)(2,1)S(1)}, bf16[1,576,512]{2,1,0:T(8,128)(2,1)}, u32[]{:S(2)}) copy-start(bf16[1,576,512]{2,1,0:T(8,128)(2,1)} %copy-done.11) | copy-start | bytes 1769476
  239.3 8.1 %copy-start.14 = (bf16[1,576,512]{2,1,0:T(8,128)(2,1)S(1)}, bf16[1,576,512]{2,1,0:T(8,128)(2,1)}, u32[]{:S(2)}) copy-start(bf16[1,576,512]{2,1,0:T(8,128)(2,1)} %copy-done.13) | copy-start | bytes 1769476
  239.3 8.1 %copy-start.16 = (bf16[1,576,512]{2,1,0:T(8,128)(2,1)S(1)}, bf16[1,576,512]{2,1,0:T(8,128)(2,1)}, u32[]{:S(2)}) copy-start(bf16[1,576,512]{2,1,0:T(8,128)(2,1)} %copy-done.15) | copy-start | bytes 1769476
  246.7 11.1 %collective-permute-start.22 = (bf16[512,1152]{1,0:T(8,128)(2,1)}, bf16[512,1152]{1,0:T(8,128)(2,1)}, u32[]{:S(2)}, u32[]{:S(2)}) collective-permute-start(bf16[512,1152]{1,0:T(8,128)(2,1)} %late_weights.2), channel_id=1, source_target_pairs={{0,8},{1,9},{2,10},{3,11},{4,12},{5,13},{6,14},{7,15},{8,0},{9,1},... | collective-permute-start | bytes 3538952 | tf_op jit(solution)/shard_map/ppermute | solution.py:760
  246.8 4.5 %collective-permute-start.21 = (bf16[1,512,512]{2,1,0:T(8,128)(2,1)}, bf16[1,512,512]{2,1,0:T(8,128)(2,1)S(1)}, u32[]{:S(2)}, u32[]{:S(2)}) collective-permute-start(bf16[1,512,512]{2,1,0:T(8,128)(2,1)} %get-tuple-element.231), channel_id=1, source_target_pairs={{0,8},{8,0},{16,24},{24,16},{1,9},{9,1},{17,25},{25,17},{2,10},{10... | collective-permute-start | bytes 1572872 | tf_op jit(solution)/shard_map/ppermute | solution.py:735
  248.8 11.5 %collective-permute-start.31 = (bf16[64,1024]{1,0:T(8,128)(2,1)}, bf16[64,1024]{1,0:T(8,128)(2,1)S(1)}, u32[]{:S(2)}, u32[]{:S(2)}) collective-permute-start(bf16[64,1024]{1,0:T(8,128)(2,1)} %add.339), channel_id=1, source_target_pairs={{0,1},{1,0},{2,3},{3,2},{4,5},{5,4},{6,7},{7,6},{8,24},{9,25},{10,... | collective-permute-start | bytes 393224 | tf_op jit(solution)/shard_map/ppermute | solution.py:760
  249.8 11.4 %collective-permute-start.30 = (bf16[32,2048]{1,0:T(8,128)(2,1)S(1)}, bf16[32,2048]{1,0:T(8,128)(2,1)S(1)}, u32[]{:S(2)}, u32[]{:S(2)}) collective-permute-start(bf16[32,2048]{1,0:T(8,128)(2,1)S(1)} %dynamic-slice_add_fusion.9), channel_id=1, source_target_pairs={{0,4},{1,5},{2,6},{3,7},{4,0},{5,1},{6,2},{7,3},{8,12},{9,13},{10,... | collective-permute-start | bytes 393224 | tf_op jit(solution)/shard_map/ppermute | solution.py:760
  259.3 4.9 %copy-start.19 = (bf16[1,512,512]{2,1,0:T(8,128)(2,1)S(1)}, bf16[1,512,512]{2,1,0:T(8,128)(2,1)}, u32[]{:S(2)}) copy-start(bf16[1,512,512]{2,1,0:T(8,128)(2,1)} %copy-done.18) | copy-start | bytes 1572868
  259.3 9.9 %collective-permute-start.23 = (bf16[256,1152]{1,0:T(8,128)(2,1)S(1)}, bf16[256,1152]{1,0:T(8,128)(2,1)S(1)}, u32[]{:S(2)}, u32[]{:S(2)}) collective-permute-start(bf16[256,1152]{1,0:T(8,128)(2,1)S(1)} %dynamic-slice_add_fusion.1), channel_id=1, source_target_pairs={{0,1},{1,0},{2,3},{3,2},{4,5},{5,4},{6,7},{7,6},{8,24},{9,25},{10,... | collective-permute-start | bytes 1769480 | tf_op jit(solution)/shard_map/ppermute | solution.py:760
  261.2 13.9 %collective-permute-start.33 = (bf16[128,1024]{1,0:T(8,128)(2,1)S(1)}, bf16[128,1024]{1,0:T(8,128)(2,1)S(1)}, u32[]{:S(2)}, u32[]{:S(2)}) collective-permute-start(bf16[128,1024]{1,0:T(8,128)(2,1)S(1)} %pad_maximum_fusion.14), channel_id=1, source_target_pairs={{0,4},{1,5},{2,6},{3,7},{4,0},{5,1},{6,2},{7,3},{8,12},{9,13},{10,... | collective-permute-start | bytes 786440 | tf_op jit(solution)/shard_map/ppermute | solution.py:760
  262.9 12.5 %collective-permute-start.32 = (bf16[64,2048]{1,0:T(8,128)(2,1)S(1)}, bf16[64,2048]{1,0:T(8,128)(2,1)S(1)}, u32[]{:S(2)}, u32[]{:S(2)}) collective-permute-start(bf16[64,2048]{1,0:T(8,128)(2,1)S(1)} %pad_maximum_fusion.13), channel_id=1, source_target_pairs={{0,2},{1,3},{2,0},{3,1},{4,6},{5,7},{6,4},{7,5},{8,10},{9,11},{10,... | collective-permute-start | bytes 786440 | tf_op jit(solution)/shard_map/ppermute | solution.py:760
  264.4 4.9 %copy-start.1 = (bf16[512,1152]{1,0:T(8,128)(2,1)S(1)}, bf16[512,1152]{1,0:T(8,128)(2,1)}, u32[]{:S(2)}) copy-start(bf16[512,1152]{1,0:T(8,128)(2,1)} %late_weights.3) | copy-start | bytes 3538948
  266.8 4.5 %copy-start.2 = (bf16[1,576,512]{2,1,0:T(8,128)(2,1)S(1)}, bf16[1,576,512]{2,1,0:T(8,128)(2,1)}, u32[]{:S(2)}) copy-start(bf16[1,576,512]{2,1,0:T(8,128)(2,1)} %get-tuple-element.288) | copy-start | bytes 1769476
  266.8 4.5 %copy-start.3 = (bf16[1,576,512]{2,1,0:T(8,128)(2,1)S(1)}, bf16[1,576,512]{2,1,0:T(8,128)(2,1)}, u32[]{:S(2)}) copy-start(bf16[1,576,512]{2,1,0:T(8,128)(2,1)} %get-tuple-element.289) | copy-start | bytes 1769476
  270.6 6.8 %collective-permute-start.24 = (bf16[128,1152]{1,0:T(8,128)(2,1)S(1)}, bf16[128,1152]{1,0:T(8,128)(2,1)S(1)}, u32[]{:S(2)}, u32[]{:S(2)}) collective-permute-start(bf16[128,1152]{1,0:T(8,128)(2,1)S(1)} %constant_dynamic-slice_fusion.6), channel_id=1, source_target_pairs={{0,16},{1,17},{2,18},{3,19},{4,20},{5,21},{6,22},{7,23},{8,9},{9,8... | collective-permute-start | bytes 884744 | tf_op jit(solution)/shard_map/ppermute | solution.py:760
  277.5 6.8 %collective-permute-start.25 = (bf16[64,1152]{1,0:T(8,128)(2,1)S(1)}, bf16[64,1152]{1,0:T(8,128)(2,1)S(1)}, u32[]{:S(2)}, u32[]{:S(2)}) collective-permute-start(bf16[64,1152]{1,0:T(8,128)(2,1)S(1)} %constant_dynamic-slice_fusion), channel_id=1, source_target_pairs={{0,2},{1,3},{2,0},{3,1},{4,6},{5,7},{6,4},{7,5},{8,10},{9,11},{10,... | collective-permute-start | bytes 442376 | tf_op jit(solution)/shard_map/ppermute | solution.py:760
  278.8 13.8 %collective-permute-start.35 = (bf16[256,1024]{1,0:T(8,128)(2,1)}, bf16[256,1024]{1,0:T(8,128)(2,1)}, u32[]{:S(2)}, u32[]{:S(2)}) collective-permute-start(bf16[256,1024]{1,0:T(8,128)(2,1)} %pad_maximum_fusion.11.refs_1_), channel_id=1, source_target_pairs={{0,2},{1,3},{2,0},{3,1},{4,6},{5,7},{6,4},{7,5},{8,10},{9,11},{10,... | collective-permute-start | bytes 1572872 | tf_op jit(solution)/shard_map/ppermute | solution.py:760
  280.4 12.3 %collective-permute-start.34 = (bf16[128,2048]{1,0:T(8,128)(2,1)S(1)}, bf16[128,2048]{1,0:T(8,128)(2,1)S(1)}, u32[]{:S(2)}, u32[]{:S(2)}) collective-permute-start(bf16[128,2048]{1,0:T(8,128)(2,1)S(1)} %pad_maximum_fusion.10), channel_id=1, source_target_pairs={{0,16},{1,17},{2,18},{3,19},{4,20},{5,21},{6,22},{7,23},{8,9},{9,8... | collective-permute-start | bytes 1572872 | tf_op jit(solution)/shard_map/ppermute | solution.py:760
  293.7 15.1 %collective-permute-start.36 = (bf16[256,2048]{1,0:T(8,128)(2,1)}, bf16[256,2048]{1,0:T(8,128)(2,1)}, u32[]{:S(2)}, u32[]{:S(2)}) collective-permute-start(bf16[256,2048]{1,0:T(8,128)(2,1)} %pad_maximum_fusion.2.refs_1_), channel_id=1, source_target_pairs={{0,1},{1,0},{2,3},{3,2},{4,5},{5,4},{6,7},{7,6},{8,24},{9,25},{10,... | collective-permute-start | bytes 3145736 | tf_op jit(solution)/shard_map/ppermute | solution.py:760
  295.1 7.6 %collective-permute-start.26 = (bf16[64,1152]{1,0:T(8,128)(2,1)S(1)}, bf16[64,1152]{1,0:T(8,128)(2,1)S(1)}, u32[]{:S(2)}, u32[]{:S(2)}) collective-permute-start(bf16[64,1152]{1,0:T(8,128)(2,1)S(1)} %dynamic-slice_add_fusion.7), channel_id=1, source_target_pairs={{0,4},{1,5},{2,6},{3,7},{4,0},{5,1},{6,2},{7,3},{8,12},{9,13},{10,... | collective-permute-start | bytes 442376 | tf_op jit(solution)/shard_map/ppermute | solution.py:760
  302.7 5.2 %collective-permute-start.27 = (bf16[64,1152]{1,0:T(8,128)(2,1)S(1)}, bf16[64,1152]{1,0:T(8,128)(2,1)S(1)}, u32[]{:S(2)}, u32[]{:S(2)}) collective-permute-start(bf16[64,1152]{1,0:T(8,128)(2,1)S(1)} %add.350), channel_id=1, source_target_pairs={{0,2},{1,3},{2,0},{3,1},{4,6},{5,7},{6,4},{7,5},{8,10},{9,11},{10,... | collective-permute-start | bytes 442376 | tf_op jit(solution)/shard_map/ppermute | solution.py:760
  308.8 12.4 %collective-permute-start.37 = (bf16[256,2048]{1,0:T(8,128)(2,1)}, bf16[256,2048]{1,0:T(8,128)(2,1)}, u32[]{:S(2)}, u32[]{:S(2)}) collective-permute-start(bf16[256,2048]{1,0:T(8,128)(2,1)} %pad_maximum_fusion.2.refs_1_), channel_id=1, source_target_pairs={{0,8},{1,9},{2,10},{3,11},{4,12},{5,13},{6,14},{7,15},{8,0},{9,1},... | collective-permute-start | bytes 3145736 | tf_op jit(solution)/shard_map/ppermute | solution.py:760
  308.8 12.4 %collective-permute-start.38 = (bf16[256,2048]{1,0:T(8,128)(2,1)}, bf16[256,2048]{1,0:T(8,128)(2,1)}, u32[]{:S(2)}, u32[]{:S(2)}) collective-permute-start(bf16[256,2048]{1,0:T(8,128)(2,1)} %collective-permute-done.36.refs_2_), channel_id=1, source_target_pairs={{0,8},{1,9},{2,10},{3,11},{4,12},{5,13},{6,14},{7,15},{8,0},{9,1},... | collective-permute-start | bytes 3145736 | tf_op jit(solution)/shard_map/ppermute | solution.py:760
  309.3 6.7 %collective-permute-start.28 = (bf16[128,1152]{1,0:T(8,128)(2,1)S(1)}, bf16[128,1152]{1,0:T(8,128)(2,1)S(1)}, u32[]{:S(2)}, u32[]{:S(2)}) collective-permute-start(bf16[128,1152]{1,0:T(8,128)(2,1)S(1)} %pad_maximum_fusion.12), channel_id=1, source_target_pairs={{0,16},{1,17},{2,18},{3,19},{4,20},{5,21},{6,22},{7,23},{8,9},{9,8... | collective-permute-start | bytes 884744 | tf_op jit(solution)/shard_map/ppermute | solution.py:760
  309.9 7.7 %collective-permute-start.39 = (bf16[256,1024]{1,0:T(8,128)(2,1)}, bf16[256,1024]{1,0:T(8,128)(2,1)}, u32[]{:S(2)}, u32[]{:S(2)}) collective-permute-start(bf16[256,1024]{1,0:T(8,128)(2,1)} %pad_maximum_fusion.11.refs_1_), channel_id=1, source_target_pairs={{0,8},{1,9},{2,10},{3,11},{4,12},{5,13},{6,14},{7,15},{8,0},{9,1},... | collective-permute-start | bytes 1572872 | tf_op jit(solution)/shard_map/ppermute | solution.py:760
  310.5 7.1 %collective-permute-start.40 = (bf16[256,1024]{1,0:T(8,128)(2,1)}, bf16[256,1024]{1,0:T(8,128)(2,1)}, u32[]{:S(2)}, u32[]{:S(2)}) collective-permute-start(bf16[256,1024]{1,0:T(8,128)(2,1)} %collective-permute-done.35.refs_2_), channel_id=1, source_target_pairs={{0,8},{1,9},{2,10},{3,11},{4,12},{5,13},{6,14},{7,15},{8,0},{9,1},... | collective-permute-start | bytes 1572872 | tf_op jit(solution)/shard_map/ppermute | solution.py:760
  316.1 10.9 %copy-start.17 = (bf16[256,1152]{1,0:T(8,128)(2,1)}, bf16[256,1152]{1,0:T(8,128)(2,1)S(1)}, u32[]{:S(2)}) copy-start(bf16[256,1152]{1,0:T(8,128)(2,1)S(1)} %pad_maximum_fusion.6.refs_1_) | copy-start | bytes 1769476
  316.1 10.9 %collective-permute-start.29 = (bf16[256,1152]{1,0:T(8,128)(2,1)S(1)}, bf16[256,1152]{1,0:T(8,128)(2,1)}, u32[]{:S(2)}, u32[]{:S(2)}) collective-permute-start(bf16[256,1152]{1,0:T(8,128)(2,1)S(1)} %pad_maximum_fusion.6.refs_1_), channel_id=1, source_target_pairs={{0,1},{1,0},{2,3},{3,2},{4,5},{5,4},{6,7},{7,6},{8,24},{9,25},{10,... | collective-permute-start | bytes 1769480 | tf_op jit(solution)/shard_map/ppermute | solution.py:760
  327.0 2.8 collective-permute-start.41
  327.1 3.5 %collective-permute-start.42 = (bf16[256,1152]{1,0:T(8,128)(2,1)}, bf16[256,1152]{1,0:T(8,128)(2,1)S(1)}, u32[]{:S(2)}, u32[]{:S(2)}) collective-permute-start(bf16[256,1152]{1,0:T(8,128)(2,1)} %collective-permute-done.29.refs_2_), channel_id=1, source_target_pairs={{0,8},{1,9},{2,10},{3,11},{4,12},{5,13},{6,14},{7,15},{8,0},{9,1},... | collective-permute-start | bytes 1769480 | tf_op jit(solution)/shard_map/ppermute | solution.py:760
  (6 other events, 8.1 us)
where the time goes:
time: 341 us; the launch traced here: 338 us
  Pallas kernels  200 us (59%)
  waiting for transfers between devices  50.3 us (15%)
  starting transfers between devices  36.1 us (11%)
  local copies, waits for them, and re-layouts  25.9 us (8%)
  other arithmetic  24 us (7%)
    pallas_call x1, Pallas kernels, forward_chain(): pl.pallas_call(lambda *refs: forward_kernel(sources, segs, *refs), grid_s...  61.1 us
    pallas_call x1, Pallas kernels, backward_chain(): pl.pallas_call(lambda *refs: chain_kernel(sources, segs, *refs), grid_spe...  48.5 us
    pallas_call x3, Pallas kernels, attention_back(): pl.pallas_call(attention_kernel, grid_spec=pltpu.PrefetchScalarGridSpec(n...  42.1 us
    ppermute x31, waiting for transfers between devices, phase_swap(): return lax.ppermute(value, ('section', 'dp'), route)  36.6 us
    ppermute x31, starting transfers between devices, phase_swap(): return lax.ppermute(value, ('section', 'dp'), route)  27.9 us
    pallas_call x2, Pallas kernels, early_weights(): pl.pallas_call(early_weights_kernel, grid_spec=pltpu.PrefetchScalarGridSp...  21.1 us
    unnamed x64, local copies, waits for them, and re-layouts  17.7 us
    pallas_call x3, Pallas kernels, unpacked(): pl.pallas_call(lambda *refs: unpack_kernel(count, parts, regions, kept, *...  13.9 us
  transfers between devices with their start and end apart: 43, of which 14 were waited for; matrix products, arithmetic and copies ran while one was open for 10% of the time, Pallas kernels for 55%

commit v1 on v0

--- a/solution.py
+++ b/solution.py
@@ -8,7 +8,6 @@
 
 HEADS = 8
 HEAD_DIM = 64
-HEADS_A_STEP = 8
 EPS = 1e-06
 MASKED = -1000000000.0
 F32 = jnp.float32
@@ -52,6 +51,17 @@
     row_head = lax.broadcasted_iota(jnp.int32, (rows, columns), 0) // HEAD_DIM
     column_head = lax.broadcasted_iota(jnp.int32, (rows, columns), 1) // HEAD_DIM
     return row_head == column_head
+
+
+def spread_slots(values):
+    pair = jnp.concatenate([values, values], axis=1)
+    return jnp.concatenate([pair] * (HEADS // 2), axis=1)
+
+
+def fold_slots(values):
+    total = lane_sums(values)
+    half = total.shape[1] // 2
+    return total[:, :half] + total[:, half:]
 
 
 def norm_back(grad_normed, normed, scale, gain, gain_inverse):
@@ -287,7 +297,7 @@
     ew_ref[0] = raised
     ewm_ref[0] = mem_raised
     mixed = (nn(vwt, raised) + nn(vwtm, mem_raised)) * inverse
-    watt = nn(jnp.where(own, mixed, 0.0).astype(BF16), fold_ref[...]).astype(BF16)
+    watt = fold_slots(jnp.where(own, mixed, 0.0)).astype(BF16)
     watt_ref[0] = watt
     new_mem = (mem + nn(wwo_ref[...], watt)).astype(BF16).astype(F32)
     carry[...] = new_mem
@@ -301,8 +311,6 @@
     place_ref,
     carry0_ref,
     weights_gains_ref,
-    spread_ref,
-    fold_ref,
     wwo_ref,
     ww_ref,
     wout_ref,
@@ -357,7 +365,7 @@
     bm_ref[0] = branch_mem
     grad_watt = nn(wwo_ref[...], branch_mem).astype(BF16)
     inverse = stat_ref[0, 3:4, :]
-    scaled = (jnp.where(own, nn(grad_watt, spread_ref[...]), 0.0) * inverse).astype(BF16)
+    scaled = (jnp.where(own, spread_slots(grad_watt.astype(F32)), 0.0) * inverse).astype(BF16)
     raised = ew_ref[0].astype(F32)
     mem_raised = ewm_ref[0].astype(F32)
     grad_probs = nn(vw_ref[0], scaled)
@@ -371,7 +379,7 @@
     gwkv_ref[:width, :] = nt(qw_ref[0], grad_scores).astype(BF16)
     gwkv_ref[width:, :] = nt(scaled, ew_ref[0]).astype(BF16)
     grad_q = (nn(kwt_ref[0], grad_scores) + nn(kwtm_ref[0], mem_grad_scores)) * HEAD_DIM**-0.5
-    gwm_ref[0, :width, :] = nn(jnp.where(own, grad_q, 0.0).astype(BF16), fold_ref[...]).astype(BF16)
+    gwm_ref[0, :width, :] = fold_slots(jnp.where(own, grad_q, 0.0)).astype(BF16)
     gwm_ref[0, width : 2 * width, :] = nt(qw_ref[0], mem_grad_scores).astype(BF16)
     gwm_ref[0, 2 * width :, :] = nt(scaled, ewm_ref[0]).astype(BF16)
 
@@ -424,10 +432,10 @@
         )
     grad_scores = jnp.concatenate(parts, axis=0)
     dsm_ref[0] = grad_scores
-    grad_k = jnp.where(own, nt(q_ref[0], grad_scores), 0.0).astype(BF16)
-    grad_v = jnp.where(own, nt(scaled, em_ref[0]), 0.0).astype(BF16)
-    gkvm_ref[0, :width, :] = nn(grad_k, fold_ref[...]).astype(BF16)
-    gkvm_ref[0, width:, :] = nn(grad_v, fold_ref[...]).astype(BF16)
+    grad_k = jnp.where(own, nt(q_ref[0], grad_scores), 0.0)
+    grad_v = jnp.where(own, nt(scaled, em_ref[0]), 0.0)
+    gkvm_ref[0, :width, :] = fold_slots(grad_k).astype(BF16)
+    gkvm_ref[0, width:, :] = fold_slots(grad_v).astype(BF16)
     grad_a1m = nn(wqkv_ref[:, width:], gkvm_ref[0])
     mem_part, mem_weighed = norm_back(
         grad_a1m, a1m_ref[0].astype(F32), rm, ga[:, :slots], gai[:, :slots]
@@ -440,59 +448,67 @@
 
 
 def attention_kernel(
+    alone,
     place_ref,
     do_ref,
     dd_ref,
     dsm_ref,
-    gh_ref,
     q_ref,
     kt_ref,
     ktm_ref,
     v_ref,
     e_ref,
-    a1_ref,
     stat_ref,
     gains_ref,
+    gh_ref,
+    a1_ref,
     wqkv_ref,
     *refs,
 ):
-    gqkv_ref, out_ref, gain_ref = refs[-3:]
-    pair = pl.program_id(1)
+    step = pl.program_id(0)
+    copies = []
+    if alone:
+        gqkv_ref, out_ref, gain_ref, *buffers, sems = refs[-7:]
+        place = place_ref[0]
+        tokens = gh_ref.shape[2]
+        lanes = pl.ds(pl.multiple_of(place * tokens, tokens), tokens)
+        sources = [gh_ref.at[pl.ds(place, 1)], a1_ref.at[:, lanes], wqkv_ref]
+        for at, (source, target) in enumerate(zip(sources, buffers)):
+            copies.append(fetch(source, target, sems.at[at]))
+        gh_ref, a1_ref, wqkv_ref = buffers
+    else:
+        gqkv_ref, out_ref, gain_ref = refs[-3:]
     width = wqkv_ref.shape[0]
     seg = q_ref.shape[2]
-    for half in range(HEADS_A_STEP):
-        head = pair * HEADS_A_STEP + half
-        base = pl.multiple_of(head * HEAD_DIM, HEAD_DIM)
-        span = slice(half * HEAD_DIM, (half + 1) * HEAD_DIM)
+    for head in range(HEADS):
+        span = slice(head * HEAD_DIM, (head + 1) * HEAD_DIM)
+        key_span = slice(width + head * HEAD_DIM, width + (head + 1) * HEAD_DIM)
+        value_span = slice(2 * width + head * HEAD_DIM, 2 * width + (head + 1) * HEAD_DIM)
         grads = do_ref[0, span, :]
         blank = jnp.zeros_like(grads)
-        padded = jnp.concatenate([grads, blank] if half % 2 == 0 else [blank, grads], axis=0)
-        dots = dd_ref[0, pl.ds(head, 1), :]
-        lanes = slice(half // 2 * 128, half // 2 * 128 + 128)
+        padded = jnp.concatenate([grads, blank] if head % 2 == 0 else [blank, grads], axis=0)
+        dots = dd_ref[0, head : head + 1, :]
+        lanes = slice(head // 2 * 128, head // 2 * 128 + 128)
         grad_probs = nn(v_ref[0, :, lanes], padded)
-        inner = (e_ref[0, half].astype(F32) * (grad_probs - dots)).astype(BF16)
+        inner = (e_ref[0, head].astype(F32) * (grad_probs - dots)).astype(BF16)
         grad_q = nn(kt_ref[0, span, :], inner) + nn(ktm_ref[0, span, :], dsm_ref[0, span, :])
-        gqkv_ref[pl.ds(base, HEAD_DIM), :] = (grad_q * HEAD_DIM**-0.5).astype(BF16)
-        gqkv_ref[pl.ds(width + base, HEAD_DIM), :] = nt(q_ref[0, span, :], inner).astype(BF16)
-        gqkv_ref[pl.ds(2 * width + base, HEAD_DIM), :] = nt(grads, e_ref[0, half]).astype(BF16)
-
-    @pl.when((pl.program_id(0) == 0) & (pair == 0))
-    def _():
-        gain_ref[...] = jnp.zeros_like(gain_ref)
-
-    @pl.when(pair == pl.num_programs(1) - 1)
-    def _():
-        grad_a1 = nn(wqkv_ref[...], gqkv_ref[...])
-        (ga,) = gain_tiles(gains_ref, 1)
-        part, weighed = norm_back(
-            grad_a1,
-            a1_ref[...].astype(F32),
-            stat_ref[0, 0:1, :],
-            wide(ga, seg),
-            wide(1.0 / ga, seg),
-        )
-        gain_ref[...] += lane_sums(weighed)
-        out_ref[0] = (gh_ref[0] + part).T.astype(BF16)
+        gqkv_ref[span, :] = (grad_q * HEAD_DIM**-0.5).astype(BF16)
+        gqkv_ref[key_span, :] = nt(q_ref[0, span, :], inner).astype(BF16)
+        gqkv_ref[value_span, :] = nt(grads, e_ref[0, head]).astype(BF16)
+
+    for copy in copies:
+        copy.wait()
+    grad_a1 = nn(wqkv_ref[...], gqkv_ref[...])
+    (ga,) = gain_tiles(gains_ref, 1)
+    part, weighed = norm_back(
+        grad_a1,
+        a1_ref[...].astype(F32),
+        stat_ref[0, 0:1, :],
+        wide(ga, seg),
+        wide(1.0 / ga, seg),
+    )
+    gain_ref[...] = jnp.where(step == 0, 0.0, gain_ref[...]) + lane_sums(weighed)
+    out_ref[0] = (gh_ref[0] + part).T.astype(BF16)
 
 
 def whole(array):
@@ -639,8 +655,6 @@
     fixed = [
         carry0,
         consts["gains"],
-        consts["spread"],
-        consts["fold"],
     ]
     weights = [w[name] for name in ("wo", "write", "out", "in", "ao", "qkv")]
     blocked = ["a1m", "q", "vm", "em", "att", "a2", "gp", "a3", "a3m", "qw"]
@@ -678,43 +692,44 @@
 def attention_back(kept, grads, which, consts, w, before):
     segs, width, seg = kept["q"].shape
     count = which.shape[0]
-    pair = HEADS_A_STEP * HEAD_DIM
-
-    def by_pair(rows, lanes):
-        return pl.BlockSpec((1, rows, lanes), lambda s, h, f: (f[s], h, 0))
 
     def by_seg(array):
+        if array.ndim == 2:
+            return pl.BlockSpec((array.shape[0], seg), lambda s, f: (0, f[s]))
         tail = (0,) * (array.ndim - 1)
-        return pl.BlockSpec((1,) + array.shape[1:], lambda s, h, f: (f[s],) + tail)
-
-    inputs = [
-        (grads["do"], by_pair(pair, seg)),
-        (grads["dd"], by_seg(grads["dd"])),
-        (grads["dsm"], by_pair(pair, seg)),
-        (grads["gh"], by_seg(grads["gh"])),
-        (kept["q"], by_pair(pair, seg)),
-        (kept["kt"], by_pair(pair, seg)),
-        (kept["ktm"], by_pair(pair, kept["ktm"].shape[2])),
-        (kept["v"], pl.BlockSpec((1, seg, pair), lambda s, h, f: (f[s], 0, h))),
-        (kept["e"], pl.BlockSpec((1, HEADS_A_STEP, seg, seg), lambda s, h, f: (f[s], h, 0, 0))),
-        (kept["a1"], pl.BlockSpec((width, seg), lambda s, h, f: (0, f[s]))),
-        (kept["stat"], by_seg(kept["stat"])),
-        (consts["gains"], whole(consts["gains"])),
-        (w["qkv"], whole(w["qkv"])),
-    ]
+        return pl.BlockSpec((1,) + array.shape[1:], lambda s, f: (f[s],) + tail)
+
+    alone = count == 1
+    blocked = [grads[name] for name in ("do", "dd", "dsm")]
+    blocked += [kept[name] for name in ("q", "kt", "ktm", "v", "e", "stat")]
+    inputs = [(array, by_seg(array)) for array in blocked]
+    inputs.append((consts["gains"], whole(consts["gains"])))
+    last = [grads["gh"], kept["a1"], w["qkv"]]
+    scratch = []
+    if alone:
+        inputs += [(array, pl.BlockSpec(memory_space=pl.ANY)) for array in last]
+        scratch = [
+            pltpu.VMEM((1, width, seg), F32),
+            pltpu.VMEM((width, seg), BF16),
+            pltpu.VMEM(w["qkv"].shape, BF16),
+            pltpu.SemaphoreType.DMA((3,)),
+        ]
+    else:
+        inputs += [(array, by_seg(array)) for array in last[:2]] + [(last[2], whole(last[2]))]
     passed = [] if before is None else [before]
     return pl.pallas_call(
-        attention_kernel,
+        lambda *refs: attention_kernel(alone, *refs),
         grid_spec=pltpu.PrefetchScalarGridSpec(
             num_scalar_prefetch=1,
-            grid=(count, HEADS // HEADS_A_STEP),
+            grid=(count,),
             in_specs=[spec for _, spec in inputs]
             + [pl.BlockSpec(memory_space=pl.ANY)] * len(passed),
             out_specs=[
-                pl.BlockSpec((3 * width, seg), lambda s, h, f: (0, f[s])),
-                pl.BlockSpec((1, seg, width), lambda s, h, f: (s, 0, 0)),
-                pl.BlockSpec((width, 128), lambda s, h, f: (0, 0)),
+                pl.BlockSpec((3 * width, seg), lambda s, f: (0, f[s])),
+                pl.BlockSpec((1, seg, width), lambda s, f: (s, 0, 0)),
+                pl.BlockSpec((width, 128), lambda s, f: (0, 0)),
             ],
+            scratch_shapes=scratch,
         ),
         out_shape=[
             jax.ShapeDtypeStruct((3 * width, segs * seg), BF16),
@@ -722,9 +737,7 @@
             jax.ShapeDtypeStruct((width, 128), F32),
         ],
         input_output_aliases={1 + len(inputs): 0} if passed else {},
-        compiler_params=pltpu.CompilerParams(
-            dimension_semantics=("arbitrary", "arbitrary"), vmem_limit_bytes=VMEM_LIMIT
-        ),
+        compiler_params=params(),
         cost_estimate=cost(10 * count),
         name="attention_back",
     )(which, *[array for array, _ in inputs], *passed)
@@ -1119,7 +1132,7 @@
         scratch_shapes=[pltpu.VMEM(shape, F32) for shape in shapes]
         + [pltpu.SemaphoreType.DMA((len(regions[0]) + len(regions[1]),))],
         compiler_params=pltpu.CompilerParams(vmem_limit_bytes=VMEM_LIMIT),
-        cost_estimate=cost(4),
+        cost_estimate=cost(60 if kept else 0.1),
         name="unpack",
     )(places, *inputs)
 
@@ -1349,8 +1362,8 @@
     if late.steps:
         advance([late])
     advance(groups, late.sent)
+    grad_write, grad_wo = unpacked(write, write_regions, [triple, square])
     grad_in, grad_out = unpacked(ffn, ffn_regions, [(width, ff), (ff, width)])
-    grad_write, grad_wo = unpacked(write, write_regions, [triple, square])
     grad_in, grad_write = late.finish(grad_in, grad_write)
     while late.steps:
         advance([late])

time: 341 us -> 337 us (0.988)
  Pallas kernels: 200 us -> 194 us
  transfers between devices with their start and end apart: 43 -> 43, of which waited for: 14 -> 17; matrix products, arithmetic and copies ran while one was open for 10% -> 11% of each run, Pallas kernels for 55% -> 54%
where the time goes in v1:
time: 337 us; the launch traced here: 334 us
  Pallas kernels  194 us (58%)
  waiting for transfers between devices  53.6 us (16%)
  starting transfers between devices  35.2 us (10%)
  local copies, waits for them, and re-layouts  25.1 us (7%)
  other arithmetic  23.7 us (7%)
    pallas_call x1, Pallas kernels, forward_chain(): pl.pallas_call(lambda *refs: forward_kernel(sources, segs, *refs), grid_s...  60 us
    pallas_call x1, Pallas kernels, backward_chain(): pl.pallas_call(lambda *refs: chain_kernel(sources, segs, *refs), grid_spe...  46.1 us
    pallas_call x3, Pallas kernels, attention_back(): pl.pallas_call(lambda *refs: attention_kernel(alone, *refs), grid_spec=pl...  40.2 us
    ppermute x31, waiting for transfers between devices, phase_swap(): return lax.ppermute(value, ('section', 'dp'), route)  39.1 us
    ppermute x31, starting transfers between devices, phase_swap(): return lax.ppermute(value, ('section', 'dp'), route)  27.1 us
    pallas_call x2, Pallas kernels, early_weights(): pl.pallas_call(early_weights_kernel, grid_spec=pltpu.PrefetchScalarGridSp...  21.1 us
    unnamed x64, local copies, waits for them, and re-layouts  16.9 us
    ppermute x12, waiting for transfers between devices, swap_pairs(): return lax.ppermute(value, axis, [(i, i ^ mask) for i in range(size)])  14.5 us
  transfers between devices with their start and end apart: 43, of which 17 were waited for; matrix products, arithmetic and copies ran while one was open for 11% of the time, Pallas kernels for 54%

profile of v1, /device:TPU:0, one launch (start us, length us, event | category | flops | bytes accessed | tf_op | source)
XLA Modules:
  0.0 333.5 jit_solution(2523144647723879031)
XLA Ops:
  2.2 1.5 dynamic-slice_bitcast_fusion
  3.7 0.8 pad_maximum_fusion.9
  4.5 1.0 pad_maximum_fusion.7
  6.0 2.5 collective-permute-start.1
  8.7 2.5 copy.34
  11.2 2.7 copy.35
  14.0 1.6 copy.32
  15.5 2.2 copy.36
  17.7 2.1 copy.33
  20.4 1.6 collective-permute-done.1.refs_15_
  22.0 11.2 %collective-permute-done.2.refs_16_ = bf16[1,528,512]{2,1,0:T(8,128)(2,1)} collective-permute-done((bf16[1,528,512]{2,1,0:T(8,128)(2,1)}, bf16[1,528,512]{2,1,0:T(8,128)(2,1)}, u32[]{:S(2)}, u32[]{:S(2)}) %collective-permute-start.2) | collective-permute-done | bytes 540704 | tf_op jit(solution)/shard_map/ppermute | solution.py:748
  33.7 1.6 collective-permute-start.4
  36.1 60.0 %forward_chain.1 = (bf16[4,576,512]{2,1,0:T(8,128)(2,1)}, bf16[512,2048]{1,0:T(8,128)(2,1)}, bf16[4,512,64]{2,1,0:T(8,128)(2,1)}, bf16[4,512,512]{2,1,0:T(8,128)...) custom-call(s32[1]{0:T(128)} %bitcast.1.refs_0_, ...), custom_call_target="tpu_custom_call" | custom-call | flops 60000002048 | bytes 1048576 | tf_op jit(solution)/shard_map/forward_chain/pallas_call | solution.py:587
  96.1 2.8 constant_dynamic-slice_fusion.5
  99.4 1.6 collective-permute-start.7
  101.0 46.1 %backward_chain.1 = (bf16[4,512,64]{2,1,0:T(8,128)(2,1)}, bf16[1024,2048]{1,0:T(8,128)(2,1)}, bf16[4,1536,64]{2,1,0:T(8,128)(2,1)}, bf16[512,2048]{1,0:T(8,128)(...) custom-call(s32[1]{0:T(128)} %bitcast.1.refs_0_, ...), custom_call_target="tpu_custom_call" | custom-call | flops 44000002048 | bytes 1048576 | tf_op jit(solution)/shard_map/backward_chain/pallas_call | solution.py:669
  147.2 10.8 %early_weights.2 = (bf16[512,2048]{1,0:T(8,128)(2,1)}, bf16[512,1024]{1,0:T(8,128)(2,1)}) custom-call(s32[1]{0:T(128)S(6)} %sub.100.side_ref.refs_0_, bf16[512,2048]{1,0:T(8,128)(2,1)} %get-tuple-element.152.refs_14_.a2_ref, bf16[2048,2048]{1,0:T(8,128)(2,1)} %get-tuple-element.172.gu_ref, bf16[512,2048]{1,0:T(8,128)(2,1)} %get-tuple-element.173.bf_ref, ...), custom_call_target="tpu_custom_call" | custom-call | flops 8999999488 | bytes 1048576 | tf_op jit(solution)/shard_map/early_weights/pallas_call | solution.py:876
  159.2 10.3 %early_weights.3 = (bf16[512,2048]{1,0:T(8,128)(2,1)}, bf16[512,1024]{1,0:T(8,128)(2,1)}) custom-call(s32[1]{0:T(128)} %bitcast.side_ref.refs_0_, bf16[512,2048]{1,0:T(8,128)(2,1)} %get-tuple-element.152.refs_14_.a2_ref, bf16[2048,2048]{1,0:T(8,128)(2,1)} %get-tuple-element.172.gu_ref, bf16[512,2048]{1,0:T(8,128)(2,1)} %get-tuple-element.173.bf_ref, ...), custom_call_target="tpu_custom_call" | custom-call | flops 8999999488 | bytes 1048576 | tf_op jit(solution)/shard_map/early_weights/pallas_call | solution.py:876
  169.5 2.2 dynamic-slice_add_fusion.3
  171.7 2.6 dynamic-slice_add_fusion
  174.3 1.7 collective-permute-start.12
  175.9 1.5 collective-permute-start.11
  177.4 10.6 %attention_back.3 = (bf16[1536,2048]{1,0:T(8,128)(2,1)}, bf16[1,512,512]{2,1,0:T(8,128)(2,1)}, f32[512,128]{1,0:T(8,128)}) custom-call(s32[1]{0:T(128)S(6)} %xor.15.refs_0_, bf16[4,512,512]{2,1,0:T(8,128)(2,1)} %get-tuple-element.187.refs_1_, f32[4,8,512]{2,1,0:T(8,128)} %get-tuple-element.188.refs_2_, bf16[4,512,512]{2,1,0:T(8,128)(2,1)} %get-tuple-element.189.refs_3_, ...), custom_call_target="tpu_custom_call" | custom-call | flops 10000000000 | bytes 1048576 | tf_op jit(solution)/shard_map/attention_back/pallas_call | solution.py:720
  188.0 0.8 collective-permute-done.12
  188.8 1.5 add_add_fusion.2
  191.1 1.8 add_add_fusion
  192.9 2.7 collective-permute-start.14
  195.7 1.5 collective-permute-start.13
  197.7 19.2 %attention_back.4 = (bf16[1536,2048]{1,0:T(8,128)(2,1)}, bf16[2,512,512]{2,1,0:T(8,128)(2,1)}, f32[512,128]{1,0:T(8,128)}) custom-call(s32[2]{0:T(128)} %pad_add_fusion.refs_0_, bf16[4,512,512]{2,1,0:T(8,128)(2,1)} %get-tuple-element.187.refs_1_, f32[4,8,512]{2,1,0:T(8,128)} %get-tuple-element.188.refs_2_, ...), custom_call_target="tpu_custom_call", output_to_operand_aliasing={{0}: (14, {})} | custom-call | flops 20000000000 | bytes 1048576 | tf_op jit(solution)/shard_map/attention_back/pallas_call | solution.py:720
  217.2 1.5 collective-permute-start.17
  218.8 1.6 collective-permute-start.15
  220.5 10.4 %attention_back.5 = (bf16[1536,2048]{1,0:T(8,128)(2,1)}, bf16[1,512,512]{2,1,0:T(8,128)(2,1)}, f32[512,128]{1,0:T(8,128)}) custom-call(s32[1]{0:T(128)S(6)} %xor.17.refs_0_, bf16[4,512,512]{2,1,0:T(8,128)(2,1)} %get-tuple-element.187.refs_1_, f32[4,8,512]{2,1,0:T(8,128)} %get-tuple-element.188.refs_2_, ...), custom_call_target="tpu_custom_call", output_to_operand_aliasing={{0}: (14, {})} | custom-call | flops 10000000000 | bytes 1048576 | tf_op jit(solution)/shard_map/attention_back/pallas_call | solution.py:720
  231.1 1.6 collective-permute-start.20
  233.0 1.7 collective-permute-done.19
  235.5 6.4 %late_weights.2 = bf16[512,1152]{1,0:T(8,128)(2,1)} custom-call(s32[1]{0:T(128)S(6)} %sub.100.side_ref.refs_0_, bf16[512,2048]{1,0:T(8,128)(2,1)} %get-tuple-element.195.refs_12_.refs_1_, bf16[1536,2048]{1,0:T(8,128)(2,1)} %get-tuple-element.221.refs_2_, bf16[512,2048]{1,0:T(8,128)(2,1)} %get-tuple-element.159.refs_13_.refs_3_, ...), custom_call_target="tpu_custom_call" | custom-call | flops 4000000000 | bytes 1048576 | tf_op jit(solution)/shard_map/late_weights/pallas_call | solution.py:967
  243.6 1.2 constant_dynamic-slice_fusion.4
  245.3 1.5 collective-permute-start.30
  246.8 6.5 %late_weights.3 = bf16[512,1152]{1,0:T(8,128)(2,1)} custom-call(s32[1]{0:T(128)} %bitcast.side_ref.refs_0_, bf16[512,2048]{1,0:T(8,128)(2,1)} %get-tuple-element.195.refs_12_.refs_1_, bf16[1536,2048]{1,0:T(8,128)(2,1)} %get-tuple-element.221.refs_2_, bf16[512,2048]{1,0:T(8,128)(2,1)} %get-tuple-element.159.refs_13_.refs_3_, ...), custom_call_target="tpu_custom_call" | custom-call | flops 4000000000 | bytes 1048576 | tf_op jit(solution)/shard_map/late_weights/pallas_call | solution.py:967
  253.3 1.4 dynamic-slice_add_fusion.1
  254.7 1.0 collective-permute-start.23
  255.7 0.9 pad_maximum_fusion.14
  256.7 2.1 collective-permute-start.33
  259.3 1.1 constant_dynamic-update-slice_fusion.1
  260.6 2.4 maximum_convert_fusion
  263.0 1.7 collective-permute-done.23
  264.7 1.3 add_add_fusion.1
  266.9 3.5 %collective-permute-done.33 = bf16[128,1024]{1,0:T(8,128)(2,1)S(1)} collective-permute-done((bf16[128,1024]{1,0:T(8,128)(2,1)S(1)}, bf16[128,1024]{1,0:T(8,128)(2,1)S(1)}, u32[]{:S(2)}, u32[]{:S(2)}) %collective-permute-start.33) | collective-permute-done | bytes 262176 | tf_op jit(solution)/shard_map/ppermute | solution.py:773
  270.5 0.9 collective-permute-done.32
  271.6 1.2 collective-permute-done.24
  273.5 0.8 pad_maximum_fusion.11.refs_1_
  274.3 1.5 collective-permute-start.35
  276.4 3.4 %collective-permute-done.25 = bf16[64,1152]{1,0:T(8,128)(2,1)S(1)} collective-permute-done((bf16[64,1152]{1,0:T(8,128)(2,1)S(1)}, bf16[64,1152]{1,0:T(8,128)(2,1)S(1)}, u32[]{:S(2)}, u32[]{:S(2)}) %collective-permute-start.25) | collective-permute-done | bytes 147488 | tf_op jit(solution)/shard_map/ppermute | solution.py:773
  279.8 8.3 %collective-permute-done.35.refs_2_ = bf16[256,1024]{1,0:T(8,128)(2,1)} collective-permute-done((bf16[256,1024]{1,0:T(8,128)(2,1)}, bf16[256,1024]{1,0:T(8,128)(2,1)}, u32[]{:S(2)}, u32[]{:S(2)}) %collective-permute-start.35) | collective-permute-done | bytes 524320 | tf_op jit(solution)/shard_map/ppermute | solution.py:773
  288.2 1.5 collective-permute-start.36
  290.4 7.0 %collective-permute-done.26 = bf16[64,1152]{1,0:T(8,128)(2,1)S(1)} collective-permute-done((bf16[64,1152]{1,0:T(8,128)(2,1)S(1)}, bf16[64,1152]{1,0:T(8,128)(2,1)S(1)}, u32[]{:S(2)}, u32[]{:S(2)}) %collective-permute-start.26) | collective-permute-done | bytes 147488 | tf_op jit(solution)/shard_map/ppermute | solution.py:773
  297.5 5.1 %collective-permute-done.27 = bf16[64,1152]{1,0:T(8,128)(2,1)S(1)} collective-permute-done((bf16[64,1152]{1,0:T(8,128)(2,1)S(1)}, bf16[64,1152]{1,0:T(8,128)(2,1)S(1)}, u32[]{:S(2)}, u32[]{:S(2)}) %collective-permute-start.27) | collective-permute-done | bytes 147488 | tf_op jit(solution)/shard_map/ppermute | solution.py:773
  303.3 1.1 collective-permute-done.36.refs_2_
  304.9 4.5 %collective-permute-done.28 = bf16[128,1152]{1,0:T(8,128)(2,1)S(1)} collective-permute-done((bf16[128,1152]{1,0:T(8,128)(2,1)S(1)}, bf16[128,1152]{1,0:T(8,128)(2,1)S(1)}, u32[]{:S(2)}, u32[]{:S(2)}) %collective-permute-start.28) | collective-permute-done | bytes 294944 | tf_op jit(solution)/shard_map/ppermute | solution.py:773
  309.5 0.9 pad_maximum_fusion.6.refs_1_
  313.9 3.6 %unpack.4 = (f32[512,1536]{1,0:T(8,128)}, f32[512,512]{1,0:T(8,128)}) custom-call(s32[3]{0:T(128)} %pad_add_fusion.3.refs_0_, bf16[256,1024]{1,0:T(8,128)(2,1)} %pad_maximum_fusion.11.refs_1_, bf16[256,1024]{1,0:T(8,128)(2,1)} %collective-permute-done.35.refs_2_, bf16[256,1024]{1,0:T(8,128)(2,1)} %collective-permute-done.39.refs_3_, ...), custom_call_target="tpu_custom_call" | custom-call | flops 100000000 | bytes 1048576 | tf_op jit(solution)/shard_map/unpack/pallas_call | solution.py:1127
  317.6 5.7 %unpack.3 = (f32[512,2048]{1,0:T(8,128)}, f32[2048,512]{1,0:T(8,128)}) custom-call(s32[3]{0:T(128)} %get-tuple-element.316.refs_0_, bf16[256,2048]{1,0:T(8,128)(2,1)} %copy-done.2, bf16[256,2048]{1,0:T(8,128)(2,1)} %collective-permute-done.36.refs_2_, bf16[256,2048]{1,0:T(8,128)(2,1)} %collective-permute-done.37.refs_3_, ...), custom_call_target="tpu_custom_call" | custom-call | flops 100000000 | bytes 1048576 | tf_op jit(solution)/shard_map/unpack/pallas_call | solution.py:1127
  324.7 1.5 slice_bitcast_fusion
  327.3 4.5 %unpack.5 = (f32[512,1536]{1,0:T(8,128)}, f32[512,512]{1,0:T(8,128)}, f32[64,512]{1,0:T(8,128)}, f32[3,512]{1,0:T(4,128)}) custom-call(s32[3]{0:T(128)} %get-tuple-element.315.refs_0_, bf16[256,1152]{1,0:T(8,128)(2,1)} %pad_maximum_fusion.6.refs_1_, bf16[256,1152]{1,0:T(8,128)(2,1)} %collective-permute-done.29.refs_2_, bf16[256,1152]{1,0:T(8,128)(2,1)} %copy-done.25, ...), custom_call_target="tpu_custom_call" | custom-call | flops 60000002048 | bytes 1048576 | tf_op jit(solution)/shard_map/unpack/pallas_call | solution.py:1127
  331.8 1.4 fusion.4
  (157 shorter events, 22.2 us)
Async XLA Ops:
  3.6 5.1 %copy-start.22 = (bf16[512]{0:T(512)(128)(2,1)S(1)}, bf16[512]{0:T(512)(128)(2,1)}, u32[]{:S(2)}) copy-start(bf16[512]{0:T(512)(128)(2,1)} %param.20) | copy-start | bytes 3076
  3.6 5.0 %copy-start.23 = (bf16[512]{0:T(512)(128)(2,1)S(1)}, bf16[512]{0:T(512)(128)(2,1)}, u32[]{:S(2)}) copy-start(bf16[512]{0:T(512)(128)(2,1)} %param.23) | copy-start | bytes 3076
  3.7 5.0 %copy-start.24 = (bf16[512]{0:T(512)(128)(2,1)S(1)}, bf16[512]{0:T(512)(128)(2,1)}, u32[]{:S(2)}) copy-start(bf16[512]{0:T(512)(128)(2,1)} %param.26) | copy-start | bytes 3076
  3.7 5.1 %copy-start.8 = (bf16[512,2048]{1,0:T(8,128)(2,1)S(1)}, bf16[512,2048]{1,0:T(8,128)(2,1)}, u32[]{:S(2)}) copy-start(bf16[512,2048]{1,0:T(8,128)(2,1)} %refs_6_.1) | copy-start | bytes 6291460
  5.6 14.9 %collective-permute-start = (bf16[1,528,512]{2,1,0:T(8,128)(2,1)}, bf16[1,528,512]{2,1,0:T(8,128)(2,1)}, u32[]{:S(2)}, u32[]{:S(2)}) collective-permute-start(bf16[1,528,512]{2,1,0:T(8,128)(2,1)} %get-tuple-element.143), channel_id=1, source_target_pairs={{0,8},{8,0},{16,24},{24,16},{1,9},{9,1},{17,25},{25,17},{2,10},{10... | collective-permute-start | bytes 1622024 | tf_op jit(solution)/shard_map/ppermute | solution.py:748
  6.0 16.0 %collective-permute-start.1 = (bf16[1,528,512]{2,1,0:T(8,128)(2,1)}, bf16[1,528,512]{2,1,0:T(8,128)(2,1)}, u32[]{:S(2)}, u32[]{:S(2)}) collective-permute-start(bf16[1,528,512]{2,1,0:T(8,128)(2,1)} %get-tuple-element.144), channel_id=1, source_target_pairs={{0,16},{8,24},{16,0},{24,8},{1,17},{9,25},{17,1},{25,9},{2,18},{10... | collective-permute-start | bytes 1622024 | tf_op jit(solution)/shard_map/ppermute | solution.py:748
  8.5 24.7 %collective-permute-start.2 = (bf16[1,528,512]{2,1,0:T(8,128)(2,1)}, bf16[1,528,512]{2,1,0:T(8,128)(2,1)}, u32[]{:S(2)}, u32[]{:S(2)}) collective-permute-start(bf16[1,528,512]{2,1,0:T(8,128)(2,1)} %pad_maximum_fusion.9), channel_id=1, source_target_pairs={{0,24},{8,16},{16,8},{24,0},{1,25},{9,17},{17,9},{25,1},{2,26},{10... | collective-permute-start | bytes 1622024 | tf_op jit(solution)/shard_map/ppermute | solution.py:748
  15.5 17.7 %copy-start.9 = (bf16[4,1,512,512]{3,2,1,0:T(8,128)(2,1)S(1)}, bf16[4,1,512,512]{3,2,1,0:T(8,128)(2,1)}, u32[]{:S(2)}) copy-start(bf16[4,1,512,512]{3,2,1,0:T(8,128)(2,1)} %param.30) | copy-start | bytes 6291460
  17.7 15.6 %copy-start.21 = (bf16[4,1,64,512]{3,2,1,0:T(8,128)(2,1)S(1)}, bf16[4,1,64,512]{3,2,1,0:T(8,128)(2,1)}, u32[]{:S(2)}) copy-start(bf16[4,1,64,512]{3,2,1,0:T(8,128)(2,1)} %param.31) | copy-start | bytes 786436
  33.5 67.5 %collective-permute-start.3 = (bf16[1,576,512]{2,1,0:T(8,128)(2,1)S(1)}, bf16[1,576,512]{2,1,0:T(8,128)(2,1)}, u32[]{:S(2)}, u32[]{:S(2)}) collective-permute-start(bf16[1,576,512]{2,1,0:T(8,128)(2,1)S(1)} %pad_maximum_fusion.3), channel_id=1, source_target_pairs={{0,8},{8,0},{16,24},{24,16},{1,9},{9,1},{17,25},{25,17},{2,10},{10... | collective-permute-start | bytes 1769480 | tf_op jit(solution)/shard_map/ppermute | solution.py:748
  33.7 67.4 %collective-permute-start.4 = (bf16[1,576,512]{2,1,0:T(8,128)(2,1)S(1)}, bf16[1,576,512]{2,1,0:T(8,128)(2,1)}, u32[]{:S(2)}, u32[]{:S(2)}) collective-permute-start(bf16[1,576,512]{2,1,0:T(8,128)(2,1)S(1)} %pad_maximum_fusion.4), channel_id=1, source_target_pairs={{0,16},{8,24},{16,0},{24,8},{1,17},{9,25},{17,1},{25,9},{2,18},{10... | collective-permute-start | bytes 1769480 | tf_op jit(solution)/shard_map/ppermute | solution.py:748
  35.3 65.7 %collective-permute-start.5 = (bf16[1,576,512]{2,1,0:T(8,128)(2,1)S(1)}, bf16[1,576,512]{2,1,0:T(8,128)(2,1)}, u32[]{:S(2)}, u32[]{:S(2)}) collective-permute-start(bf16[1,576,512]{2,1,0:T(8,128)(2,1)S(1)} %pad_maximum_fusion.5), channel_id=1, source_target_pairs={{0,24},{8,16},{16,8},{24,0},{1,25},{9,17},{17,9},{25,1},{2,26},{10... | collective-permute-start | bytes 1769480 | tf_op jit(solution)/shard_map/ppermute | solution.py:748
  99.0 48.1 %collective-permute-start.6 = (bf16[1,576,512]{2,1,0:T(8,128)(2,1)}, bf16[1,576,512]{2,1,0:T(8,128)(2,1)S(1)}, u32[]{:S(2)}, u32[]{:S(2)}) collective-permute-start(bf16[1,576,512]{2,1,0:T(8,128)(2,1)} %get-tuple-element.293), channel_id=1, source_target_pairs={{0,8},{8,0},{16,24},{24,16},{1,9},{9,1},{17,25},{25,17},{2,10},{10... | collective-permute-start | bytes 1769480 | tf_op jit(solution)/shard_map/ppermute | solution.py:748
  99.4 47.7 %collective-permute-start.7 = (bf16[1,576,512]{2,1,0:T(8,128)(2,1)}, bf16[1,576,512]{2,1,0:T(8,128)(2,1)S(1)}, u32[]{:S(2)}, u32[]{:S(2)}) collective-permute-start(bf16[1,576,512]{2,1,0:T(8,128)(2,1)} %get-tuple-element.292), channel_id=1, source_target_pairs={{0,16},{8,24},{16,0},{24,8},{1,17},{9,25},{17,1},{25,9},{2,18},{10... | collective-permute-start | bytes 1769480 | tf_op jit(solution)/shard_map/ppermute | solution.py:748
  101.0 46.1 %collective-permute-start.8 = (bf16[1,576,512]{2,1,0:T(8,128)(2,1)}, bf16[1,576,512]{2,1,0:T(8,128)(2,1)S(1)}, u32[]{:S(2)}, u32[]{:S(2)}) collective-permute-start(bf16[1,576,512]{2,1,0:T(8,128)(2,1)} %get-tuple-element.291), channel_id=1, source_target_pairs={{0,24},{8,16},{16,8},{24,0},{1,25},{9,17},{17,9},{25,1},{2,26},{10... | collective-permute-start | bytes 1769480 | tf_op jit(solution)/shard_map/ppermute | solution.py:748
  147.1 10.9 %copy-start.12 = (bf16[1,576,512]{2,1,0:T(8,128)(2,1)}, bf16[1,576,512]{2,1,0:T(8,128)(2,1)S(1)}, u32[]{:S(2)}) copy-start(bf16[1,576,512]{2,1,0:T(8,128)(2,1)S(1)} %collective-permute-done.6) | copy-start | bytes 1769476
  147.1 10.9 %copy-start.14 = (bf16[1,576,512]{2,1,0:T(8,128)(2,1)}, bf16[1,576,512]{2,1,0:T(8,128)(2,1)S(1)}, u32[]{:S(2)}) copy-start(bf16[1,576,512]{2,1,0:T(8,128)(2,1)S(1)} %collective-permute-done.7) | copy-start | bytes 1769476
  147.2 10.9 %copy-start.16 = (bf16[1,576,512]{2,1,0:T(8,128)(2,1)}, bf16[1,576,512]{2,1,0:T(8,128)(2,1)S(1)}, u32[]{:S(2)}) copy-start(bf16[1,576,512]{2,1,0:T(8,128)(2,1)S(1)} %collective-permute-done.8) | copy-start | bytes 1769476
  158.0 13.6 %collective-permute-start.9 = (bf16[512,2048]{1,0:T(8,128)(2,1)}, bf16[512,2048]{1,0:T(8,128)(2,1)S(1)}, u32[]{:S(2)}, u32[]{:S(2)}) collective-permute-start(bf16[512,2048]{1,0:T(8,128)(2,1)} %get-tuple-element.179), channel_id=1, source_target_pairs={{0,8},{1,9},{2,10},{3,11},{4,12},{5,13},{6,14},{7,15},{8,0},{9,1},... | collective-permute-start | bytes 6291464 | tf_op jit(solution)/shard_map/ppermute | solution.py:773
  158.5 11.0 %collective-permute-start.10 = (bf16[512,1024]{1,0:T(8,128)(2,1)}, bf16[512,1024]{1,0:T(8,128)(2,1)}, u32[]{:S(2)}, u32[]{:S(2)}) collective-permute-start(bf16[512,1024]{1,0:T(8,128)(2,1)} %get-tuple-element.180), channel_id=1, source_target_pairs={{0,8},{1,9},{2,10},{3,11},{4,12},{5,13},{6,14},{7,15},{8,0},{9,1},... | collective-permute-start | bytes 3145736 | tf_op jit(solution)/shard_map/ppermute | solution.py:773
  174.3 14.6 %collective-permute-start.12 = (bf16[256,1024]{1,0:T(8,128)(2,1)}, bf16[256,1024]{1,0:T(8,128)(2,1)}, u32[]{:S(2)}, u32[]{:S(2)}) collective-permute-start(bf16[256,1024]{1,0:T(8,128)(2,1)} %dynamic-slice_add_fusion.3), channel_id=1, source_target_pairs={{0,2},{1,3},{2,0},{3,1},{4,6},{5,7},{6,4},{7,5},{8,10},{9,11},{10,... | collective-permute-start | bytes 1572872 | tf_op jit(solution)/shard_map/ppermute | solution.py:773
  175.9 15.2 %collective-permute-start.11 = (bf16[256,2048]{1,0:T(8,128)(2,1)}, bf16[256,2048]{1,0:T(8,128)(2,1)}, u32[]{:S(2)}, u32[]{:S(2)}) collective-permute-start(bf16[256,2048]{1,0:T(8,128)(2,1)} %dynamic-slice_add_fusion), channel_id=1, source_target_pairs={{0,1},{1,0},{2,3},{3,2},{4,5},{5,4},{6,7},{7,6},{8,24},{9,25},{10,... | collective-permute-start | bytes 3145736 | tf_op jit(solution)/shard_map/ppermute | solution.py:773
  177.4 11.4 %copy-start.10 = (bf16[512,1024]{1,0:T(8,128)(2,1)S(1)}, bf16[512,1024]{1,0:T(8,128)(2,1)}, u32[]{:S(2)}) copy-start(bf16[512,1024]{1,0:T(8,128)(2,1)} %get-tuple-element.183) | copy-start | bytes 3145732
  188.0 3.1 copy-start.5
  192.9 24.0 %collective-permute-start.14 = (bf16[128,1024]{1,0:T(8,128)(2,1)S(1)}, bf16[128,1024]{1,0:T(8,128)(2,1)S(1)}, u32[]{:S(2)}, u32[]{:S(2)}) collective-permute-start(bf16[128,1024]{1,0:T(8,128)(2,1)S(1)} %constant_dynamic-slice_fusion.14), channel_id=1, source_target_pairs={{0,4},{1,5},{2,6},{3,7},{4,0},{5,1},{6,2},{7,3},{8,12},{9,13},{10,... | collective-permute-start | bytes 786440 | tf_op jit(solution)/shard_map/ppermute | solution.py:773
  195.7 21.4 %collective-permute-start.13 = (bf16[128,2048]{1,0:T(8,128)(2,1)S(1)}, bf16[128,2048]{1,0:T(8,128)(2,1)S(1)}, u32[]{:S(2)}, u32[]{:S(2)}) collective-permute-start(bf16[128,2048]{1,0:T(8,128)(2,1)S(1)} %constant_dynamic-slice_fusion.15), channel_id=1, source_target_pairs={{0,16},{1,17},{2,18},{3,19},{4,20},{5,21},{6,22},{7,23},{8,9},{9,8... | collective-permute-start | bytes 1572872 | tf_op jit(solution)/shard_map/ppermute | solution.py:773
  197.2 23.2 %collective-permute-start.16 = (bf16[1,512,512]{2,1,0:T(8,128)(2,1)}, bf16[1,512,512]{2,1,0:T(8,128)(2,1)}, u32[]{:S(2)}, u32[]{:S(2)}) collective-permute-start(bf16[1,512,512]{2,1,0:T(8,128)(2,1)} %get-tuple-element.210), channel_id=1, source_target_pairs={{0,16},{8,24},{16,0},{24,8},{1,17},{9,25},{17,1},{25,9},{2,18},{10... | collective-permute-start | bytes 1572872 | tf_op jit(solution)/shard_map/ppermute | solution.py:748
  197.7 19.2 %copy-start.7 = (bf16[256,1024]{1,0:T(8,128)(2,1)S(1)}, bf16[256,1024]{1,0:T(8,128)(2,1)}, u32[]{:S(2)}) copy-start(bf16[256,1024]{1,0:T(8,128)(2,1)} %copy-done.6) | copy-start | bytes 1572868
  216.9 3.5 %copy-start.11 = (bf16[2,512,512]{2,1,0:T(8,128)(2,1)S(1)}, bf16[2,512,512]{2,1,0:T(8,128)(2,1)}, u32[]{:S(2)}) copy-start(bf16[2,512,512]{2,1,0:T(8,128)(2,1)} %get-tuple-element.219) | copy-start | bytes 3145732
  217.2 13.7 %collective-permute-start.17 = (bf16[64,1024]{1,0:T(8,128)(2,1)S(1)}, bf16[64,1024]{1,0:T(8,128)(2,1)S(1)}, u32[]{:S(2)}, u32[]{:S(2)}) collective-permute-start(bf16[64,1024]{1,0:T(8,128)(2,1)S(1)} %constant_dynamic-slice_fusion.12), channel_id=1, source_target_pairs={{0,1},{1,0},{2,3},{3,2},{4,5},{5,4},{6,7},{7,6},{8,24},{9,25},{10,... | collective-permute-start | bytes 393224 | tf_op jit(solution)/shard_map/ppermute | solution.py:773
  218.8 12.2 %collective-permute-start.15 = (bf16[64,2048]{1,0:T(8,128)(2,1)S(1)}, bf16[64,2048]{1,0:T(8,128)(2,1)S(1)}, u32[]{:S(2)}, u32[]{:S(2)}) collective-permute-start(bf16[64,2048]{1,0:T(8,128)(2,1)S(1)} %constant_dynamic-slice_fusion.13), channel_id=1, source_target_pairs={{0,2},{1,3},{2,0},{3,1},{4,6},{5,7},{6,4},{7,5},{8,10},{9,11},{10,... | collective-permute-start | bytes 786440 | tf_op jit(solution)/shard_map/ppermute | solution.py:773
  220.5 14.2 %collective-permute-start.19 = (bf16[1,512,512]{2,1,0:T(8,128)(2,1)S(1)}, bf16[1,512,512]{2,1,0:T(8,128)(2,1)S(1)}, u32[]{:S(2)}, u32[]{:S(2)}) collective-permute-start(bf16[1,512,512]{2,1,0:T(8,128)(2,1)S(1)} %get-tuple-element.305), channel_id=1, source_target_pairs={{0,24},{8,16},{16,8},{24,0},{1,25},{9,17},{17,9},{25,1},{2,26},{10... | collective-permute-start | bytes 1572872 | tf_op jit(solution)/shard_map/ppermute | solution.py:748
  231.1 10.8 %collective-permute-start.20 = (bf16[64,1024]{1,0:T(8,128)(2,1)S(1)}, bf16[64,1024]{1,0:T(8,128)(2,1)S(1)}, u32[]{:S(2)}, u32[]{:S(2)}) collective-permute-start(bf16[64,1024]{1,0:T(8,128)(2,1)S(1)} %dynamic-slice_add_fusion.8), channel_id=1, source_target_pairs={{0,16},{1,17},{2,18},{3,19},{4,20},{5,21},{6,22},{7,23},{8,9},{9,8... | collective-permute-start | bytes 393224 | tf_op jit(solution)/shard_map/ppermute | solution.py:773
  232.7 10.0 %collective-permute-start.18 = (bf16[32,2048]{1,0:T(8,128)(2,1)S(1)}, bf16[32,2048]{1,0:T(8,128)(2,1)S(1)}, u32[]{:S(2)}, u32[]{:S(2)}) collective-permute-start(bf16[32,2048]{1,0:T(8,128)(2,1)S(1)} %constant_dynamic-slice_fusion.11), channel_id=1, source_target_pairs={{0,4},{1,5},{2,6},{3,7},{4,0},{5,1},{6,2},{7,3},{8,12},{9,13},{10,... | collective-permute-start | bytes 393224 | tf_op jit(solution)/shard_map/ppermute | solution.py:773
  235.5 7.8 %copy-start.13 = (bf16[1,576,512]{2,1,0:T(8,128)(2,1)S(1)}, bf16[1,576,512]{2,1,0:T(8,128)(2,1)}, u32[]{:S(2)}) copy-start(bf16[1,576,512]{2,1,0:T(8,128)(2,1)} %copy-done.12) | copy-start | bytes 1769476
  235.5 7.8 %copy-start.15 = (bf16[1,576,512]{2,1,0:T(8,128)(2,1)S(1)}, bf16[1,576,512]{2,1,0:T(8,128)(2,1)}, u32[]{:S(2)}) copy-start(bf16[1,576,512]{2,1,0:T(8,128)(2,1)} %copy-done.14) | copy-start | bytes 1769476
  235.5 7.8 %copy-start.17 = (bf16[1,576,512]{2,1,0:T(8,128)(2,1)S(1)}, bf16[1,576,512]{2,1,0:T(8,128)(2,1)}, u32[]{:S(2)}) copy-start(bf16[1,576,512]{2,1,0:T(8,128)(2,1)} %copy-done.16) | copy-start | bytes 1769476
  242.7 10.6 %collective-permute-start.22 = (bf16[512,1152]{1,0:T(8,128)(2,1)}, bf16[512,1152]{1,0:T(8,128)(2,1)}, u32[]{:S(2)}, u32[]{:S(2)}) collective-permute-start(bf16[512,1152]{1,0:T(8,128)(2,1)} %late_weights.2), channel_id=1, source_target_pairs={{0,8},{1,9},{2,10},{3,11},{4,12},{5,13},{6,14},{7,15},{8,0},{9,1},... | collective-permute-start | bytes 3538952 | tf_op jit(solution)/shard_map/ppermute | solution.py:773
  242.9 3.9 %collective-permute-start.21 = (bf16[1,512,512]{2,1,0:T(8,128)(2,1)}, bf16[1,512,512]{2,1,0:T(8,128)(2,1)S(1)}, u32[]{:S(2)}, u32[]{:S(2)}) collective-permute-start(bf16[1,512,512]{2,1,0:T(8,128)(2,1)} %get-tuple-element.231), channel_id=1, source_target_pairs={{0,8},{8,0},{16,24},{24,16},{1,9},{9,1},{17,25},{25,17},{2,10},{10... | collective-permute-start | bytes 1572872 | tf_op jit(solution)/shard_map/ppermute | solution.py:748
  244.7 11.0 %collective-permute-start.31 = (bf16[64,1024]{1,0:T(8,128)(2,1)}, bf16[64,1024]{1,0:T(8,128)(2,1)S(1)}, u32[]{:S(2)}, u32[]{:S(2)}) collective-permute-start(bf16[64,1024]{1,0:T(8,128)(2,1)} %add.339), channel_id=1, source_target_pairs={{0,1},{1,0},{2,3},{3,2},{4,5},{5,4},{6,7},{7,6},{8,24},{9,25},{10,... | collective-permute-start | bytes 393224 | tf_op jit(solution)/shard_map/ppermute | solution.py:773
  245.3 11.4 %collective-permute-start.30 = (bf16[32,2048]{1,0:T(8,128)(2,1)S(1)}, bf16[32,2048]{1,0:T(8,128)(2,1)S(1)}, u32[]{:S(2)}, u32[]{:S(2)}) collective-permute-start(bf16[32,2048]{1,0:T(8,128)(2,1)S(1)} %dynamic-slice_add_fusion.9), channel_id=1, source_target_pairs={{0,4},{1,5},{2,6},{3,7},{4,0},{5,1},{6,2},{7,3},{8,12},{9,13},{10,... | collective-permute-start | bytes 393224 | tf_op jit(solution)/shard_map/ppermute | solution.py:773
  254.7 5.7 %copy-start.19 = (bf16[1,512,512]{2,1,0:T(8,128)(2,1)S(1)}, bf16[1,512,512]{2,1,0:T(8,128)(2,1)}, u32[]{:S(2)}) copy-start(bf16[1,512,512]{2,1,0:T(8,128)(2,1)} %copy-done.18) | copy-start | bytes 1572868
  254.7 9.9 %collective-permute-start.23 = (bf16[256,1152]{1,0:T(8,128)(2,1)S(1)}, bf16[256,1152]{1,0:T(8,128)(2,1)S(1)}, u32[]{:S(2)}, u32[]{:S(2)}) collective-permute-start(bf16[256,1152]{1,0:T(8,128)(2,1)S(1)} %dynamic-slice_add_fusion.1), channel_id=1, source_target_pairs={{0,1},{1,0},{2,3},{3,2},{4,5},{5,4},{6,7},{7,6},{8,24},{9,25},{10,... | collective-permute-start | bytes 1769480 | tf_op jit(solution)/shard_map/ppermute | solution.py:773
  256.7 13.8 %collective-permute-start.33 = (bf16[128,1024]{1,0:T(8,128)(2,1)S(1)}, bf16[128,1024]{1,0:T(8,128)(2,1)S(1)}, u32[]{:S(2)}, u32[]{:S(2)}) collective-permute-start(bf16[128,1024]{1,0:T(8,128)(2,1)S(1)} %pad_maximum_fusion.14), channel_id=1, source_target_pairs={{0,4},{1,5},{2,6},{3,7},{4,0},{5,1},{6,2},{7,3},{8,12},{9,13},{10,... | collective-permute-start | bytes 786440 | tf_op jit(solution)/shard_map/ppermute | solution.py:773
  258.8 12.6 %collective-permute-start.32 = (bf16[64,2048]{1,0:T(8,128)(2,1)S(1)}, bf16[64,2048]{1,0:T(8,128)(2,1)S(1)}, u32[]{:S(2)}, u32[]{:S(2)}) collective-permute-start(bf16[64,2048]{1,0:T(8,128)(2,1)S(1)} %pad_maximum_fusion.13), channel_id=1, source_target_pairs={{0,2},{1,3},{2,0},{3,1},{4,6},{5,7},{6,4},{7,5},{8,10},{9,11},{10,... | collective-permute-start | bytes 786440 | tf_op jit(solution)/shard_map/ppermute | solution.py:773
  260.6 4.1 %copy-start.1 = (bf16[512,1152]{1,0:T(8,128)(2,1)S(1)}, bf16[512,1152]{1,0:T(8,128)(2,1)}, u32[]{:S(2)}) copy-start(bf16[512,1152]{1,0:T(8,128)(2,1)} %late_weights.3) | copy-start | bytes 3538948
  263.0 3.7 %copy-start.3 = (bf16[1,576,512]{2,1,0:T(8,128)(2,1)S(1)}, bf16[1,576,512]{2,1,0:T(8,128)(2,1)}, u32[]{:S(2)}) copy-start(bf16[1,576,512]{2,1,0:T(8,128)(2,1)} %get-tuple-element.288) | copy-start | bytes 1769476
  263.0 3.7 %copy-start.4 = (bf16[1,576,512]{2,1,0:T(8,128)(2,1)S(1)}, bf16[1,576,512]{2,1,0:T(8,128)(2,1)}, u32[]{:S(2)}) copy-start(bf16[1,576,512]{2,1,0:T(8,128)(2,1)} %get-tuple-element.289) | copy-start | bytes 1769476
  266.0 6.8 %collective-permute-start.24 = (bf16[128,1152]{1,0:T(8,128)(2,1)S(1)}, bf16[128,1152]{1,0:T(8,128)(2,1)S(1)}, u32[]{:S(2)}, u32[]{:S(2)}) collective-permute-start(bf16[128,1152]{1,0:T(8,128)(2,1)S(1)} %constant_dynamic-slice_fusion.6), channel_id=1, source_target_pairs={{0,16},{1,17},{2,18},{3,19},{4,20},{5,21},{6,22},{7,23},{8,9},{9,8... | collective-permute-start | bytes 884744 | tf_op jit(solution)/shard_map/ppermute | solution.py:773
  272.9 6.9 %collective-permute-start.25 = (bf16[64,1152]{1,0:T(8,128)(2,1)S(1)}, bf16[64,1152]{1,0:T(8,128)(2,1)S(1)}, u32[]{:S(2)}, u32[]{:S(2)}) collective-permute-start(bf16[64,1152]{1,0:T(8,128)(2,1)S(1)} %constant_dynamic-slice_fusion), channel_id=1, source_target_pairs={{0,2},{1,3},{2,0},{3,1},{4,6},{5,7},{6,4},{7,5},{8,10},{9,11},{10,... | collective-permute-start | bytes 442376 | tf_op jit(solution)/shard_map/ppermute | solution.py:773
  274.3 13.8 %collective-permute-start.35 = (bf16[256,1024]{1,0:T(8,128)(2,1)}, bf16[256,1024]{1,0:T(8,128)(2,1)}, u32[]{:S(2)}, u32[]{:S(2)}) collective-permute-start(bf16[256,1024]{1,0:T(8,128)(2,1)} %pad_maximum_fusion.11.refs_1_), channel_id=1, source_target_pairs={{0,2},{1,3},{2,0},{3,1},{4,6},{5,7},{6,4},{7,5},{8,10},{9,11},{10,... | collective-permute-start | bytes 1572872 | tf_op jit(solution)/shard_map/ppermute | solution.py:773
  275.8 12.2 %collective-permute-start.34 = (bf16[128,2048]{1,0:T(8,128)(2,1)S(1)}, bf16[128,2048]{1,0:T(8,128)(2,1)S(1)}, u32[]{:S(2)}, u32[]{:S(2)}) collective-permute-start(bf16[128,2048]{1,0:T(8,128)(2,1)S(1)} %pad_maximum_fusion.10), channel_id=1, source_target_pairs={{0,16},{1,17},{2,18},{3,19},{4,20},{5,21},{6,22},{7,23},{8,9},{9,8... | collective-permute-start | bytes 1572872 | tf_op jit(solution)/shard_map/ppermute | solution.py:773
  288.2 29.4 %copy-start.2 = (bf16[256,2048]{1,0:T(8,128)(2,1)}, bf16[256,2048]{1,0:T(8,128)(2,1)S(1)}, u32[]{:S(2)}) copy-start(bf16[256,2048]{1,0:T(8,128)(2,1)S(1)} %pad_maximum_fusion.2.refs_1_) | copy-start | bytes 3145732
  288.2 16.2 %collective-permute-start.36 = (bf16[256,2048]{1,0:T(8,128)(2,1)S(1)}, bf16[256,2048]{1,0:T(8,128)(2,1)}, u32[]{:S(2)}, u32[]{:S(2)}) collective-permute-start(bf16[256,2048]{1,0:T(8,128)(2,1)S(1)} %pad_maximum_fusion.2.refs_1_), channel_id=1, source_target_pairs={{0,1},{1,0},{2,3},{3,2},{4,5},{5,4},{6,7},{7,6},{8,24},{9,25},{10,... | collective-permute-start | bytes 3145736 | tf_op jit(solution)/shard_map/ppermute | solution.py:773
  289.7 7.7 %collective-permute-start.26 = (bf16[64,1152]{1,0:T(8,128)(2,1)S(1)}, bf16[64,1152]{1,0:T(8,128)(2,1)S(1)}, u32[]{:S(2)}, u32[]{:S(2)}) collective-permute-start(bf16[64,1152]{1,0:T(8,128)(2,1)S(1)} %dynamic-slice_add_fusion.7), channel_id=1, source_target_pairs={{0,4},{1,5},{2,6},{3,7},{4,0},{5,1},{6,2},{7,3},{8,12},{9,13},{10,... | collective-permute-start | bytes 442376 | tf_op jit(solution)/shard_map/ppermute | solution.py:773
  297.4 5.2 %collective-permute-start.27 = (bf16[64,1152]{1,0:T(8,128)(2,1)S(1)}, bf16[64,1152]{1,0:T(8,128)(2,1)S(1)}, u32[]{:S(2)}, u32[]{:S(2)}) collective-permute-start(bf16[64,1152]{1,0:T(8,128)(2,1)S(1)} %add.350), channel_id=1, source_target_pairs={{0,2},{1,3},{2,0},{3,1},{4,6},{5,7},{6,4},{7,5},{8,10},{9,11},{10,... | collective-permute-start | bytes 442376 | tf_op jit(solution)/shard_map/ppermute | solution.py:773
  302.7 6.8 %collective-permute-start.28 = (bf16[128,1152]{1,0:T(8,128)(2,1)S(1)}, bf16[128,1152]{1,0:T(8,128)(2,1)S(1)}, u32[]{:S(2)}, u32[]{:S(2)}) collective-permute-start(bf16[128,1152]{1,0:T(8,128)(2,1)S(1)} %pad_maximum_fusion.12), channel_id=1, source_target_pairs={{0,16},{1,17},{2,18},{3,19},{4,20},{5,21},{6,22},{7,23},{8,9},{9,8... | collective-permute-start | bytes 884744 | tf_op jit(solution)/shard_map/ppermute | solution.py:773
  304.4 13.2 %collective-permute-start.37 = (bf16[256,2048]{1,0:T(8,128)(2,1)S(1)}, bf16[256,2048]{1,0:T(8,128)(2,1)}, u32[]{:S(2)}, u32[]{:S(2)}) collective-permute-start(bf16[256,2048]{1,0:T(8,128)(2,1)S(1)} %pad_maximum_fusion.2.refs_1_), channel_id=1, source_target_pairs={{0,8},{1,9},{2,10},{3,11},{4,12},{5,13},{6,14},{7,15},{8,0},{9,1},... | collective-permute-start | bytes 3145736 | tf_op jit(solution)/shard_map/ppermute | solution.py:773
  304.4 13.2 %collective-permute-start.38 = (bf16[256,2048]{1,0:T(8,128)(2,1)}, bf16[256,2048]{1,0:T(8,128)(2,1)}, u32[]{:S(2)}, u32[]{:S(2)}) collective-permute-start(bf16[256,2048]{1,0:T(8,128)(2,1)} %collective-permute-done.36.refs_2_), channel_id=1, source_target_pairs={{0,8},{1,9},{2,10},{3,11},{4,12},{5,13},{6,14},{7,15},{8,0},{9,1},... | collective-permute-start | bytes 3145736 | tf_op jit(solution)/shard_map/ppermute | solution.py:773
  310.4 13.0 %collective-permute-start.29 = (bf16[256,1152]{1,0:T(8,128)(2,1)}, bf16[256,1152]{1,0:T(8,128)(2,1)}, u32[]{:S(2)}, u32[]{:S(2)}) collective-permute-start(bf16[256,1152]{1,0:T(8,128)(2,1)} %pad_maximum_fusion.6.refs_1_), channel_id=1, source_target_pairs={{0,1},{1,0},{2,3},{3,2},{4,5},{5,4},{6,7},{7,6},{8,24},{9,25},{10,... | collective-permute-start | bytes 1769480 | tf_op jit(solution)/shard_map/ppermute | solution.py:773
  310.9 2.3 collective-permute-start.39
  310.9 3.0 collective-permute-start.40
  323.4 2.8 collective-permute-start.41
  323.6 2.9 collective-permute-start.42
  (6 other events, 8.4 us)

commit v2 on v1

--- a/solution.py
+++ b/solution.py
@@ -1354,8 +1354,9 @@
     (done,) = late.finish(done)
     advance([late])
     advance([late])
-    advance(groups, late.sent)
+    advance([ffn], late.sent)
     advance([late])
+    advance([write], late.sent)
     advance([late])
     while ffn.steps or write.steps:
         advance(groups, late.sent)

time: 337 us -> 334 us (level)
  waiting for transfers between devices: 53.6 us -> 47.5 us
  starting transfers between devices: 35.2 us -> 38.8 us
    ppermute x31, waiting for transfers between devices: 39.1 us -> 33 us  [phase_swap(): return lax.ppermute(value, ('section', 'dp'), route)]
    ppermute x31, starting transfers between devices: 27.1 us -> 30.7 us  [phase_swap(): return lax.ppermute(value, ('section', 'dp'), route)]
  transfers between devices with their start and end apart: 43 -> 43, of which waited for: 17 -> 18; matrix products, arithmetic and copies ran while one was open for 11% -> 11% of each run, Pallas kernels for 54% -> 54%
where the time goes in v2:
time: 334 us; the launch traced here: 331 us
  Pallas kernels  194 us (58%)
  waiting for transfers between devices  47.5 us (14%)
  starting transfers between devices  38.8 us (12%)
  local copies, waits for them, and re-layouts  25.1 us (8%)
  other arithmetic  23.7 us (7%)
    pallas_call x1, Pallas kernels, forward_chain(): pl.pallas_call(lambda *refs: forward_kernel(sources, segs, *refs), grid_s...  60 us
    pallas_call x1, Pallas kernels, backward_chain(): pl.pallas_call(lambda *refs: chain_kernel(sources, segs, *refs), grid_spe...  46.1 us
    pallas_call x3, Pallas kernels, attention_back(): pl.pallas_call(lambda *refs: attention_kernel(alone, *refs), grid_spec=pl...  40.2 us
    ppermute x31, waiting for transfers between devices, phase_swap(): return lax.ppermute(value, ('section', 'dp'), route)  33 us
    ppermute x31, starting transfers between devices, phase_swap(): return lax.ppermute(value, ('section', 'dp'), route)  30.7 us
    pallas_call x2, Pallas kernels, early_weights(): pl.pallas_call(early_weights_kernel, grid_spec=pltpu.PrefetchScalarGridSp...  21.1 us
    unnamed x64, local copies, waits for them, and re-layouts  16.9 us
    ppermute x12, waiting for transfers between devices, swap_pairs(): return lax.ppermute(value, axis, [(i, i ^ mask) for i in range(size)])  14.5 us
  transfers between devices with their start and end apart: 43, of which 18 were waited for; matrix products, arithmetic and copies ran while one was open for 11% of the time, Pallas kernels for 54%

profile of v2, /device:TPU:0, one launch (start us, length us, event | category | flops | bytes accessed | tf_op | source)
XLA Modules:
  0.0 331.1 jit_solution(10511705637061102717)
XLA Ops:
  2.2 1.5 dynamic-slice_bitcast_fusion
  4.5 1.0 pad_maximum_fusion.7
  6.0 2.5 collective-permute-start.1
  8.7 2.5 copy.34
  11.2 2.7 copy.35
  14.0 1.6 copy.32
  15.5 2.2 copy.36
  17.7 2.1 copy.33
  20.4 1.6 collective-permute-done.1.refs_15_
  22.0 11.2 %collective-permute-done.2.refs_16_ = bf16[1,528,512]{2,1,0:T(8,128)(2,1)} collective-permute-done((bf16[1,528,512]{2,1,0:T(8,128)(2,1)}, bf16[1,528,512]{2,1,0:T(8,128)(2,1)}, u32[]{:S(2)}, u32[]{:S(2)}) %collective-permute-start.2) | collective-permute-done | bytes 540704 | tf_op jit(solution)/shard_map/ppermute | solution.py:748
  33.7 1.6 collective-permute-start.4
  36.1 60.0 %forward_chain.1 = (bf16[4,576,512]{2,1,0:T(8,128)(2,1)}, bf16[512,2048]{1,0:T(8,128)(2,1)}, bf16[4,512,64]{2,1,0:T(8,128)(2,1)}, bf16[4,512,512]{2,1,0:T(8,128)...) custom-call(s32[1]{0:T(128)} %bitcast.1.refs_0_, ...), custom_call_target="tpu_custom_call" | custom-call | flops 60000002048 | bytes 1048576 | tf_op jit(solution)/shard_map/forward_chain/pallas_call | solution.py:587
  96.1 2.8 constant_dynamic-slice_fusion.5
  99.4 1.6 collective-permute-start.7
  101.0 46.1 %backward_chain.1 = (bf16[4,512,64]{2,1,0:T(8,128)(2,1)}, bf16[1024,2048]{1,0:T(8,128)(2,1)}, bf16[4,1536,64]{2,1,0:T(8,128)(2,1)}, bf16[512,2048]{1,0:T(8,128)(...) custom-call(s32[1]{0:T(128)} %bitcast.1.refs_0_, ...), custom_call_target="tpu_custom_call" | custom-call | flops 44000002048 | bytes 1048576 | tf_op jit(solution)/shard_map/backward_chain/pallas_call | solution.py:669
  147.2 10.8 %early_weights.2 = (bf16[512,2048]{1,0:T(8,128)(2,1)}, bf16[512,1024]{1,0:T(8,128)(2,1)}) custom-call(s32[1]{0:T(128)S(6)} %sub.100.side_ref.refs_0_, bf16[512,2048]{1,0:T(8,128)(2,1)} %get-tuple-element.151.refs_14_.a2_ref, bf16[2048,2048]{1,0:T(8,128)(2,1)} %get-tuple-element.171.gu_ref, bf16[512,2048]{1,0:T(8,128)(2,1)} %get-tuple-element.172.bf_ref, ...), custom_call_target="tpu_custom_call" | custom-call | flops 8999999488 | bytes 1048576 | tf_op jit(solution)/shard_map/early_weights/pallas_call | solution.py:876
  159.2 10.3 %early_weights.3 = (bf16[512,2048]{1,0:T(8,128)(2,1)}, bf16[512,1024]{1,0:T(8,128)(2,1)}) custom-call(s32[1]{0:T(128)} %bitcast.side_ref.refs_0_, bf16[512,2048]{1,0:T(8,128)(2,1)} %get-tuple-element.151.refs_14_.a2_ref, bf16[2048,2048]{1,0:T(8,128)(2,1)} %get-tuple-element.171.gu_ref, bf16[512,2048]{1,0:T(8,128)(2,1)} %get-tuple-element.172.bf_ref, ...), custom_call_target="tpu_custom_call" | custom-call | flops 8999999488 | bytes 1048576 | tf_op jit(solution)/shard_map/early_weights/pallas_call | solution.py:876
  169.5 2.2 dynamic-slice_add_fusion.3
  171.7 2.6 dynamic-slice_add_fusion
  174.3 1.7 collective-permute-start.12
  175.9 1.5 collective-permute-start.11
  177.4 10.6 %attention_back.3 = (bf16[1536,2048]{1,0:T(8,128)(2,1)}, bf16[1,512,512]{2,1,0:T(8,128)(2,1)}, f32[512,128]{1,0:T(8,128)}) custom-call(s32[1]{0:T(128)S(6)} %xor.15.refs_0_, bf16[4,512,512]{2,1,0:T(8,128)(2,1)} %get-tuple-element.186.refs_1_, f32[4,8,512]{2,1,0:T(8,128)} %get-tuple-element.187.refs_2_, bf16[4,512,512]{2,1,0:T(8,128)(2,1)} %get-tuple-element.188.refs_3_, ...), custom_call_target="tpu_custom_call" | custom-call | flops 10000000000 | bytes 1048576 | tf_op jit(solution)/shard_map/attention_back/pallas_call | solution.py:720
  188.8 1.5 add_add_fusion.2
  191.1 1.8 add_add_fusion
  192.9 2.7 collective-permute-start.14
  195.7 1.5 collective-permute-start.13
  197.7 19.2 %attention_back.4 = (bf16[1536,2048]{1,0:T(8,128)(2,1)}, bf16[2,512,512]{2,1,0:T(8,128)(2,1)}, f32[512,128]{1,0:T(8,128)}) custom-call(s32[2]{0:T(128)} %pad_add_fusion.refs_0_, bf16[4,512,512]{2,1,0:T(8,128)(2,1)} %get-tuple-element.186.refs_1_, f32[4,8,512]{2,1,0:T(8,128)} %get-tuple-element.187.refs_2_, ...), custom_call_target="tpu_custom_call", output_to_operand_aliasing={{0}: (14, {})} | custom-call | flops 20000000000 | bytes 1048576 | tf_op jit(solution)/shard_map/attention_back/pallas_call | solution.py:720
  217.2 1.5 collective-permute-start.17
  218.8 1.6 collective-permute-start.15
  220.5 10.4 %attention_back.5 = (bf16[1536,2048]{1,0:T(8,128)(2,1)}, bf16[1,512,512]{2,1,0:T(8,128)(2,1)}, f32[512,128]{1,0:T(8,128)}) custom-call(s32[1]{0:T(128)S(6)} %xor.17.refs_0_, bf16[4,512,512]{2,1,0:T(8,128)(2,1)} %get-tuple-element.186.refs_1_, f32[4,8,512]{2,1,0:T(8,128)} %get-tuple-element.187.refs_2_, ...), custom_call_target="tpu_custom_call", output_to_operand_aliasing={{0}: (14, {})} | custom-call | flops 10000000000 | bytes 1048576 | tf_op jit(solution)/shard_map/attention_back/pallas_call | solution.py:720
  231.1 1.6 collective-permute-start.20
  233.0 1.7 collective-permute-done.19
  235.5 6.4 %late_weights.2 = bf16[512,1152]{1,0:T(8,128)(2,1)} custom-call(s32[1]{0:T(128)S(6)} %sub.100.side_ref.refs_0_, bf16[512,2048]{1,0:T(8,128)(2,1)} %get-tuple-element.194.refs_12_.refs_1_, bf16[1536,2048]{1,0:T(8,128)(2,1)} %get-tuple-element.220.refs_2_, bf16[512,2048]{1,0:T(8,128)(2,1)} %get-tuple-element.158.refs_13_.refs_3_, ...), custom_call_target="tpu_custom_call" | custom-call | flops 4000000000 | bytes 1048576 | tf_op jit(solution)/shard_map/late_weights/pallas_call | solution.py:967
  243.6 1.2 constant_dynamic-slice_fusion.4
  245.3 1.5 collective-permute-start.30
  246.8 6.5 %late_weights.3 = bf16[512,1152]{1,0:T(8,128)(2,1)} custom-call(s32[1]{0:T(128)} %bitcast.side_ref.refs_0_, bf16[512,2048]{1,0:T(8,128)(2,1)} %get-tuple-element.194.refs_12_.refs_1_, bf16[1536,2048]{1,0:T(8,128)(2,1)} %get-tuple-element.220.refs_2_, bf16[512,2048]{1,0:T(8,128)(2,1)} %get-tuple-element.158.refs_13_.refs_3_, ...), custom_call_target="tpu_custom_call" | custom-call | flops 4000000000 | bytes 1048576 | tf_op jit(solution)/shard_map/late_weights/pallas_call | solution.py:967
  253.3 1.4 dynamic-slice_add_fusion.1
  254.7 1.0 collective-permute-start.23
  255.7 0.9 pad_maximum_fusion.14
  256.7 2.1 collective-permute-start.33
  259.3 1.1 constant_dynamic-update-slice_fusion.1
  260.6 2.4 maximum_convert_fusion
  263.0 1.7 collective-permute-done.23
  264.7 1.3 add_add_fusion.1
  266.9 3.5 %collective-permute-done.33 = bf16[128,1024]{1,0:T(8,128)(2,1)S(1)} collective-permute-done((bf16[128,1024]{1,0:T(8,128)(2,1)S(1)}, bf16[128,1024]{1,0:T(8,128)(2,1)S(1)}, u32[]{:S(2)}, u32[]{:S(2)}) %collective-permute-start.33) | collective-permute-done | bytes 262176 | tf_op jit(solution)/shard_map/ppermute | solution.py:773
  270.5 0.9 collective-permute-done.32
  271.6 1.2 collective-permute-done.24
  274.8 3.3 collective-permute-done.25
  278.2 5.7 %collective-permute-done.34 = bf16[128,2048]{1,0:T(8,128)(2,1)S(1)} collective-permute-done((bf16[128,2048]{1,0:T(8,128)(2,1)S(1)}, bf16[128,2048]{1,0:T(8,128)(2,1)S(1)}, u32[]{:S(2)}, u32[]{:S(2)}) %collective-permute-start.34) | collective-permute-done | bytes 524320 | tf_op jit(solution)/shard_map/ppermute | solution.py:773
  284.5 3.0 collective-permute-start.26
  287.5 4.4 %collective-permute-done.26 = bf16[64,1152]{1,0:T(8,128)(2,1)S(1)} collective-permute-done((bf16[64,1152]{1,0:T(8,128)(2,1)S(1)}, bf16[64,1152]{1,0:T(8,128)(2,1)S(1)}, u32[]{:S(2)}, u32[]{:S(2)}) %collective-permute-start.26) | collective-permute-done | bytes 147488 | tf_op jit(solution)/shard_map/ppermute | solution.py:773
  291.9 1.5 collective-permute-start.27
  293.5 4.3 %collective-permute-done.27 = bf16[64,1152]{1,0:T(8,128)(2,1)S(1)} collective-permute-done((bf16[64,1152]{1,0:T(8,128)(2,1)S(1)}, bf16[64,1152]{1,0:T(8,128)(2,1)S(1)}, u32[]{:S(2)}, u32[]{:S(2)}) %collective-permute-start.27) | collective-permute-done | bytes 147488 | tf_op jit(solution)/shard_map/ppermute | solution.py:773
  298.4 1.7 collective-permute-start.38
  300.1 2.0 collective-permute-done.35.refs_2_
  302.6 2.0 collective-permute-done.28
  304.6 0.9 pad_maximum_fusion.6.refs_1_
  305.5 1.4 collective-permute-start.29
  306.9 1.6 collective-permute-done.38.refs_2_
  311.5 3.6 %unpack.4 = (f32[512,1536]{1,0:T(8,128)}, f32[512,512]{1,0:T(8,128)}) custom-call(s32[3]{0:T(128)} %pad_add_fusion.3.refs_0_, bf16[256,1024]{1,0:T(8,128)(2,1)} %pad_maximum_fusion.11.refs_1_, bf16[256,1024]{1,0:T(8,128)(2,1)} %collective-permute-done.38.refs_2_, bf16[256,1024]{1,0:T(8,128)(2,1)} %collective-permute-done.39.refs_3_, ...), custom_call_target="tpu_custom_call" | custom-call | flops 100000000 | bytes 1048576 | tf_op jit(solution)/shard_map/unpack/pallas_call | solution.py:1127
  315.2 5.7 %unpack.3 = (f32[512,2048]{1,0:T(8,128)}, f32[2048,512]{1,0:T(8,128)}) custom-call(s32[3]{0:T(128)} %get-tuple-element.314.refs_0_, bf16[256,2048]{1,0:T(8,128)(2,1)} %copy-done.2, bf16[256,2048]{1,0:T(8,128)(2,1)} %collective-permute-done.35.refs_2_, bf16[256,2048]{1,0:T(8,128)(2,1)} %collective-permute-done.36.refs_3_, ...), custom_call_target="tpu_custom_call" | custom-call | flops 100000000 | bytes 1048576 | tf_op jit(solution)/shard_map/unpack/pallas_call | solution.py:1127
  322.2 1.5 slice_bitcast_fusion
  324.9 4.5 %unpack.5 = (f32[512,1536]{1,0:T(8,128)}, f32[512,512]{1,0:T(8,128)}, f32[64,512]{1,0:T(8,128)}, f32[3,512]{1,0:T(4,128)}) custom-call(s32[3]{0:T(128)} %get-tuple-element.313.refs_0_, bf16[256,1152]{1,0:T(8,128)(2,1)} %pad_maximum_fusion.6.refs_1_, bf16[256,1152]{1,0:T(8,128)(2,1)} %collective-permute-done.29.refs_2_, bf16[256,1152]{1,0:T(8,128)(2,1)} %copy-done.25, ...), custom_call_target="tpu_custom_call" | custom-call | flops 60000002048 | bytes 1048576 | tf_op jit(solution)/shard_map/unpack/pallas_call | solution.py:1127
  329.4 1.4 fusion.4
  (157 shorter events, 23.7 us)
Async XLA Ops:
  3.6 5.1 %copy-start.22 = (bf16[512]{0:T(512)(128)(2,1)S(1)}, bf16[512]{0:T(512)(128)(2,1)}, u32[]{:S(2)}) copy-start(bf16[512]{0:T(512)(128)(2,1)} %param.20) | copy-start | bytes 3076
  3.6 5.0 %copy-start.23 = (bf16[512]{0:T(512)(128)(2,1)S(1)}, bf16[512]{0:T(512)(128)(2,1)}, u32[]{:S(2)}) copy-start(bf16[512]{0:T(512)(128)(2,1)} %param.23) | copy-start | bytes 3076
  3.7 5.0 %copy-start.24 = (bf16[512]{0:T(512)(128)(2,1)S(1)}, bf16[512]{0:T(512)(128)(2,1)}, u32[]{:S(2)}) copy-start(bf16[512]{0:T(512)(128)(2,1)} %param.26) | copy-start | bytes 3076
  3.7 5.1 %copy-start.8 = (bf16[512,2048]{1,0:T(8,128)(2,1)S(1)}, bf16[512,2048]{1,0:T(8,128)(2,1)}, u32[]{:S(2)}) copy-start(bf16[512,2048]{1,0:T(8,128)(2,1)} %refs_6_.1) | copy-start | bytes 6291460
  5.6 14.9 %collective-permute-start = (bf16[1,528,512]{2,1,0:T(8,128)(2,1)}, bf16[1,528,512]{2,1,0:T(8,128)(2,1)}, u32[]{:S(2)}, u32[]{:S(2)}) collective-permute-start(bf16[1,528,512]{2,1,0:T(8,128)(2,1)} %get-tuple-element.142), channel_id=1, source_target_pairs={{0,8},{8,0},{16,24},{24,16},{1,9},{9,1},{17,25},{25,17},{2,10},{10... | collective-permute-start | bytes 1622024 | tf_op jit(solution)/shard_map/ppermute | solution.py:748
  6.0 16.0 %collective-permute-start.1 = (bf16[1,528,512]{2,1,0:T(8,128)(2,1)}, bf16[1,528,512]{2,1,0:T(8,128)(2,1)}, u32[]{:S(2)}, u32[]{:S(2)}) collective-permute-start(bf16[1,528,512]{2,1,0:T(8,128)(2,1)} %get-tuple-element.143), channel_id=1, source_target_pairs={{0,16},{8,24},{16,0},{24,8},{1,17},{9,25},{17,1},{25,9},{2,18},{10... | collective-permute-start | bytes 1622024 | tf_op jit(solution)/shard_map/ppermute | solution.py:748
  8.5 24.7 %collective-permute-start.2 = (bf16[1,528,512]{2,1,0:T(8,128)(2,1)}, bf16[1,528,512]{2,1,0:T(8,128)(2,1)}, u32[]{:S(2)}, u32[]{:S(2)}) collective-permute-start(bf16[1,528,512]{2,1,0:T(8,128)(2,1)} %pad_maximum_fusion.9), channel_id=1, source_target_pairs={{0,24},{8,16},{16,8},{24,0},{1,25},{9,17},{17,9},{25,1},{2,26},{10... | collective-permute-start | bytes 1622024 | tf_op jit(solution)/shard_map/ppermute | solution.py:748
  15.5 17.7 %copy-start.9 = (bf16[4,1,512,512]{3,2,1,0:T(8,128)(2,1)S(1)}, bf16[4,1,512,512]{3,2,1,0:T(8,128)(2,1)}, u32[]{:S(2)}) copy-start(bf16[4,1,512,512]{3,2,1,0:T(8,128)(2,1)} %param.30) | copy-start | bytes 6291460
  17.7 15.6 %copy-start.21 = (bf16[4,1,64,512]{3,2,1,0:T(8,128)(2,1)S(1)}, bf16[4,1,64,512]{3,2,1,0:T(8,128)(2,1)}, u32[]{:S(2)}) copy-start(bf16[4,1,64,512]{3,2,1,0:T(8,128)(2,1)} %param.31) | copy-start | bytes 786436
  33.5 67.5 %collective-permute-start.3 = (bf16[1,576,512]{2,1,0:T(8,128)(2,1)S(1)}, bf16[1,576,512]{2,1,0:T(8,128)(2,1)}, u32[]{:S(2)}, u32[]{:S(2)}) collective-permute-start(bf16[1,576,512]{2,1,0:T(8,128)(2,1)S(1)} %pad_maximum_fusion.3), channel_id=1, source_target_pairs={{0,8},{8,0},{16,24},{24,16},{1,9},{9,1},{17,25},{25,17},{2,10},{10... | collective-permute-start | bytes 1769480 | tf_op jit(solution)/shard_map/ppermute | solution.py:748
  33.7 67.4 %collective-permute-start.4 = (bf16[1,576,512]{2,1,0:T(8,128)(2,1)S(1)}, bf16[1,576,512]{2,1,0:T(8,128)(2,1)}, u32[]{:S(2)}, u32[]{:S(2)}) collective-permute-start(bf16[1,576,512]{2,1,0:T(8,128)(2,1)S(1)} %pad_maximum_fusion.4), channel_id=1, source_target_pairs={{0,16},{8,24},{16,0},{24,8},{1,17},{9,25},{17,1},{25,9},{2,18},{10... | collective-permute-start | bytes 1769480 | tf_op jit(solution)/shard_map/ppermute | solution.py:748
  35.3 65.7 %collective-permute-start.5 = (bf16[1,576,512]{2,1,0:T(8,128)(2,1)S(1)}, bf16[1,576,512]{2,1,0:T(8,128)(2,1)}, u32[]{:S(2)}, u32[]{:S(2)}) collective-permute-start(bf16[1,576,512]{2,1,0:T(8,128)(2,1)S(1)} %pad_maximum_fusion.5), channel_id=1, source_target_pairs={{0,24},{8,16},{16,8},{24,0},{1,25},{9,17},{17,9},{25,1},{2,26},{10... | collective-permute-start | bytes 1769480 | tf_op jit(solution)/shard_map/ppermute | solution.py:748
  99.0 48.1 %collective-permute-start.6 = (bf16[1,576,512]{2,1,0:T(8,128)(2,1)}, bf16[1,576,512]{2,1,0:T(8,128)(2,1)S(1)}, u32[]{:S(2)}, u32[]{:S(2)}) collective-permute-start(bf16[1,576,512]{2,1,0:T(8,128)(2,1)} %get-tuple-element.291), channel_id=1, source_target_pairs={{0,8},{8,0},{16,24},{24,16},{1,9},{9,1},{17,25},{25,17},{2,10},{10... | collective-permute-start | bytes 1769480 | tf_op jit(solution)/shard_map/ppermute | solution.py:748
  99.4 47.7 %collective-permute-start.7 = (bf16[1,576,512]{2,1,0:T(8,128)(2,1)}, bf16[1,576,512]{2,1,0:T(8,128)(2,1)S(1)}, u32[]{:S(2)}, u32[]{:S(2)}) collective-permute-start(bf16[1,576,512]{2,1,0:T(8,128)(2,1)} %get-tuple-element.290), channel_id=1, source_target_pairs={{0,16},{8,24},{16,0},{24,8},{1,17},{9,25},{17,1},{25,9},{2,18},{10... | collective-permute-start | bytes 1769480 | tf_op jit(solution)/shard_map/ppermute | solution.py:748
  101.0 46.1 %collective-permute-start.8 = (bf16[1,576,512]{2,1,0:T(8,128)(2,1)}, bf16[1,576,512]{2,1,0:T(8,128)(2,1)S(1)}, u32[]{:S(2)}, u32[]{:S(2)}) collective-permute-start(bf16[1,576,512]{2,1,0:T(8,128)(2,1)} %get-tuple-element.289), channel_id=1, source_target_pairs={{0,24},{8,16},{16,8},{24,0},{1,25},{9,17},{17,9},{25,1},{2,26},{10... | collective-permute-start | bytes 1769480 | tf_op jit(solution)/shard_map/ppermute | solution.py:748
  147.1 10.9 %copy-start.12 = (bf16[1,576,512]{2,1,0:T(8,128)(2,1)}, bf16[1,576,512]{2,1,0:T(8,128)(2,1)S(1)}, u32[]{:S(2)}) copy-start(bf16[1,576,512]{2,1,0:T(8,128)(2,1)S(1)} %collective-permute-done.6) | copy-start | bytes 1769476
  147.1 10.9 %copy-start.14 = (bf16[1,576,512]{2,1,0:T(8,128)(2,1)}, bf16[1,576,512]{2,1,0:T(8,128)(2,1)S(1)}, u32[]{:S(2)}) copy-start(bf16[1,576,512]{2,1,0:T(8,128)(2,1)S(1)} %collective-permute-done.7) | copy-start | bytes 1769476
  147.2 10.9 %copy-start.16 = (bf16[1,576,512]{2,1,0:T(8,128)(2,1)}, bf16[1,576,512]{2,1,0:T(8,128)(2,1)S(1)}, u32[]{:S(2)}) copy-start(bf16[1,576,512]{2,1,0:T(8,128)(2,1)S(1)} %collective-permute-done.8) | copy-start | bytes 1769476
  158.0 13.6 %collective-permute-start.9 = (bf16[512,2048]{1,0:T(8,128)(2,1)}, bf16[512,2048]{1,0:T(8,128)(2,1)S(1)}, u32[]{:S(2)}, u32[]{:S(2)}) collective-permute-start(bf16[512,2048]{1,0:T(8,128)(2,1)} %get-tuple-element.178), channel_id=1, source_target_pairs={{0,8},{1,9},{2,10},{3,11},{4,12},{5,13},{6,14},{7,15},{8,0},{9,1},... | collective-permute-start | bytes 6291464 | tf_op jit(solution)/shard_map/ppermute | solution.py:773
  158.5 11.0 %collective-permute-start.10 = (bf16[512,1024]{1,0:T(8,128)(2,1)}, bf16[512,1024]{1,0:T(8,128)(2,1)}, u32[]{:S(2)}, u32[]{:S(2)}) collective-permute-start(bf16[512,1024]{1,0:T(8,128)(2,1)} %get-tuple-element.179), channel_id=1, source_target_pairs={{0,8},{1,9},{2,10},{3,11},{4,12},{5,13},{6,14},{7,15},{8,0},{9,1},... | collective-permute-start | bytes 3145736 | tf_op jit(solution)/shard_map/ppermute | solution.py:773
  174.3 14.6 %collective-permute-start.12 = (bf16[256,1024]{1,0:T(8,128)(2,1)}, bf16[256,1024]{1,0:T(8,128)(2,1)}, u32[]{:S(2)}, u32[]{:S(2)}) collective-permute-start(bf16[256,1024]{1,0:T(8,128)(2,1)} %dynamic-slice_add_fusion.3), channel_id=1, source_target_pairs={{0,2},{1,3},{2,0},{3,1},{4,6},{5,7},{6,4},{7,5},{8,10},{9,11},{10,... | collective-permute-start | bytes 1572872 | tf_op jit(solution)/shard_map/ppermute | solution.py:773
  175.9 15.2 %collective-permute-start.11 = (bf16[256,2048]{1,0:T(8,128)(2,1)}, bf16[256,2048]{1,0:T(8,128)(2,1)}, u32[]{:S(2)}, u32[]{:S(2)}) collective-permute-start(bf16[256,2048]{1,0:T(8,128)(2,1)} %dynamic-slice_add_fusion), channel_id=1, source_target_pairs={{0,1},{1,0},{2,3},{3,2},{4,5},{5,4},{6,7},{7,6},{8,24},{9,25},{10,... | collective-permute-start | bytes 3145736 | tf_op jit(solution)/shard_map/ppermute | solution.py:773
  177.4 11.4 %copy-start.10 = (bf16[512,1024]{1,0:T(8,128)(2,1)S(1)}, bf16[512,1024]{1,0:T(8,128)(2,1)}, u32[]{:S(2)}) copy-start(bf16[512,1024]{1,0:T(8,128)(2,1)} %get-tuple-element.182) | copy-start | bytes 3145732
  188.0 3.1 copy-start.5
  192.9 24.0 %collective-permute-start.14 = (bf16[128,1024]{1,0:T(8,128)(2,1)S(1)}, bf16[128,1024]{1,0:T(8,128)(2,1)S(1)}, u32[]{:S(2)}, u32[]{:S(2)}) collective-permute-start(bf16[128,1024]{1,0:T(8,128)(2,1)S(1)} %constant_dynamic-slice_fusion.14), channel_id=1, source_target_pairs={{0,4},{1,5},{2,6},{3,7},{4,0},{5,1},{6,2},{7,3},{8,12},{9,13},{10,... | collective-permute-start | bytes 786440 | tf_op jit(solution)/shard_map/ppermute | solution.py:773
  195.7 21.4 %collective-permute-start.13 = (bf16[128,2048]{1,0:T(8,128)(2,1)S(1)}, bf16[128,2048]{1,0:T(8,128)(2,1)S(1)}, u32[]{:S(2)}, u32[]{:S(2)}) collective-permute-start(bf16[128,2048]{1,0:T(8,128)(2,1)S(1)} %constant_dynamic-slice_fusion.15), channel_id=1, source_target_pairs={{0,16},{1,17},{2,18},{3,19},{4,20},{5,21},{6,22},{7,23},{8,9},{9,8... | collective-permute-start | bytes 1572872 | tf_op jit(solution)/shard_map/ppermute | solution.py:773
  197.2 23.2 %collective-permute-start.16 = (bf16[1,512,512]{2,1,0:T(8,128)(2,1)}, bf16[1,512,512]{2,1,0:T(8,128)(2,1)}, u32[]{:S(2)}, u32[]{:S(2)}) collective-permute-start(bf16[1,512,512]{2,1,0:T(8,128)(2,1)} %get-tuple-element.209), channel_id=1, source_target_pairs={{0,16},{8,24},{16,0},{24,8},{1,17},{9,25},{17,1},{25,9},{2,18},{10... | collective-permute-start | bytes 1572872 | tf_op jit(solution)/shard_map/ppermute | solution.py:748
  197.7 19.2 %copy-start.7 = (bf16[256,1024]{1,0:T(8,128)(2,1)S(1)}, bf16[256,1024]{1,0:T(8,128)(2,1)}, u32[]{:S(2)}) copy-start(bf16[256,1024]{1,0:T(8,128)(2,1)} %copy-done.6) | copy-start | bytes 1572868
  216.9 3.5 %copy-start.11 = (bf16[2,512,512]{2,1,0:T(8,128)(2,1)S(1)}, bf16[2,512,512]{2,1,0:T(8,128)(2,1)}, u32[]{:S(2)}) copy-start(bf16[2,512,512]{2,1,0:T(8,128)(2,1)} %get-tuple-element.218) | copy-start | bytes 3145732
  217.2 13.7 %collective-permute-start.17 = (bf16[64,1024]{1,0:T(8,128)(2,1)S(1)}, bf16[64,1024]{1,0:T(8,128)(2,1)S(1)}, u32[]{:S(2)}, u32[]{:S(2)}) collective-permute-start(bf16[64,1024]{1,0:T(8,128)(2,1)S(1)} %constant_dynamic-slice_fusion.12), channel_id=1, source_target_pairs={{0,1},{1,0},{2,3},{3,2},{4,5},{5,4},{6,7},{7,6},{8,24},{9,25},{10,... | collective-permute-start | bytes 393224 | tf_op jit(solution)/shard_map/ppermute | solution.py:773
  218.8 12.2 %collective-permute-start.15 = (bf16[64,2048]{1,0:T(8,128)(2,1)S(1)}, bf16[64,2048]{1,0:T(8,128)(2,1)S(1)}, u32[]{:S(2)}, u32[]{:S(2)}) collective-permute-start(bf16[64,2048]{1,0:T(8,128)(2,1)S(1)} %constant_dynamic-slice_fusion.13), channel_id=1, source_target_pairs={{0,2},{1,3},{2,0},{3,1},{4,6},{5,7},{6,4},{7,5},{8,10},{9,11},{10,... | collective-permute-start | bytes 786440 | tf_op jit(solution)/shard_map/ppermute | solution.py:773
  220.5 14.2 %collective-permute-start.19 = (bf16[1,512,512]{2,1,0:T(8,128)(2,1)S(1)}, bf16[1,512,512]{2,1,0:T(8,128)(2,1)S(1)}, u32[]{:S(2)}, u32[]{:S(2)}) collective-permute-start(bf16[1,512,512]{2,1,0:T(8,128)(2,1)S(1)} %get-tuple-element.303), channel_id=1, source_target_pairs={{0,24},{8,16},{16,8},{24,0},{1,25},{9,17},{17,9},{25,1},{2,26},{10... | collective-permute-start | bytes 1572872 | tf_op jit(solution)/shard_map/ppermute | solution.py:748
  231.1 10.8 %collective-permute-start.20 = (bf16[64,1024]{1,0:T(8,128)(2,1)S(1)}, bf16[64,1024]{1,0:T(8,128)(2,1)S(1)}, u32[]{:S(2)}, u32[]{:S(2)}) collective-permute-start(bf16[64,1024]{1,0:T(8,128)(2,1)S(1)} %dynamic-slice_add_fusion.8), channel_id=1, source_target_pairs={{0,16},{1,17},{2,18},{3,19},{4,20},{5,21},{6,22},{7,23},{8,9},{9,8... | collective-permute-start | bytes 393224 | tf_op jit(solution)/shard_map/ppermute | solution.py:773
  232.7 10.0 %collective-permute-start.18 = (bf16[32,2048]{1,0:T(8,128)(2,1)S(1)}, bf16[32,2048]{1,0:T(8,128)(2,1)S(1)}, u32[]{:S(2)}, u32[]{:S(2)}) collective-permute-start(bf16[32,2048]{1,0:T(8,128)(2,1)S(1)} %constant_dynamic-slice_fusion.11), channel_id=1, source_target_pairs={{0,4},{1,5},{2,6},{3,7},{4,0},{5,1},{6,2},{7,3},{8,12},{9,13},{10,... | collective-permute-start | bytes 393224 | tf_op jit(solution)/shard_map/ppermute | solution.py:773
  235.5 7.8 %copy-start.13 = (bf16[1,576,512]{2,1,0:T(8,128)(2,1)S(1)}, bf16[1,576,512]{2,1,0:T(8,128)(2,1)}, u32[]{:S(2)}) copy-start(bf16[1,576,512]{2,1,0:T(8,128)(2,1)} %copy-done.12) | copy-start | bytes 1769476
  235.5 7.8 %copy-start.15 = (bf16[1,576,512]{2,1,0:T(8,128)(2,1)S(1)}, bf16[1,576,512]{2,1,0:T(8,128)(2,1)}, u32[]{:S(2)}) copy-start(bf16[1,576,512]{2,1,0:T(8,128)(2,1)} %copy-done.14) | copy-start | bytes 1769476
  235.5 7.8 %copy-start.17 = (bf16[1,576,512]{2,1,0:T(8,128)(2,1)S(1)}, bf16[1,576,512]{2,1,0:T(8,128)(2,1)}, u32[]{:S(2)}) copy-start(bf16[1,576,512]{2,1,0:T(8,128)(2,1)} %copy-done.16) | copy-start | bytes 1769476
  242.7 10.6 %collective-permute-start.22 = (bf16[512,1152]{1,0:T(8,128)(2,1)}, bf16[512,1152]{1,0:T(8,128)(2,1)}, u32[]{:S(2)}, u32[]{:S(2)}) collective-permute-start(bf16[512,1152]{1,0:T(8,128)(2,1)} %late_weights.2), channel_id=1, source_target_pairs={{0,8},{1,9},{2,10},{3,11},{4,12},{5,13},{6,14},{7,15},{8,0},{9,1},... | collective-permute-start | bytes 3538952 | tf_op jit(solution)/shard_map/ppermute | solution.py:773
  242.9 3.9 %collective-permute-start.21 = (bf16[1,512,512]{2,1,0:T(8,128)(2,1)}, bf16[1,512,512]{2,1,0:T(8,128)(2,1)S(1)}, u32[]{:S(2)}, u32[]{:S(2)}) collective-permute-start(bf16[1,512,512]{2,1,0:T(8,128)(2,1)} %get-tuple-element.230), channel_id=1, source_target_pairs={{0,8},{8,0},{16,24},{24,16},{1,9},{9,1},{17,25},{25,17},{2,10},{10... | collective-permute-start | bytes 1572872 | tf_op jit(solution)/shard_map/ppermute | solution.py:748
  244.7 11.0 %collective-permute-start.31 = (bf16[64,1024]{1,0:T(8,128)(2,1)}, bf16[64,1024]{1,0:T(8,128)(2,1)S(1)}, u32[]{:S(2)}, u32[]{:S(2)}) collective-permute-start(bf16[64,1024]{1,0:T(8,128)(2,1)} %add.339), channel_id=1, source_target_pairs={{0,1},{1,0},{2,3},{3,2},{4,5},{5,4},{6,7},{7,6},{8,24},{9,25},{10,... | collective-permute-start | bytes 393224 | tf_op jit(solution)/shard_map/ppermute | solution.py:773
  245.3 11.4 %collective-permute-start.30 = (bf16[32,2048]{1,0:T(8,128)(2,1)S(1)}, bf16[32,2048]{1,0:T(8,128)(2,1)S(1)}, u32[]{:S(2)}, u32[]{:S(2)}) collective-permute-start(bf16[32,2048]{1,0:T(8,128)(2,1)S(1)} %dynamic-slice_add_fusion.9), channel_id=1, source_target_pairs={{0,4},{1,5},{2,6},{3,7},{4,0},{5,1},{6,2},{7,3},{8,12},{9,13},{10,... | collective-permute-start | bytes 393224 | tf_op jit(solution)/shard_map/ppermute | solution.py:773
  254.7 5.7 %copy-start.19 = (bf16[1,512,512]{2,1,0:T(8,128)(2,1)S(1)}, bf16[1,512,512]{2,1,0:T(8,128)(2,1)}, u32[]{:S(2)}) copy-start(bf16[1,512,512]{2,1,0:T(8,128)(2,1)} %copy-done.18) | copy-start | bytes 1572868
  254.7 9.9 %collective-permute-start.23 = (bf16[256,1152]{1,0:T(8,128)(2,1)S(1)}, bf16[256,1152]{1,0:T(8,128)(2,1)S(1)}, u32[]{:S(2)}, u32[]{:S(2)}) collective-permute-start(bf16[256,1152]{1,0:T(8,128)(2,1)S(1)} %dynamic-slice_add_fusion.1), channel_id=1, source_target_pairs={{0,1},{1,0},{2,3},{3,2},{4,5},{5,4},{6,7},{7,6},{8,24},{9,25},{10,... | collective-permute-start | bytes 1769480 | tf_op jit(solution)/shard_map/ppermute | solution.py:773
  256.7 13.8 %collective-permute-start.33 = (bf16[128,1024]{1,0:T(8,128)(2,1)S(1)}, bf16[128,1024]{1,0:T(8,128)(2,1)S(1)}, u32[]{:S(2)}, u32[]{:S(2)}) collective-permute-start(bf16[128,1024]{1,0:T(8,128)(2,1)S(1)} %pad_maximum_fusion.14), channel_id=1, source_target_pairs={{0,4},{1,5},{2,6},{3,7},{4,0},{5,1},{6,2},{7,3},{8,12},{9,13},{10,... | collective-permute-start | bytes 786440 | tf_op jit(solution)/shard_map/ppermute | solution.py:773
  258.8 12.6 %collective-permute-start.32 = (bf16[64,2048]{1,0:T(8,128)(2,1)S(1)}, bf16[64,2048]{1,0:T(8,128)(2,1)S(1)}, u32[]{:S(2)}, u32[]{:S(2)}) collective-permute-start(bf16[64,2048]{1,0:T(8,128)(2,1)S(1)} %pad_maximum_fusion.13), channel_id=1, source_target_pairs={{0,2},{1,3},{2,0},{3,1},{4,6},{5,7},{6,4},{7,5},{8,10},{9,11},{10,... | collective-permute-start | bytes 786440 | tf_op jit(solution)/shard_map/ppermute | solution.py:773
  260.6 4.1 %copy-start.1 = (bf16[512,1152]{1,0:T(8,128)(2,1)S(1)}, bf16[512,1152]{1,0:T(8,128)(2,1)}, u32[]{:S(2)}) copy-start(bf16[512,1152]{1,0:T(8,128)(2,1)} %late_weights.3) | copy-start | bytes 3538948
  263.0 3.7 %copy-start.3 = (bf16[1,576,512]{2,1,0:T(8,128)(2,1)S(1)}, bf16[1,576,512]{2,1,0:T(8,128)(2,1)}, u32[]{:S(2)}) copy-start(bf16[1,576,512]{2,1,0:T(8,128)(2,1)} %get-tuple-element.286) | copy-start | bytes 1769476
  263.0 3.7 %copy-start.4 = (bf16[1,576,512]{2,1,0:T(8,128)(2,1)S(1)}, bf16[1,576,512]{2,1,0:T(8,128)(2,1)}, u32[]{:S(2)}) copy-start(bf16[1,576,512]{2,1,0:T(8,128)(2,1)} %get-tuple-element.287) | copy-start | bytes 1769476
  266.0 6.8 %collective-permute-start.24 = (bf16[128,1152]{1,0:T(8,128)(2,1)S(1)}, bf16[128,1152]{1,0:T(8,128)(2,1)S(1)}, u32[]{:S(2)}, u32[]{:S(2)}) collective-permute-start(bf16[128,1152]{1,0:T(8,128)(2,1)S(1)} %constant_dynamic-slice_fusion.6), channel_id=1, source_target_pairs={{0,16},{1,17},{2,18},{3,19},{4,20},{5,21},{6,22},{7,23},{8,9},{9,8... | collective-permute-start | bytes 884744 | tf_op jit(solution)/shard_map/ppermute | solution.py:773
  272.9 5.2 %collective-permute-start.25 = (bf16[64,1152]{1,0:T(8,128)(2,1)S(1)}, bf16[64,1152]{1,0:T(8,128)(2,1)S(1)}, u32[]{:S(2)}, u32[]{:S(2)}) collective-permute-start(bf16[64,1152]{1,0:T(8,128)(2,1)S(1)} %constant_dynamic-slice_fusion), channel_id=1, source_target_pairs={{0,2},{1,3},{2,0},{3,1},{4,6},{5,7},{6,4},{7,5},{8,10},{9,11},{10,... | collective-permute-start | bytes 442376 | tf_op jit(solution)/shard_map/ppermute | solution.py:773
  274.3 9.6 %collective-permute-start.34 = (bf16[128,2048]{1,0:T(8,128)(2,1)S(1)}, bf16[128,2048]{1,0:T(8,128)(2,1)S(1)}, u32[]{:S(2)}, u32[]{:S(2)}) collective-permute-start(bf16[128,2048]{1,0:T(8,128)(2,1)S(1)} %pad_maximum_fusion.10), channel_id=1, source_target_pairs={{0,16},{1,17},{2,18},{3,19},{4,20},{5,21},{6,22},{7,23},{8,9},{9,8... | collective-permute-start | bytes 1572872 | tf_op jit(solution)/shard_map/ppermute | solution.py:773
  284.0 31.2 %copy-start.2 = (bf16[256,2048]{1,0:T(8,128)(2,1)}, bf16[256,2048]{1,0:T(8,128)(2,1)S(1)}, u32[]{:S(2)}) copy-start(bf16[256,2048]{1,0:T(8,128)(2,1)S(1)} %pad_maximum_fusion.2.refs_1_) | copy-start | bytes 3145732
  284.0 18.1 %collective-permute-start.35 = (bf16[256,2048]{1,0:T(8,128)(2,1)S(1)}, bf16[256,2048]{1,0:T(8,128)(2,1)}, u32[]{:S(2)}, u32[]{:S(2)}) collective-permute-start(bf16[256,2048]{1,0:T(8,128)(2,1)S(1)} %pad_maximum_fusion.2.refs_1_), channel_id=1, source_target_pairs={{0,1},{1,0},{2,3},{3,2},{4,5},{5,4},{6,7},{7,6},{8,24},{9,25},{10,... | collective-permute-start | bytes 3145736 | tf_op jit(solution)/shard_map/ppermute | solution.py:773
  284.5 7.4 %collective-permute-start.26 = (bf16[64,1152]{1,0:T(8,128)(2,1)S(1)}, bf16[64,1152]{1,0:T(8,128)(2,1)S(1)}, u32[]{:S(2)}, u32[]{:S(2)}) collective-permute-start(bf16[64,1152]{1,0:T(8,128)(2,1)S(1)} %dynamic-slice_add_fusion.7), channel_id=1, source_target_pairs={{0,4},{1,5},{2,6},{3,7},{4,0},{5,1},{6,2},{7,3},{8,12},{9,13},{10,... | collective-permute-start | bytes 442376 | tf_op jit(solution)/shard_map/ppermute | solution.py:773
  291.9 5.9 %collective-permute-start.27 = (bf16[64,1152]{1,0:T(8,128)(2,1)S(1)}, bf16[64,1152]{1,0:T(8,128)(2,1)S(1)}, u32[]{:S(2)}, u32[]{:S(2)}) collective-permute-start(bf16[64,1152]{1,0:T(8,128)(2,1)S(1)} %add.350), channel_id=1, source_target_pairs={{0,2},{1,3},{2,0},{3,1},{4,6},{5,7},{6,4},{7,5},{8,10},{9,11},{10,... | collective-permute-start | bytes 442376 | tf_op jit(solution)/shard_map/ppermute | solution.py:773
  297.8 6.8 %collective-permute-start.28 = (bf16[128,1152]{1,0:T(8,128)(2,1)S(1)}, bf16[128,1152]{1,0:T(8,128)(2,1)S(1)}, u32[]{:S(2)}, u32[]{:S(2)}) collective-permute-start(bf16[128,1152]{1,0:T(8,128)(2,1)S(1)} %pad_maximum_fusion.12), channel_id=1, source_target_pairs={{0,16},{1,17},{2,18},{3,19},{4,20},{5,21},{6,22},{7,23},{8,9},{9,8... | collective-permute-start | bytes 884744 | tf_op jit(solution)/shard_map/ppermute | solution.py:773
  298.4 10.1 %collective-permute-start.38 = (bf16[256,1024]{1,0:T(8,128)(2,1)}, bf16[256,1024]{1,0:T(8,128)(2,1)}, u32[]{:S(2)}, u32[]{:S(2)}) collective-permute-start(bf16[256,1024]{1,0:T(8,128)(2,1)} %pad_maximum_fusion.11.refs_1_), channel_id=1, source_target_pairs={{0,2},{1,3},{2,0},{3,1},{4,6},{5,7},{6,4},{7,5},{8,10},{9,11},{10,... | collective-permute-start | bytes 1572872 | tf_op jit(solution)/shard_map/ppermute | solution.py:773
  302.1 13.1 %collective-permute-start.36 = (bf16[256,2048]{1,0:T(8,128)(2,1)S(1)}, bf16[256,2048]{1,0:T(8,128)(2,1)}, u32[]{:S(2)}, u32[]{:S(2)}) collective-permute-start(bf16[256,2048]{1,0:T(8,128)(2,1)S(1)} %pad_maximum_fusion.2.refs_1_), channel_id=1, source_target_pairs={{0,8},{1,9},{2,10},{3,11},{4,12},{5,13},{6,14},{7,15},{8,0},{9,1},... | collective-permute-start | bytes 3145736 | tf_op jit(solution)/shard_map/ppermute | solution.py:773
  302.1 13.1 %collective-permute-start.37 = (bf16[256,2048]{1,0:T(8,128)(2,1)}, bf16[256,2048]{1,0:T(8,128)(2,1)}, u32[]{:S(2)}, u32[]{:S(2)}) collective-permute-start(bf16[256,2048]{1,0:T(8,128)(2,1)} %collective-permute-done.35.refs_2_), channel_id=1, source_target_pairs={{0,8},{1,9},{2,10},{3,11},{4,12},{5,13},{6,14},{7,15},{8,0},{9,1},... | collective-permute-start | bytes 3145736 | tf_op jit(solution)/shard_map/ppermute | solution.py:773
  305.5 15.4 %collective-permute-start.29 = (bf16[256,1152]{1,0:T(8,128)(2,1)}, bf16[256,1152]{1,0:T(8,128)(2,1)}, u32[]{:S(2)}, u32[]{:S(2)}) collective-permute-start(bf16[256,1152]{1,0:T(8,128)(2,1)} %pad_maximum_fusion.6.refs_1_), channel_id=1, source_target_pairs={{0,1},{1,0},{2,3},{3,2},{4,5},{5,4},{6,7},{7,6},{8,24},{9,25},{10,... | collective-permute-start | bytes 1769480 | tf_op jit(solution)/shard_map/ppermute | solution.py:773
  308.5 2.3 collective-permute-start.39
  308.5 3.0 collective-permute-start.40
  320.9 2.8 collective-permute-start.41
  321.1 2.9 collective-permute-start.42
  (6 other events, 8.4 us)

commit v3 on v2

--- a/solution.py
+++ b/solution.py
@@ -1075,8 +1075,9 @@
     gains_ref = None
     if kept:
         gains_ref, refs = refs[0], refs[1:]
-    outs = len(refs) // 2
-    out_refs, staged, sems = refs[:outs], refs[outs : 2 * outs], refs[2 * outs]
+    rows_out = gains_ref.shape[0] if kept else 1
+    outs = (len(refs) - rows_out) // 2
+    out_refs, staged, sems = refs[: outs + rows_out - 1], refs[outs + rows_out - 1 : -1], refs[-1]
     each = count // parts
     rows = own_refs[0].shape[0] // each
     height = rows * count
@@ -1106,9 +1107,11 @@
                 pltpu.make_async_copy(*copy).wait()
 
     if kept:
-        init_ref, total_ref = out_refs[outs - 2 :]
+        init_ref, total_refs = out_refs[outs - 2], out_refs[outs - 1 :]
         init_ref[...] = staged[outs - 2][...].T[: init_ref.shape[0], :]
-        total_ref[...] = staged[outs - 1][...].T[: total_ref.shape[0], :] / gains_ref[...]
+        totals = staged[outs - 1][...].T[: gains_ref.shape[0], :] / gains_ref[...]
+        for at, ref in enumerate(total_refs):
+            ref[...] = totals[at : at + 1, :]
 
 
 def unpacked(total, regions, shapes, slots=0, gains=None):
@@ -1122,8 +1125,9 @@
     inputs = [*own, *other]
     if kept:
         inputs.append(gains)
-        outs += [jax.ShapeDtypeStruct((rows, shapes[-1][0]), F32) for rows in (slots, gains.shape[0])]
-        specs += [vmem] * 2
+        rows = [slots] + [1] * gains.shape[0]
+        outs += [jax.ShapeDtypeStruct((height, shapes[-1][0]), F32) for height in rows]
+        specs += [vmem] * len(rows)
     return pl.pallas_call(
         lambda *refs: unpack_kernel(count, parts, regions, kept, *refs),
         in_specs=[pl.BlockSpec(memory_space=pltpu.SMEM)] + [vmem] * len(inputs),
@@ -1370,20 +1374,20 @@
         advance([late])
     if late.started is not None:
         late.finish()
-    grad_qkv, grad_ao, grad_init, gains = unpacked(
+    grad_qkv, grad_ao, grad_init, *gains = unpacked(
         late, late_regions, [triple, square, (width, 128), (width, 128)], slots, consts["gains"]
     )
     return (
         done[:, None, :seg],
         done[:, None, seg:],
         token_grads[:, None],
-        gains[0],
+        gains[0].reshape(width),
         grad_qkv,
         grad_ao,
-        gains[1],
+        gains[1].reshape(width),
         grad_in,
         grad_out,
-        gains[2],
+        gains[2].reshape(width),
         grad_write,
         grad_wo,
         grad_init,

time: 334 us -> 333 us (level)
  no operation moved by 1% of the time
where the time goes in v3:
time: 333 us; the launch traced here: 330 us
  Pallas kernels  194 us (58%)
  waiting for transfers between devices  48.2 us (14%)
  starting transfers between devices  38.2 us (11%)
  other arithmetic  23.7 us (7%)
  local copies, waits for them, and re-layouts  23.7 us (7%)
    pallas_call x1, Pallas kernels, forward_chain(): pl.pallas_call(lambda *refs: forward_kernel(sources, segs, *refs), grid_s...  60 us
    pallas_call x1, Pallas kernels, backward_chain(): pl.pallas_call(lambda *refs: chain_kernel(sources, segs, *refs), grid_spe...  46.1 us
    pallas_call x3, Pallas kernels, attention_back(): pl.pallas_call(lambda *refs: attention_kernel(alone, *refs), grid_spec=pl...  40.2 us
    ppermute x31, waiting for transfers between devices, phase_swap(): return lax.ppermute(value, ('section', 'dp'), route)  33.7 us
    ppermute x31, starting transfers between devices, phase_swap(): return lax.ppermute(value, ('section', 'dp'), route)  30.1 us
    pallas_call x2, Pallas kernels, early_weights(): pl.pallas_call(early_weights_kernel, grid_spec=pltpu.PrefetchScalarGridSp...  21.1 us
    unnamed x64, local copies, waits for them, and re-layouts  16.9 us
    ppermute x12, waiting for transfers between devices, swap_pairs(): return lax.ppermute(value, axis, [(i, i ^ mask) for i in range(size)])  14.5 us
  transfers between devices with their start and end apart: 43, of which 18 were waited for; matrix products, arithmetic and copies ran while one was open for 11% of the time, Pallas kernels for 54%

profile of v3, /device:TPU:0, one launch (start us, length us, event | category | flops | bytes accessed | tf_op | source)
XLA Modules:
  0.0 329.7 jit_solution(17528517145432409002)
XLA Ops:
  2.2 1.5 dynamic-slice_bitcast_fusion
  3.7 0.8 pad_maximum_fusion.9
  4.5 1.0 pad_maximum_fusion.7
  6.0 2.5 collective-permute-start.1
  8.7 2.5 copy.34
  11.2 2.7 copy.35
  14.0 1.6 copy.32
  15.5 2.2 copy.36
  17.7 2.1 copy.33
  20.4 1.5 collective-permute-done.1.refs_15_
  22.0 11.2 %collective-permute-done.2.refs_16_ = bf16[1,528,512]{2,1,0:T(8,128)(2,1)} collective-permute-done((bf16[1,528,512]{2,1,0:T(8,128)(2,1)}, bf16[1,528,512]{2,1,0:T(8,128)(2,1)}, u32[]{:S(2)}, u32[]{:S(2)}) %collective-permute-start.2) | collective-permute-done | bytes 540704 | tf_op jit(solution)/shard_map/ppermute | solution.py:748
  33.7 1.6 collective-permute-start.4
  36.1 60.0 %forward_chain.1 = (bf16[4,576,512]{2,1,0:T(8,128)(2,1)}, bf16[512,2048]{1,0:T(8,128)(2,1)}, bf16[4,512,64]{2,1,0:T(8,128)(2,1)}, bf16[4,512,512]{2,1,0:T(8,128)...) custom-call(s32[1]{0:T(128)} %bitcast.1.refs_0_, ...), custom_call_target="tpu_custom_call" | custom-call | flops 60000002048 | bytes 1048576 | tf_op jit(solution)/shard_map/forward_chain/pallas_call | solution.py:587
  96.1 2.9 constant_dynamic-slice_fusion.5
  99.4 1.6 collective-permute-start.7
  101.0 46.1 %backward_chain.1 = (bf16[4,512,64]{2,1,0:T(8,128)(2,1)}, bf16[1024,2048]{1,0:T(8,128)(2,1)}, bf16[4,1536,64]{2,1,0:T(8,128)(2,1)}, bf16[512,2048]{1,0:T(8,128)(...) custom-call(s32[1]{0:T(128)} %bitcast.1.refs_0_, ...), custom_call_target="tpu_custom_call" | custom-call | flops 44000002048 | bytes 1048576 | tf_op jit(solution)/shard_map/backward_chain/pallas_call | solution.py:669
  147.2 10.8 %early_weights.2 = (bf16[512,2048]{1,0:T(8,128)(2,1)}, bf16[512,1024]{1,0:T(8,128)(2,1)}) custom-call(s32[1]{0:T(128)S(6)} %sub.100.side_ref.refs_0_, bf16[512,2048]{1,0:T(8,128)(2,1)} %get-tuple-element.153.refs_14_.a2_ref, bf16[2048,2048]{1,0:T(8,128)(2,1)} %get-tuple-element.173.gu_ref, bf16[512,2048]{1,0:T(8,128)(2,1)} %get-tuple-element.174.bf_ref, ...), custom_call_target="tpu_custom_call" | custom-call | flops 8999999488 | bytes 1048576 | tf_op jit(solution)/shard_map/early_weights/pallas_call | solution.py:876
  159.2 10.2 %early_weights.3 = (bf16[512,2048]{1,0:T(8,128)(2,1)}, bf16[512,1024]{1,0:T(8,128)(2,1)}) custom-call(s32[1]{0:T(128)} %bitcast.side_ref.refs_0_, bf16[512,2048]{1,0:T(8,128)(2,1)} %get-tuple-element.153.refs_14_.a2_ref, bf16[2048,2048]{1,0:T(8,128)(2,1)} %get-tuple-element.173.gu_ref, bf16[512,2048]{1,0:T(8,128)(2,1)} %get-tuple-element.174.bf_ref, ...), custom_call_target="tpu_custom_call" | custom-call | flops 8999999488 | bytes 1048576 | tf_op jit(solution)/shard_map/early_weights/pallas_call | solution.py:876
  169.5 2.2 dynamic-slice_add_fusion.3
  171.7 2.6 dynamic-slice_add_fusion
  174.3 1.6 collective-permute-start.12
  175.9 1.5 collective-permute-start.11
  177.4 10.6 %attention_back.3 = (bf16[1536,2048]{1,0:T(8,128)(2,1)}, bf16[1,512,512]{2,1,0:T(8,128)(2,1)}, f32[512,128]{1,0:T(8,128)}) custom-call(s32[1]{0:T(128)S(6)} %xor.15.refs_0_, bf16[4,512,512]{2,1,0:T(8,128)(2,1)} %get-tuple-element.188.refs_1_, f32[4,8,512]{2,1,0:T(8,128)} %get-tuple-element.189.refs_2_, bf16[4,512,512]{2,1,0:T(8,128)(2,1)} %get-tuple-element.190.refs_3_, ...), custom_call_target="tpu_custom_call" | custom-call | flops 10000000000 | bytes 1048576 | tf_op jit(solution)/shard_map/attention_back/pallas_call | solution.py:720
  188.8 1.5 add_add_fusion.2
  191.1 1.8 add_add_fusion
  192.9 2.7 collective-permute-start.14
  195.7 1.5 collective-permute-start.13
  197.7 19.2 %attention_back.4 = (bf16[1536,2048]{1,0:T(8,128)(2,1)}, bf16[2,512,512]{2,1,0:T(8,128)(2,1)}, f32[512,128]{1,0:T(8,128)}) custom-call(s32[2]{0:T(128)} %pad_add_fusion.refs_0_, bf16[4,512,512]{2,1,0:T(8,128)(2,1)} %get-tuple-element.188.refs_1_, f32[4,8,512]{2,1,0:T(8,128)} %get-tuple-element.189.refs_2_, ...), custom_call_target="tpu_custom_call", output_to_operand_aliasing={{0}: (14, {})} | custom-call | flops 20000000000 | bytes 1048576 | tf_op jit(solution)/shard_map/attention_back/pallas_call | solution.py:720
  217.2 1.5 collective-permute-start.17
  218.8 1.6 collective-permute-start.15
  220.5 10.4 %attention_back.5 = (bf16[1536,2048]{1,0:T(8,128)(2,1)}, bf16[1,512,512]{2,1,0:T(8,128)(2,1)}, f32[512,128]{1,0:T(8,128)}) custom-call(s32[1]{0:T(128)S(6)} %xor.17.refs_0_, bf16[4,512,512]{2,1,0:T(8,128)(2,1)} %get-tuple-element.188.refs_1_, f32[4,8,512]{2,1,0:T(8,128)} %get-tuple-element.189.refs_2_, ...), custom_call_target="tpu_custom_call", output_to_operand_aliasing={{0}: (14, {})} | custom-call | flops 10000000000 | bytes 1048576 | tf_op jit(solution)/shard_map/attention_back/pallas_call | solution.py:720
  231.1 1.6 collective-permute-start.20
  233.0 1.7 collective-permute-done.19
  235.5 6.4 %late_weights.2 = bf16[512,1152]{1,0:T(8,128)(2,1)} custom-call(s32[1]{0:T(128)S(6)} %sub.100.side_ref.refs_0_, bf16[512,2048]{1,0:T(8,128)(2,1)} %get-tuple-element.196.refs_12_.refs_1_, bf16[1536,2048]{1,0:T(8,128)(2,1)} %get-tuple-element.222.refs_2_, bf16[512,2048]{1,0:T(8,128)(2,1)} %get-tuple-element.160.refs_13_.refs_3_, ...), custom_call_target="tpu_custom_call" | custom-call | flops 4000000000 | bytes 1048576 | tf_op jit(solution)/shard_map/late_weights/pallas_call | solution.py:967
  243.6 1.2 constant_dynamic-slice_fusion.4
  245.3 1.5 collective-permute-start.30
  246.8 6.5 %late_weights.3 = bf16[512,1152]{1,0:T(8,128)(2,1)} custom-call(s32[1]{0:T(128)} %bitcast.side_ref.refs_0_, bf16[512,2048]{1,0:T(8,128)(2,1)} %get-tuple-element.196.refs_12_.refs_1_, bf16[1536,2048]{1,0:T(8,128)(2,1)} %get-tuple-element.222.refs_2_, bf16[512,2048]{1,0:T(8,128)(2,1)} %get-tuple-element.160.refs_13_.refs_3_, ...), custom_call_target="tpu_custom_call" | custom-call | flops 4000000000 | bytes 1048576 | tf_op jit(solution)/shard_map/late_weights/pallas_call | solution.py:967
  253.3 1.4 dynamic-slice_add_fusion.1
  254.7 1.0 collective-permute-start.23
  255.7 0.9 pad_maximum_fusion.14
  256.7 2.1 collective-permute-start.33
  259.3 1.1 constant_dynamic-update-slice_fusion.1
  260.6 2.4 maximum_convert_fusion
  263.0 1.7 collective-permute-done.23
  264.6 1.3 add_add_fusion.1
  266.9 3.6 %collective-permute-done.33 = bf16[128,1024]{1,0:T(8,128)(2,1)S(1)} collective-permute-done((bf16[128,1024]{1,0:T(8,128)(2,1)S(1)}, bf16[128,1024]{1,0:T(8,128)(2,1)S(1)}, u32[]{:S(2)}, u32[]{:S(2)}) %collective-permute-start.33) | collective-permute-done | bytes 262176 | tf_op jit(solution)/shard_map/ppermute | solution.py:773
  270.5 0.9 collective-permute-done.32
  271.6 1.1 collective-permute-done.24
  274.8 3.3 %collective-permute-done.25 = bf16[64,1152]{1,0:T(8,128)(2,1)S(1)} collective-permute-done((bf16[64,1152]{1,0:T(8,128)(2,1)S(1)}, bf16[64,1152]{1,0:T(8,128)(2,1)S(1)}, u32[]{:S(2)}, u32[]{:S(2)}) %collective-permute-start.25) | collective-permute-done | bytes 147488 | tf_op jit(solution)/shard_map/ppermute | solution.py:773
  278.1 5.7 %collective-permute-done.34 = bf16[128,2048]{1,0:T(8,128)(2,1)S(1)} collective-permute-done((bf16[128,2048]{1,0:T(8,128)(2,1)S(1)}, bf16[128,2048]{1,0:T(8,128)(2,1)S(1)}, u32[]{:S(2)}, u32[]{:S(2)}) %collective-permute-start.34) | collective-permute-done | bytes 524320 | tf_op jit(solution)/shard_map/ppermute | solution.py:773
  284.5 2.9 collective-permute-start.26
  287.5 4.5 %collective-permute-done.26 = bf16[64,1152]{1,0:T(8,128)(2,1)S(1)} collective-permute-done((bf16[64,1152]{1,0:T(8,128)(2,1)S(1)}, bf16[64,1152]{1,0:T(8,128)(2,1)S(1)}, u32[]{:S(2)}, u32[]{:S(2)}) %collective-permute-start.26) | collective-permute-done | bytes 147488 | tf_op jit(solution)/shard_map/ppermute | solution.py:773
  292.0 1.3 collective-permute-start.27
  293.3 4.6 %collective-permute-done.27 = bf16[64,1152]{1,0:T(8,128)(2,1)S(1)} collective-permute-done((bf16[64,1152]{1,0:T(8,128)(2,1)S(1)}, bf16[64,1152]{1,0:T(8,128)(2,1)S(1)}, u32[]{:S(2)}, u32[]{:S(2)}) %collective-permute-start.27) | collective-permute-done | bytes 147488 | tf_op jit(solution)/shard_map/ppermute | solution.py:773
  298.6 1.5 collective-permute-start.38
  300.1 2.0 collective-permute-done.35.refs_2_
  302.6 2.2 collective-permute-done.28
  304.7 0.9 pad_maximum_fusion.6.refs_1_
  305.6 1.1 collective-permute-start.29
  306.7 1.8 collective-permute-done.38.refs_2_
  311.5 3.6 %unpack.4 = (f32[512,1536]{1,0:T(8,128)}, f32[512,512]{1,0:T(8,128)}) custom-call(s32[3]{0:T(128)} %pad_add_fusion.3.refs_0_, bf16[256,1024]{1,0:T(8,128)(2,1)} %pad_maximum_fusion.11.refs_1_, bf16[256,1024]{1,0:T(8,128)(2,1)} %collective-permute-done.38.refs_2_, bf16[256,1024]{1,0:T(8,128)(2,1)} %collective-permute-done.39.refs_3_, ...), custom_call_target="tpu_custom_call" | custom-call | flops 100000000 | bytes 1048576 | tf_op jit(solution)/shard_map/unpack/pallas_call | solution.py:1131
  315.2 5.7 %unpack.3 = (f32[512,2048]{1,0:T(8,128)}, f32[2048,512]{1,0:T(8,128)}) custom-call(s32[3]{0:T(128)} %get-tuple-element.315.refs_0_, bf16[256,2048]{1,0:T(8,128)(2,1)} %copy-done.2, bf16[256,2048]{1,0:T(8,128)(2,1)} %collective-permute-done.35.refs_2_, bf16[256,2048]{1,0:T(8,128)(2,1)} %collective-permute-done.36.refs_3_, ...), custom_call_target="tpu_custom_call" | custom-call | flops 100000000 | bytes 1048576 | tf_op jit(solution)/shard_map/unpack/pallas_call | solution.py:1131
  322.3 1.5 slice_bitcast_fusion
  324.9 4.5 %unpack.5 = (f32[512,1536]{1,0:T(8,128)}, f32[512,512]{1,0:T(8,128)}, f32[64,512]{1,0:T(8,128)}, f32[1,512]{1,0:T(1,128)}, f32[1,512]{1,0:T(1,128)}, /*index=5*/f32[1,512]{1,0:T(1,128)}) custom-call(s32[3]{0:T(128)} %get-tuple-element.314.refs_0_, bf16[256,1152]{1,0:T(8,128)(2,1)} %pad_maximum_fusion.6.refs_1_, ...), custom_call_target="tpu_custom_call" | custom-call | flops 60000002048 | bytes 1048576 | tf_op jit(solution)/shard_map/unpack/pallas_call | solution.py:1131
  (156 shorter events, 22.9 us)
Async XLA Ops:
  3.6 5.1 %copy-start.22 = (bf16[512]{0:T(512)(128)(2,1)S(1)}, bf16[512]{0:T(512)(128)(2,1)}, u32[]{:S(2)}) copy-start(bf16[512]{0:T(512)(128)(2,1)} %param.20) | copy-start | bytes 3076
  3.6 5.0 %copy-start.23 = (bf16[512]{0:T(512)(128)(2,1)S(1)}, bf16[512]{0:T(512)(128)(2,1)}, u32[]{:S(2)}) copy-start(bf16[512]{0:T(512)(128)(2,1)} %param.23) | copy-start | bytes 3076
  3.7 5.0 %copy-start.24 = (bf16[512]{0:T(512)(128)(2,1)S(1)}, bf16[512]{0:T(512)(128)(2,1)}, u32[]{:S(2)}) copy-start(bf16[512]{0:T(512)(128)(2,1)} %param.26) | copy-start | bytes 3076
  3.7 5.1 %copy-start.8 = (bf16[512,2048]{1,0:T(8,128)(2,1)S(1)}, bf16[512,2048]{1,0:T(8,128)(2,1)}, u32[]{:S(2)}) copy-start(bf16[512,2048]{1,0:T(8,128)(2,1)} %refs_6_.1) | copy-start | bytes 6291460
  5.6 14.9 %collective-permute-start = (bf16[1,528,512]{2,1,0:T(8,128)(2,1)}, bf16[1,528,512]{2,1,0:T(8,128)(2,1)}, u32[]{:S(2)}, u32[]{:S(2)}) collective-permute-start(bf16[1,528,512]{2,1,0:T(8,128)(2,1)} %get-tuple-element.144), channel_id=1, source_target_pairs={{0,8},{8,0},{16,24},{24,16},{1,9},{9,1},{17,25},{25,17},{2,10},{10... | collective-permute-start | bytes 1622024 | tf_op jit(solution)/shard_map/ppermute | solution.py:748
  6.0 16.0 %collective-permute-start.1 = (bf16[1,528,512]{2,1,0:T(8,128)(2,1)}, bf16[1,528,512]{2,1,0:T(8,128)(2,1)}, u32[]{:S(2)}, u32[]{:S(2)}) collective-permute-start(bf16[1,528,512]{2,1,0:T(8,128)(2,1)} %get-tuple-element.145), channel_id=1, source_target_pairs={{0,16},{8,24},{16,0},{24,8},{1,17},{9,25},{17,1},{25,9},{2,18},{10... | collective-permute-start | bytes 1622024 | tf_op jit(solution)/shard_map/ppermute | solution.py:748
  8.5 24.7 %collective-permute-start.2 = (bf16[1,528,512]{2,1,0:T(8,128)(2,1)}, bf16[1,528,512]{2,1,0:T(8,128)(2,1)}, u32[]{:S(2)}, u32[]{:S(2)}) collective-permute-start(bf16[1,528,512]{2,1,0:T(8,128)(2,1)} %pad_maximum_fusion.9), channel_id=1, source_target_pairs={{0,24},{8,16},{16,8},{24,0},{1,25},{9,17},{17,9},{25,1},{2,26},{10... | collective-permute-start | bytes 1622024 | tf_op jit(solution)/shard_map/ppermute | solution.py:748
  15.5 17.7 %copy-start.9 = (bf16[4,1,512,512]{3,2,1,0:T(8,128)(2,1)S(1)}, bf16[4,1,512,512]{3,2,1,0:T(8,128)(2,1)}, u32[]{:S(2)}) copy-start(bf16[4,1,512,512]{3,2,1,0:T(8,128)(2,1)} %param.30) | copy-start | bytes 6291460
  17.7 15.6 %copy-start.21 = (bf16[4,1,64,512]{3,2,1,0:T(8,128)(2,1)S(1)}, bf16[4,1,64,512]{3,2,1,0:T(8,128)(2,1)}, u32[]{:S(2)}) copy-start(bf16[4,1,64,512]{3,2,1,0:T(8,128)(2,1)} %param.31) | copy-start | bytes 786436
  33.5 67.5 %collective-permute-start.3 = (bf16[1,576,512]{2,1,0:T(8,128)(2,1)S(1)}, bf16[1,576,512]{2,1,0:T(8,128)(2,1)}, u32[]{:S(2)}, u32[]{:S(2)}) collective-permute-start(bf16[1,576,512]{2,1,0:T(8,128)(2,1)S(1)} %pad_maximum_fusion.3), channel_id=1, source_target_pairs={{0,8},{8,0},{16,24},{24,16},{1,9},{9,1},{17,25},{25,17},{2,10},{10... | collective-permute-start | bytes 1769480 | tf_op jit(solution)/shard_map/ppermute | solution.py:748
  33.7 67.4 %collective-permute-start.4 = (bf16[1,576,512]{2,1,0:T(8,128)(2,1)S(1)}, bf16[1,576,512]{2,1,0:T(8,128)(2,1)}, u32[]{:S(2)}, u32[]{:S(2)}) collective-permute-start(bf16[1,576,512]{2,1,0:T(8,128)(2,1)S(1)} %pad_maximum_fusion.4), channel_id=1, source_target_pairs={{0,16},{8,24},{16,0},{24,8},{1,17},{9,25},{17,1},{25,9},{2,18},{10... | collective-permute-start | bytes 1769480 | tf_op jit(solution)/shard_map/ppermute | solution.py:748
  35.3 65.7 %collective-permute-start.5 = (bf16[1,576,512]{2,1,0:T(8,128)(2,1)S(1)}, bf16[1,576,512]{2,1,0:T(8,128)(2,1)}, u32[]{:S(2)}, u32[]{:S(2)}) collective-permute-start(bf16[1,576,512]{2,1,0:T(8,128)(2,1)S(1)} %pad_maximum_fusion.5), channel_id=1, source_target_pairs={{0,24},{8,16},{16,8},{24,0},{1,25},{9,17},{17,9},{25,1},{2,26},{10... | collective-permute-start | bytes 1769480 | tf_op jit(solution)/shard_map/ppermute | solution.py:748
  99.0 48.2 %collective-permute-start.6 = (bf16[1,576,512]{2,1,0:T(8,128)(2,1)}, bf16[1,576,512]{2,1,0:T(8,128)(2,1)S(1)}, u32[]{:S(2)}, u32[]{:S(2)}) collective-permute-start(bf16[1,576,512]{2,1,0:T(8,128)(2,1)} %get-tuple-element.295), channel_id=1, source_target_pairs={{0,8},{8,0},{16,24},{24,16},{1,9},{9,1},{17,25},{25,17},{2,10},{10... | collective-permute-start | bytes 1769480 | tf_op jit(solution)/shard_map/ppermute | solution.py:748
  99.4 47.7 %collective-permute-start.7 = (bf16[1,576,512]{2,1,0:T(8,128)(2,1)}, bf16[1,576,512]{2,1,0:T(8,128)(2,1)S(1)}, u32[]{:S(2)}, u32[]{:S(2)}) collective-permute-start(bf16[1,576,512]{2,1,0:T(8,128)(2,1)} %get-tuple-element.294), channel_id=1, source_target_pairs={{0,16},{8,24},{16,0},{24,8},{1,17},{9,25},{17,1},{25,9},{2,18},{10... | collective-permute-start | bytes 1769480 | tf_op jit(solution)/shard_map/ppermute | solution.py:748
  101.0 46.1 %collective-permute-start.8 = (bf16[1,576,512]{2,1,0:T(8,128)(2,1)}, bf16[1,576,512]{2,1,0:T(8,128)(2,1)S(1)}, u32[]{:S(2)}, u32[]{:S(2)}) collective-permute-start(bf16[1,576,512]{2,1,0:T(8,128)(2,1)} %get-tuple-element.293), channel_id=1, source_target_pairs={{0,24},{8,16},{16,8},{24,0},{1,25},{9,17},{17,9},{25,1},{2,26},{10... | collective-permute-start | bytes 1769480 | tf_op jit(solution)/shard_map/ppermute | solution.py:748
  147.1 10.9 %copy-start.12 = (bf16[1,576,512]{2,1,0:T(8,128)(2,1)}, bf16[1,576,512]{2,1,0:T(8,128)(2,1)S(1)}, u32[]{:S(2)}) copy-start(bf16[1,576,512]{2,1,0:T(8,128)(2,1)S(1)} %collective-permute-done.6) | copy-start | bytes 1769476
  147.2 10.9 %copy-start.14 = (bf16[1,576,512]{2,1,0:T(8,128)(2,1)}, bf16[1,576,512]{2,1,0:T(8,128)(2,1)S(1)}, u32[]{:S(2)}) copy-start(bf16[1,576,512]{2,1,0:T(8,128)(2,1)S(1)} %collective-permute-done.7) | copy-start | bytes 1769476
  147.2 10.9 %copy-start.16 = (bf16[1,576,512]{2,1,0:T(8,128)(2,1)}, bf16[1,576,512]{2,1,0:T(8,128)(2,1)S(1)}, u32[]{:S(2)}) copy-start(bf16[1,576,512]{2,1,0:T(8,128)(2,1)S(1)} %collective-permute-done.8) | copy-start | bytes 1769476
  158.0 13.6 %collective-permute-start.9 = (bf16[512,2048]{1,0:T(8,128)(2,1)}, bf16[512,2048]{1,0:T(8,128)(2,1)S(1)}, u32[]{:S(2)}, u32[]{:S(2)}) collective-permute-start(bf16[512,2048]{1,0:T(8,128)(2,1)} %get-tuple-element.180), channel_id=1, source_target_pairs={{0,8},{1,9},{2,10},{3,11},{4,12},{5,13},{6,14},{7,15},{8,0},{9,1},... | collective-permute-start | bytes 6291464 | tf_op jit(solution)/shard_map/ppermute | solution.py:773
  158.5 10.9 %collective-permute-start.10 = (bf16[512,1024]{1,0:T(8,128)(2,1)}, bf16[512,1024]{1,0:T(8,128)(2,1)}, u32[]{:S(2)}, u32[]{:S(2)}) collective-permute-start(bf16[512,1024]{1,0:T(8,128)(2,1)} %get-tuple-element.181), channel_id=1, source_target_pairs={{0,8},{1,9},{2,10},{3,11},{4,12},{5,13},{6,14},{7,15},{8,0},{9,1},... | collective-permute-start | bytes 3145736 | tf_op jit(solution)/shard_map/ppermute | solution.py:773
  174.3 14.6 %collective-permute-start.12 = (bf16[256,1024]{1,0:T(8,128)(2,1)}, bf16[256,1024]{1,0:T(8,128)(2,1)}, u32[]{:S(2)}, u32[]{:S(2)}) collective-permute-start(bf16[256,1024]{1,0:T(8,128)(2,1)} %dynamic-slice_add_fusion.3), channel_id=1, source_target_pairs={{0,2},{1,3},{2,0},{3,1},{4,6},{5,7},{6,4},{7,5},{8,10},{9,11},{10,... | collective-permute-start | bytes 1572872 | tf_op jit(solution)/shard_map/ppermute | solution.py:773
  175.9 15.2 %collective-permute-start.11 = (bf16[256,2048]{1,0:T(8,128)(2,1)}, bf16[256,2048]{1,0:T(8,128)(2,1)}, u32[]{:S(2)}, u32[]{:S(2)}) collective-permute-start(bf16[256,2048]{1,0:T(8,128)(2,1)} %dynamic-slice_add_fusion), channel_id=1, source_target_pairs={{0,1},{1,0},{2,3},{3,2},{4,5},{5,4},{6,7},{7,6},{8,24},{9,25},{10,... | collective-permute-start | bytes 3145736 | tf_op jit(solution)/shard_map/ppermute | solution.py:773
  177.4 11.4 %copy-start.10 = (bf16[512,1024]{1,0:T(8,128)(2,1)S(1)}, bf16[512,1024]{1,0:T(8,128)(2,1)}, u32[]{:S(2)}) copy-start(bf16[512,1024]{1,0:T(8,128)(2,1)} %get-tuple-element.184) | copy-start | bytes 3145732
  188.0 3.1 copy-start.5
  192.9 24.0 %collective-permute-start.14 = (bf16[128,1024]{1,0:T(8,128)(2,1)S(1)}, bf16[128,1024]{1,0:T(8,128)(2,1)S(1)}, u32[]{:S(2)}, u32[]{:S(2)}) collective-permute-start(bf16[128,1024]{1,0:T(8,128)(2,1)S(1)} %constant_dynamic-slice_fusion.14), channel_id=1, source_target_pairs={{0,4},{1,5},{2,6},{3,7},{4,0},{5,1},{6,2},{7,3},{8,12},{9,13},{10,... | collective-permute-start | bytes 786440 | tf_op jit(solution)/shard_map/ppermute | solution.py:773
  195.7 21.4 %collective-permute-start.13 = (bf16[128,2048]{1,0:T(8,128)(2,1)S(1)}, bf16[128,2048]{1,0:T(8,128)(2,1)S(1)}, u32[]{:S(2)}, u32[]{:S(2)}) collective-permute-start(bf16[128,2048]{1,0:T(8,128)(2,1)S(1)} %constant_dynamic-slice_fusion.15), channel_id=1, source_target_pairs={{0,16},{1,17},{2,18},{3,19},{4,20},{5,21},{6,22},{7,23},{8,9},{9,8... | collective-permute-start | bytes 1572872 | tf_op jit(solution)/shard_map/ppermute | solution.py:773
  197.2 23.2 %collective-permute-start.16 = (bf16[1,512,512]{2,1,0:T(8,128)(2,1)}, bf16[1,512,512]{2,1,0:T(8,128)(2,1)}, u32[]{:S(2)}, u32[]{:S(2)}) collective-permute-start(bf16[1,512,512]{2,1,0:T(8,128)(2,1)} %get-tuple-element.211), channel_id=1, source_target_pairs={{0,16},{8,24},{16,0},{24,8},{1,17},{9,25},{17,1},{25,9},{2,18},{10... | collective-permute-start | bytes 1572872 | tf_op jit(solution)/shard_map/ppermute | solution.py:748
  197.7 19.2 %copy-start.7 = (bf16[256,1024]{1,0:T(8,128)(2,1)S(1)}, bf16[256,1024]{1,0:T(8,128)(2,1)}, u32[]{:S(2)}) copy-start(bf16[256,1024]{1,0:T(8,128)(2,1)} %copy-done.6) | copy-start | bytes 1572868
  216.9 3.5 %copy-start.11 = (bf16[2,512,512]{2,1,0:T(8,128)(2,1)S(1)}, bf16[2,512,512]{2,1,0:T(8,128)(2,1)}, u32[]{:S(2)}) copy-start(bf16[2,512,512]{2,1,0:T(8,128)(2,1)} %get-tuple-element.220) | copy-start | bytes 3145732
  217.2 13.7 %collective-permute-start.17 = (bf16[64,1024]{1,0:T(8,128)(2,1)S(1)}, bf16[64,1024]{1,0:T(8,128)(2,1)S(1)}, u32[]{:S(2)}, u32[]{:S(2)}) collective-permute-start(bf16[64,1024]{1,0:T(8,128)(2,1)S(1)} %constant_dynamic-slice_fusion.12), channel_id=1, source_target_pairs={{0,1},{1,0},{2,3},{3,2},{4,5},{5,4},{6,7},{7,6},{8,24},{9,25},{10,... | collective-permute-start | bytes 393224 | tf_op jit(solution)/shard_map/ppermute | solution.py:773
  218.8 12.2 %collective-permute-start.15 = (bf16[64,2048]{1,0:T(8,128)(2,1)S(1)}, bf16[64,2048]{1,0:T(8,128)(2,1)S(1)}, u32[]{:S(2)}, u32[]{:S(2)}) collective-permute-start(bf16[64,2048]{1,0:T(8,128)(2,1)S(1)} %constant_dynamic-slice_fusion.13), channel_id=1, source_target_pairs={{0,2},{1,3},{2,0},{3,1},{4,6},{5,7},{6,4},{7,5},{8,10},{9,11},{10,... | collective-permute-start | bytes 786440 | tf_op jit(solution)/shard_map/ppermute | solution.py:773
  220.5 14.2 %collective-permute-start.19 = (bf16[1,512,512]{2,1,0:T(8,128)(2,1)S(1)}, bf16[1,512,512]{2,1,0:T(8,128)(2,1)S(1)}, u32[]{:S(2)}, u32[]{:S(2)}) collective-permute-start(bf16[1,512,512]{2,1,0:T(8,128)(2,1)S(1)} %get-tuple-element.307), channel_id=1, source_target_pairs={{0,24},{8,16},{16,8},{24,0},{1,25},{9,17},{17,9},{25,1},{2,26},{10... | collective-permute-start | bytes 1572872 | tf_op jit(solution)/shard_map/ppermute | solution.py:748
  231.1 10.8 %collective-permute-start.20 = (bf16[64,1024]{1,0:T(8,128)(2,1)S(1)}, bf16[64,1024]{1,0:T(8,128)(2,1)S(1)}, u32[]{:S(2)}, u32[]{:S(2)}) collective-permute-start(bf16[64,1024]{1,0:T(8,128)(2,1)S(1)} %dynamic-slice_add_fusion.8), channel_id=1, source_target_pairs={{0,16},{1,17},{2,18},{3,19},{4,20},{5,21},{6,22},{7,23},{8,9},{9,8... | collective-permute-start | bytes 393224 | tf_op jit(solution)/shard_map/ppermute | solution.py:773
  232.7 10.0 %collective-permute-start.18 = (bf16[32,2048]{1,0:T(8,128)(2,1)S(1)}, bf16[32,2048]{1,0:T(8,128)(2,1)S(1)}, u32[]{:S(2)}, u32[]{:S(2)}) collective-permute-start(bf16[32,2048]{1,0:T(8,128)(2,1)S(1)} %constant_dynamic-slice_fusion.11), channel_id=1, source_target_pairs={{0,4},{1,5},{2,6},{3,7},{4,0},{5,1},{6,2},{7,3},{8,12},{9,13},{10,... | collective-permute-start | bytes 393224 | tf_op jit(solution)/shard_map/ppermute | solution.py:773
  235.5 7.8 %copy-start.13 = (bf16[1,576,512]{2,1,0:T(8,128)(2,1)S(1)}, bf16[1,576,512]{2,1,0:T(8,128)(2,1)}, u32[]{:S(2)}) copy-start(bf16[1,576,512]{2,1,0:T(8,128)(2,1)} %copy-done.12) | copy-start | bytes 1769476
  235.5 7.8 %copy-start.15 = (bf16[1,576,512]{2,1,0:T(8,128)(2,1)S(1)}, bf16[1,576,512]{2,1,0:T(8,128)(2,1)}, u32[]{:S(2)}) copy-start(bf16[1,576,512]{2,1,0:T(8,128)(2,1)} %copy-done.14) | copy-start | bytes 1769476
  235.5 7.8 %copy-start.17 = (bf16[1,576,512]{2,1,0:T(8,128)(2,1)S(1)}, bf16[1,576,512]{2,1,0:T(8,128)(2,1)}, u32[]{:S(2)}) copy-start(bf16[1,576,512]{2,1,0:T(8,128)(2,1)} %copy-done.16) | copy-start | bytes 1769476
  242.7 10.6 %collective-permute-start.22 = (bf16[512,1152]{1,0:T(8,128)(2,1)}, bf16[512,1152]{1,0:T(8,128)(2,1)}, u32[]{:S(2)}, u32[]{:S(2)}) collective-permute-start(bf16[512,1152]{1,0:T(8,128)(2,1)} %late_weights.2), channel_id=1, source_target_pairs={{0,8},{1,9},{2,10},{3,11},{4,12},{5,13},{6,14},{7,15},{8,0},{9,1},... | collective-permute-start | bytes 3538952 | tf_op jit(solution)/shard_map/ppermute | solution.py:773
  242.9 3.9 %collective-permute-start.21 = (bf16[1,512,512]{2,1,0:T(8,128)(2,1)}, bf16[1,512,512]{2,1,0:T(8,128)(2,1)S(1)}, u32[]{:S(2)}, u32[]{:S(2)}) collective-permute-start(bf16[1,512,512]{2,1,0:T(8,128)(2,1)} %get-tuple-element.232), channel_id=1, source_target_pairs={{0,8},{8,0},{16,24},{24,16},{1,9},{9,1},{17,25},{25,17},{2,10},{10... | collective-permute-start | bytes 1572872 | tf_op jit(solution)/shard_map/ppermute | solution.py:748
  244.7 11.0 %collective-permute-start.31 = (bf16[64,1024]{1,0:T(8,128)(2,1)}, bf16[64,1024]{1,0:T(8,128)(2,1)S(1)}, u32[]{:S(2)}, u32[]{:S(2)}) collective-permute-start(bf16[64,1024]{1,0:T(8,128)(2,1)} %add.339), channel_id=1, source_target_pairs={{0,1},{1,0},{2,3},{3,2},{4,5},{5,4},{6,7},{7,6},{8,24},{9,25},{10,... | collective-permute-start | bytes 393224 | tf_op jit(solution)/shard_map/ppermute | solution.py:773
  245.3 11.4 %collective-permute-start.30 = (bf16[32,2048]{1,0:T(8,128)(2,1)S(1)}, bf16[32,2048]{1,0:T(8,128)(2,1)S(1)}, u32[]{:S(2)}, u32[]{:S(2)}) collective-permute-start(bf16[32,2048]{1,0:T(8,128)(2,1)S(1)} %dynamic-slice_add_fusion.9), channel_id=1, source_target_pairs={{0,4},{1,5},{2,6},{3,7},{4,0},{5,1},{6,2},{7,3},{8,12},{9,13},{10,... | collective-permute-start | bytes 393224 | tf_op jit(solution)/shard_map/ppermute | solution.py:773
  254.7 5.7 %copy-start.19 = (bf16[1,512,512]{2,1,0:T(8,128)(2,1)S(1)}, bf16[1,512,512]{2,1,0:T(8,128)(2,1)}, u32[]{:S(2)}) copy-start(bf16[1,512,512]{2,1,0:T(8,128)(2,1)} %copy-done.18) | copy-start | bytes 1572868
  254.7 9.9 %collective-permute-start.23 = (bf16[256,1152]{1,0:T(8,128)(2,1)S(1)}, bf16[256,1152]{1,0:T(8,128)(2,1)S(1)}, u32[]{:S(2)}, u32[]{:S(2)}) collective-permute-start(bf16[256,1152]{1,0:T(8,128)(2,1)S(1)} %dynamic-slice_add_fusion.1), channel_id=1, source_target_pairs={{0,1},{1,0},{2,3},{3,2},{4,5},{5,4},{6,7},{7,6},{8,24},{9,25},{10,... | collective-permute-start | bytes 1769480 | tf_op jit(solution)/shard_map/ppermute | solution.py:773
  256.7 13.8 %collective-permute-start.33 = (bf16[128,1024]{1,0:T(8,128)(2,1)S(1)}, bf16[128,1024]{1,0:T(8,128)(2,1)S(1)}, u32[]{:S(2)}, u32[]{:S(2)}) collective-permute-start(bf16[128,1024]{1,0:T(8,128)(2,1)S(1)} %pad_maximum_fusion.14), channel_id=1, source_target_pairs={{0,4},{1,5},{2,6},{3,7},{4,0},{5,1},{6,2},{7,3},{8,12},{9,13},{10,... | collective-permute-start | bytes 786440 | tf_op jit(solution)/shard_map/ppermute | solution.py:773
  258.8 12.6 %collective-permute-start.32 = (bf16[64,2048]{1,0:T(8,128)(2,1)S(1)}, bf16[64,2048]{1,0:T(8,128)(2,1)S(1)}, u32[]{:S(2)}, u32[]{:S(2)}) collective-permute-start(bf16[64,2048]{1,0:T(8,128)(2,1)S(1)} %pad_maximum_fusion.13), channel_id=1, source_target_pairs={{0,2},{1,3},{2,0},{3,1},{4,6},{5,7},{6,4},{7,5},{8,10},{9,11},{10,... | collective-permute-start | bytes 786440 | tf_op jit(solution)/shard_map/ppermute | solution.py:773
  260.6 4.1 %copy-start.1 = (bf16[512,1152]{1,0:T(8,128)(2,1)S(1)}, bf16[512,1152]{1,0:T(8,128)(2,1)}, u32[]{:S(2)}) copy-start(bf16[512,1152]{1,0:T(8,128)(2,1)} %late_weights.3) | copy-start | bytes 3538948
  263.0 3.6 %copy-start.3 = (bf16[1,576,512]{2,1,0:T(8,128)(2,1)S(1)}, bf16[1,576,512]{2,1,0:T(8,128)(2,1)}, u32[]{:S(2)}) copy-start(bf16[1,576,512]{2,1,0:T(8,128)(2,1)} %get-tuple-element.290) | copy-start | bytes 1769476
  263.0 3.6 %copy-start.4 = (bf16[1,576,512]{2,1,0:T(8,128)(2,1)S(1)}, bf16[1,576,512]{2,1,0:T(8,128)(2,1)}, u32[]{:S(2)}) copy-start(bf16[1,576,512]{2,1,0:T(8,128)(2,1)} %get-tuple-element.291) | copy-start | bytes 1769476
  266.0 6.8 %collective-permute-start.24 = (bf16[128,1152]{1,0:T(8,128)(2,1)S(1)}, bf16[128,1152]{1,0:T(8,128)(2,1)S(1)}, u32[]{:S(2)}, u32[]{:S(2)}) collective-permute-start(bf16[128,1152]{1,0:T(8,128)(2,1)S(1)} %constant_dynamic-slice_fusion.6), channel_id=1, source_target_pairs={{0,16},{1,17},{2,18},{3,19},{4,20},{5,21},{6,22},{7,23},{8,9},{9,8... | collective-permute-start | bytes 884744 | tf_op jit(solution)/shard_map/ppermute | solution.py:773
  272.9 5.2 %collective-permute-start.25 = (bf16[64,1152]{1,0:T(8,128)(2,1)S(1)}, bf16[64,1152]{1,0:T(8,128)(2,1)S(1)}, u32[]{:S(2)}, u32[]{:S(2)}) collective-permute-start(bf16[64,1152]{1,0:T(8,128)(2,1)S(1)} %constant_dynamic-slice_fusion), channel_id=1, source_target_pairs={{0,2},{1,3},{2,0},{3,1},{4,6},{5,7},{6,4},{7,5},{8,10},{9,11},{10,... | collective-permute-start | bytes 442376 | tf_op jit(solution)/shard_map/ppermute | solution.py:773
  274.3 9.6 %collective-permute-start.34 = (bf16[128,2048]{1,0:T(8,128)(2,1)S(1)}, bf16[128,2048]{1,0:T(8,128)(2,1)S(1)}, u32[]{:S(2)}, u32[]{:S(2)}) collective-permute-start(bf16[128,2048]{1,0:T(8,128)(2,1)S(1)} %pad_maximum_fusion.10), channel_id=1, source_target_pairs={{0,16},{1,17},{2,18},{3,19},{4,20},{5,21},{6,22},{7,23},{8,9},{9,8... | collective-permute-start | bytes 1572872 | tf_op jit(solution)/shard_map/ppermute | solution.py:773
  283.9 31.3 %copy-start.2 = (bf16[256,2048]{1,0:T(8,128)(2,1)}, bf16[256,2048]{1,0:T(8,128)(2,1)S(1)}, u32[]{:S(2)}) copy-start(bf16[256,2048]{1,0:T(8,128)(2,1)S(1)} %pad_maximum_fusion.2.refs_1_) | copy-start | bytes 3145732
  283.9 18.1 %collective-permute-start.35 = (bf16[256,2048]{1,0:T(8,128)(2,1)S(1)}, bf16[256,2048]{1,0:T(8,128)(2,1)}, u32[]{:S(2)}, u32[]{:S(2)}) collective-permute-start(bf16[256,2048]{1,0:T(8,128)(2,1)S(1)} %pad_maximum_fusion.2.refs_1_), channel_id=1, source_target_pairs={{0,1},{1,0},{2,3},{3,2},{4,5},{5,4},{6,7},{7,6},{8,24},{9,25},{10,... | collective-permute-start | bytes 3145736 | tf_op jit(solution)/shard_map/ppermute | solution.py:773
  284.5 7.4 %collective-permute-start.26 = (bf16[64,1152]{1,0:T(8,128)(2,1)S(1)}, bf16[64,1152]{1,0:T(8,128)(2,1)S(1)}, u32[]{:S(2)}, u32[]{:S(2)}) collective-permute-start(bf16[64,1152]{1,0:T(8,128)(2,1)S(1)} %dynamic-slice_add_fusion.7), channel_id=1, source_target_pairs={{0,4},{1,5},{2,6},{3,7},{4,0},{5,1},{6,2},{7,3},{8,12},{9,13},{10,... | collective-permute-start | bytes 442376 | tf_op jit(solution)/shard_map/ppermute | solution.py:773
  292.0 5.9 %collective-permute-start.27 = (bf16[64,1152]{1,0:T(8,128)(2,1)S(1)}, bf16[64,1152]{1,0:T(8,128)(2,1)S(1)}, u32[]{:S(2)}, u32[]{:S(2)}) collective-permute-start(bf16[64,1152]{1,0:T(8,128)(2,1)S(1)} %add.350), channel_id=1, source_target_pairs={{0,2},{1,3},{2,0},{3,1},{4,6},{5,7},{6,4},{7,5},{8,10},{9,11},{10,... | collective-permute-start | bytes 442376 | tf_op jit(solution)/shard_map/ppermute | solution.py:773
  297.9 6.8 %collective-permute-start.28 = (bf16[128,1152]{1,0:T(8,128)(2,1)S(1)}, bf16[128,1152]{1,0:T(8,128)(2,1)S(1)}, u32[]{:S(2)}, u32[]{:S(2)}) collective-permute-start(bf16[128,1152]{1,0:T(8,128)(2,1)S(1)} %pad_maximum_fusion.12), channel_id=1, source_target_pairs={{0,16},{1,17},{2,18},{3,19},{4,20},{5,21},{6,22},{7,23},{8,9},{9,8... | collective-permute-start | bytes 884744 | tf_op jit(solution)/shard_map/ppermute | solution.py:773
  298.6 10.0 %collective-permute-start.38 = (bf16[256,1024]{1,0:T(8,128)(2,1)}, bf16[256,1024]{1,0:T(8,128)(2,1)}, u32[]{:S(2)}, u32[]{:S(2)}) collective-permute-start(bf16[256,1024]{1,0:T(8,128)(2,1)} %pad_maximum_fusion.11.refs_1_), channel_id=1, source_target_pairs={{0,2},{1,3},{2,0},{3,1},{4,6},{5,7},{6,4},{7,5},{8,10},{9,11},{10,... | collective-permute-start | bytes 1572872 | tf_op jit(solution)/shard_map/ppermute | solution.py:773
  302.1 13.1 %collective-permute-start.36 = (bf16[256,2048]{1,0:T(8,128)(2,1)S(1)}, bf16[256,2048]{1,0:T(8,128)(2,1)}, u32[]{:S(2)}, u32[]{:S(2)}) collective-permute-start(bf16[256,2048]{1,0:T(8,128)(2,1)S(1)} %pad_maximum_fusion.2.refs_1_), channel_id=1, source_target_pairs={{0,8},{1,9},{2,10},{3,11},{4,12},{5,13},{6,14},{7,15},{8,0},{9,1},... | collective-permute-start | bytes 3145736 | tf_op jit(solution)/shard_map/ppermute | solution.py:773
  302.1 13.1 %collective-permute-start.37 = (bf16[256,2048]{1,0:T(8,128)(2,1)}, bf16[256,2048]{1,0:T(8,128)(2,1)}, u32[]{:S(2)}, u32[]{:S(2)}) collective-permute-start(bf16[256,2048]{1,0:T(8,128)(2,1)} %collective-permute-done.35.refs_2_), channel_id=1, source_target_pairs={{0,8},{1,9},{2,10},{3,11},{4,12},{5,13},{6,14},{7,15},{8,0},{9,1},... | collective-permute-start | bytes 3145736 | tf_op jit(solution)/shard_map/ppermute | solution.py:773
  305.6 15.4 %collective-permute-start.29 = (bf16[256,1152]{1,0:T(8,128)(2,1)}, bf16[256,1152]{1,0:T(8,128)(2,1)}, u32[]{:S(2)}, u32[]{:S(2)}) collective-permute-start(bf16[256,1152]{1,0:T(8,128)(2,1)} %pad_maximum_fusion.6.refs_1_), channel_id=1, source_target_pairs={{0,1},{1,0},{2,3},{3,2},{4,5},{5,4},{6,7},{7,6},{8,24},{9,25},{10,... | collective-permute-start | bytes 1769480 | tf_op jit(solution)/shard_map/ppermute | solution.py:773
  308.5 2.3 collective-permute-start.39
  308.5 3.0 collective-permute-start.40
  321.0 2.8 collective-permute-start.41
  321.2 2.9 collective-permute-start.42
  (6 other events, 8.3 us)
